TPU v7x, 32 devices: a whole 2x2x4 slice. The times are simulated.
32 devices in a mesh: dp: 16 (over z, y, x), mp: 2 (over core).
Axes of the slice: x: 2, y: 2, z: 4, core: 2. Of those that a mesh axis runs over, the one named last changes fastest.
Arguments:
- inputs: bfloat16 [16, 2048, 512], P('dp', 'mp'), may hold values from -6 to 6
- cotangent: bfloat16 [16, 2048, 512], P('dp', 'mp'), may hold values from -6 to 6
- lengths: int32 [16], P('dp'), may hold values from 1024 to 2048, as said below
- hidden_weights: float32 [2, 4, 512, 1024], P(None, None, None, 'mp'), may hold values from -0.25 to 0.25
- mlp_weights: float32 [2, 2, 512, 2048], P(None, None, None, 'mp'), may hold values from -0.25 to 0.25
- norm_gains: float32 [2, 2, 512], replicated, may hold values from 0.5 to 1.5
- gate_bias: float32 [2, 2, 1024], P(None, None, 'mp'), may hold values from -8.5 to 4
- left_bases: float32 [2, 6, 512, 512], replicated, may hold values from -1 to 1, as said below
- hidden_blocks: float32 [2, 4, 8, 128, 128], P(None, None, 'mp'), may hold values from -1 to 1, as said below
- mlp_blocks: float32 [2, 2, 16, 128, 128], P(None, None, 'mp'), may hold values from -1 to 1, as said below
- hidden_first: float32 [512, 2, 4, 1024], P('dp', None, None, 'mp'), as said below
- hidden_second: float32 [512, 2, 4, 1024], P('dp', None, None, 'mp'), as said below
- mlp_first: float32 [512, 2, 2, 2048], P('dp', None, None, 'mp'), as said below
- mlp_second: float32 [512, 2, 2, 2048], P('dp', None, None, 'mp'), as said below
- gain_first: float32 [2, 2, 512], replicated, as said below
- gain_second: float32 [2, 2, 512], replicated, as said below
- bias_first: float32 [2, 2, 1024], P(None, None, 'mp'), as said below
- bias_second: float32 [2, 2, 1024], P(None, None, 'mp'), as said below
- step_count: int32 [1], replicated, may hold values from 2 to 20
- row_owner: int32 [16], replicated, may hold values from 0 to 15, each once
Outputs:
- output: float32 [16, 2048, 512], P('dp', 'mp')
- input_grad: float32 [16, 2048, 512], P('dp', 'mp')
- hidden_grad: float32 [512, 2, 4, 1024], P('dp', None, None, 'mp')
- hidden_first_new: float32 [512, 2, 4, 1024], P('dp', None, None, 'mp')
- hidden_second_new: float32 [512, 2, 2, 1024], P('dp', None, None, 'mp')
- gate_second_new: float32 [512, 2, 2, 1024], P('dp', None, None, 'mp')
- hidden_new: float32 [2, 4, 512, 1024], P(None, None, None, 'mp')
- mlp_grad: float32 [512, 2, 2, 2048], P('dp', None, None, 'mp')
- mlp_first_new: float32 [512, 2, 2, 2048], P('dp', None, None, 'mp')
- mlp_second_new: float32 [512, 2, 2, 2048], P('dp', None, None, 'mp')
- mlp_new: float32 [2, 2, 512, 2048], P(None, None, None, 'mp')
- gain_grad: float32 [2, 2, 512], replicated
- gain_first_new: float32 [2, 2, 512], replicated
- gain_second_new: float32 [2, 2, 512], replicated
- gain_new: float32 [2, 2, 512], replicated
- bias_grad: float32 [2, 2, 1024], P(None, None, 'mp')
- bias_first_new: float32 [2, 2, 1024], P(None, None, 'mp')
- bias_second_new: float32 [2, 2, 1024], P(None, None, 'mp')
- bias_new: float32 [2, 2, 1024], P(None, None, 'mp')
Inputs may be any that keep to these rules, and one draw needn't show every extreme that they name: `lengths`: positions at or past a sequence's length are padding; at least one sequence has length 2048. `left_bases`: each [512, 512] matrix is orthogonal. `hidden_blocks`: each [128, 128] block is orthogonal. `mlp_blocks`: each [128, 128] block is orthogonal. `hidden_first`: real values of either sign. `hidden_second`: Positive. `mlp_first`: real values of either sign. `mlp_second`: Positive. `gain_first`: real values of either sign. `gain_second`: Positive. `bias_first`: real values of either sign. `bias_second`: Positive. `row_owner`: each dp index appears once.
All inputs are finite; a program needn't handle non-finite values.
Results may differ from a plain program's by a relative error of at most 0.025.
The roundings to bfloat16 on the way count: a program that leaves them out, or rounds other values in their place, can miss the bound.
Values may be sent and summed in bfloat16 or wider, within the bound.
No kernel may reach another device: no remote copies, remote signals or barrier semaphores. Data moves between devices by JAX's collectives and lax.ppermute only.
A program may use at most 384 MiB of HBM per device.

v0:
```python
import jax
import jax.numpy as jnp
from jax import lax
from jax.sharding import PartitionSpec as P

NORM_EPS = 1e-05
BETA_ONE = 0.9
BETA_TWO = 0.95
ADAM_EPS = 1e-08
MATRIX_RATE = 0.08
GAIN_RATE = 0.5
BIAS_RATE = 4.0
DECAY_RATE = 0.01
HIGHEST = lax.Precision.HIGHEST


def candidate(values):
    return jnp.where(values >= 0, values + 0.5, jax.nn.sigmoid(values))


def candidate_slope(values):
    sigmoid_value = jax.nn.sigmoid(values)
    return jnp.where(values >= 0, 1.0, sigmoid_value * (1.0 - sigmoid_value))


def gelu_slope(values):
    normal_cdf = 0.5 * (1.0 + lax.erf(values * 0.7071067811865476))
    return normal_cdf + values * jnp.exp(-0.5 * values * values) * 0.3989422804014327


def affine_combine(earlier, later):
    return (earlier[0] * later[0], later[0] * earlier[1] + later[1])


def linear_scan(keep_rate, drive, reverse):
    if reverse:
        keep_next = jnp.concatenate(
            [keep_rate[:, 1:, :], jnp.zeros_like(keep_rate[:, :1, :])], axis=1
        )
        flipped = lax.associative_scan(
            affine_combine, (jnp.flip(keep_next, 1), jnp.flip(drive, 1)), axis=1
        )[1]
        return (jnp.flip(flipped, 1), None)
    states = lax.associative_scan(affine_combine, (keep_rate, drive), axis=1)[1]
    before = jnp.concatenate([jnp.zeros_like(states[:, :1, :]), states[:, :-1, :]], axis=1)
    return (states, before)


def row_scale(values):
    return lax.rsqrt(jnp.mean(values * values, axis=-1, keepdims=True) + NORM_EPS)


def forward_proj(acts, weight):
    return jnp.einsum("std,dx->stx", acts, weight, preferred_element_type=jnp.float32)


def backward_proj(acts, weight):
    return jnp.einsum("stx,dx->std", acts, weight, preferred_element_type=jnp.float32)


def weight_grad(left_acts, right_acts):
    return jnp.einsum("std,stx->dx", left_acts, right_acts, preferred_element_type=jnp.float32)


def own_rows(values, piece_len, tok_start):
    return lax.dynamic_slice_in_dim(values, tok_start, piece_len, 1)


def collect_branch(branch_part):
    return lax.psum(branch_part, "mp")


def collect_normed_grad(grad_part):
    return lax.psum(grad_part, "mp")


def norm_back(resid_in, scale_rows, gain, grad_norm, grad_now, piece_len, tok_start):
    unit_rows = resid_in * scale_rows
    scaled_grad = grad_norm * gain
    grad_now = grad_now + scale_rows * (
        scaled_grad - unit_rows * jnp.mean(scaled_grad * unit_rows, axis=-1, keepdims=True)
    )
    gain_part = jnp.sum(own_rows(grad_norm * unit_rows, piece_len, tok_start), axis=(0, 1))
    return (grad_now, gain_part)


def turn_right(grads, blocks, inverse):
    size = blocks.shape[-1]
    tiles = grads.reshape(grads.shape[:3] + (grads.shape[3] // size, size))
    form = "lkdbj,lkbij->lkdbi" if inverse else "lkdbi,lkbij->lkdbj"
    return jnp.einsum(form, tiles, blocks, precision=HIGHEST).reshape(grads.shape)


def adam_moments(grads, first, second, fix_one, fix_two):
    first = BETA_ONE * first + (1.0 - BETA_ONE) * grads
    second = BETA_TWO * second + (1.0 - BETA_TWO) * grads * grads
    moves = first / fix_one / (jnp.sqrt(second / fix_two) + ADAM_EPS)
    return (first, second, moves)


def per_device(
    inputs,
    cotangent,
    lengths,
    hidden_weights,
    mlp_weights,
    norm_gains,
    gate_bias,
    left_bases,
    hidden_blocks,
    mlp_blocks,
    hidden_first,
    hidden_second,
    mlp_first,
    mlp_second,
    gain_first,
    gain_second,
    bias_first,
    bias_second,
    step_count,
    row_owner,
):
    piece_len = inputs.shape[1]
    tok_start = lax.axis_index("mp") * piece_len
    whole_in, whole_cot = (
        lax.all_gather(inputs, "mp", axis=1, tiled=True),
        lax.all_gather(cotangent, "mp", axis=1, tiled=True),
    )
    residual = whole_in.astype(jnp.float32)
    seed_grad = whole_cot.astype(jnp.float32)
    span_len = residual.shape[1]
    positions = jnp.arange(span_len, dtype=jnp.int32)
    pad_mask = (positions[None, :] < lengths[:, None]).astype(jnp.float32)[:, :, None]
    hidden_low = hidden_weights.astype(jnp.bfloat16)
    mlp_low = mlp_weights.astype(jnp.bfloat16)
    layer_count = hidden_weights.shape[0]
    kept_layers = []
    for layer_at in range(layer_count):
        w_hidden = hidden_low[layer_at]
        w_mlp = mlp_low[layer_at]
        scale_in = row_scale(residual)
        normed_in = (residual * scale_in * norm_gains[layer_at, 0]).astype(jnp.bfloat16)
        key_forget = forward_proj(normed_in, w_hidden[0]) + gate_bias[layer_at, 0]
        key_input = forward_proj(normed_in, w_hidden[1]) + gate_bias[layer_at, 1]
        key_cand = forward_proj(normed_in, w_hidden[2])
        gate_gap = jax.nn.softplus(-key_forget) - jax.nn.softplus(-key_input)
        keep_rate = jax.nn.sigmoid(-gate_gap)
        take_rate = jax.nn.sigmoid(gate_gap)
        cand_value = candidate(key_cand)
        states, before = linear_scan(keep_rate, take_rate * cand_value, False)
        states_low = states.astype(jnp.bfloat16)
        middle = residual + collect_branch(backward_proj(states_low, w_hidden[3]))
        scale_mid = row_scale(middle)
        normed_mid = (middle * scale_mid * norm_gains[layer_at, 1]).astype(jnp.bfloat16)
        pre_act = forward_proj(normed_mid, w_mlp[0])
        act_low = jax.nn.gelu(pre_act, approximate=False).astype(jnp.bfloat16)
        kept_layers.append(
            (
                residual,
                scale_in,
                normed_in,
                key_forget,
                key_input,
                key_cand,
                keep_rate,
                take_rate,
                cand_value,
                before,
                states_low,
                middle,
                scale_mid,
                normed_mid,
                pre_act,
                act_low,
            )
        )
        residual = middle + collect_branch(backward_proj(act_low, w_mlp[1]))
    output = own_rows(residual * pad_mask, piece_len, tok_start)
    grad_now = seed_grad * pad_mask
    hidden_list = [None] * layer_count
    mlp_list = [None] * layer_count
    gain_list = [None] * layer_count
    bias_list = [None] * layer_count
    for layer_at in reversed(range(layer_count)):
        (
            resid_in,
            scale_in,
            normed_in,
            key_forget,
            key_input,
            key_cand,
            keep_rate,
            take_rate,
            cand_value,
            before,
            states_low,
            middle,
            scale_mid,
            normed_mid,
            pre_act,
            act_low,
        ) = kept_layers[layer_at]
        w_hidden = hidden_low[layer_at]
        w_mlp = mlp_low[layer_at]
        top_low = grad_now.astype(jnp.bfloat16)
        grad_down = weight_grad(top_low, act_low)
        grad_pre = (forward_proj(top_low, w_mlp[1]) * gelu_slope(pre_act)).astype(jnp.bfloat16)
        grad_up = weight_grad(normed_mid, grad_pre)
        grad_mid = collect_normed_grad(backward_proj(grad_pre, w_mlp[0]))
        grad_now, gain_mid_part = norm_back(
            middle, scale_mid, norm_gains[layer_at, 1], grad_mid, grad_now, piece_len, tok_start
        )
        out_low = grad_now.astype(jnp.bfloat16)
        grad_out = weight_grad(out_low, states_low)
        grad_states = forward_proj(out_low, w_hidden[3])
        adjoint = linear_scan(keep_rate, grad_states, True)[0]
        grad_gap = keep_rate * take_rate * adjoint * (cand_value - before)
        grad_keys = jnp.stack(
            [
                -grad_gap * jax.nn.sigmoid(-key_forget),
                grad_gap * jax.nn.sigmoid(-key_input),
                adjoint * take_rate * candidate_slope(key_cand),
            ]
        ).astype(jnp.bfloat16)
        grad_inproj = jnp.einsum(
            "std,kstx->kdx", normed_in, grad_keys, preferred_element_type=jnp.float32
        )
        bias_list[layer_at] = jnp.sum(grad_keys[:2].astype(jnp.float32), axis=(1, 2))
        grad_norm_in = collect_normed_grad(
            jnp.einsum("kstx,kdx->std", grad_keys, w_hidden[:3], preferred_element_type=jnp.float32)
        )
        grad_now, gain_in_part = norm_back(
            resid_in,
            scale_in,
            norm_gains[layer_at, 0],
            grad_norm_in,
            grad_now,
            piece_len,
            tok_start,
        )
        hidden_list[layer_at] = jnp.concatenate([grad_inproj, grad_out[None]], axis=0)
        mlp_list[layer_at] = jnp.stack([grad_up, grad_down])
        gain_list[layer_at] = jnp.stack([gain_in_part, gain_mid_part])
    input_grad = own_rows(grad_now, piece_len, tok_start)
    grad_hidden = jnp.stack(hidden_list)
    grad_mlp = jnp.stack(mlp_list)
    turned_hidden = turn_right(grad_hidden, hidden_blocks, False)
    turned_mlp = turn_right(grad_mlp, mlp_blocks, False)
    left_hidden = left_bases[:, :4]
    left_mlp = left_bases[:, 4:]
    width_d = grad_hidden.shape[2]
    width_h = grad_hidden.shape[3]
    width_f = grad_mlp.shape[3]
    dp_count = lax.axis_size("dp")
    row_share = width_d // dp_count
    hidden_cols = layer_count * 4 * width_h
    owner_ids = jnp.arange(dp_count, dtype=jnp.int32)
    source_block = jnp.sum(
        owner_ids[None, :] * (row_owner[None, :] == owner_ids[:, None]).astype(jnp.int32), axis=1
    )

    def source_rows(row_count):
        stored = jnp.arange(row_count, dtype=jnp.int32)
        return jnp.take(source_block, stored // row_share) * row_share + stored % row_share

    picked = source_rows(row_share * lax.axis_size("dp"))
    part_hidden = jnp.take(left_hidden, picked, axis=3)
    part_mlp = jnp.take(left_mlp, picked, axis=3)
    rot_hidden = jnp.einsum("lkdc,lkdx->clkx", part_hidden, turned_hidden, precision=HIGHEST)
    rot_mlp = jnp.einsum("lkdc,lkdx->clkx", part_mlp, turned_mlp, precision=HIGHEST)
    summed = lax.psum_scatter(
        jnp.concatenate(
            [
                rot_hidden.reshape(row_share * lax.axis_size("dp"), -1),
                rot_mlp.reshape(row_share * lax.axis_size("dp"), -1),
            ],
            axis=1,
        ),
        "dp",
        scatter_dimension=0,
        tiled=True,
    )
    hidden_grad = summed[:, :hidden_cols].reshape(row_share, layer_count, 4, width_h)
    mlp_grad = summed[:, hidden_cols:].reshape(row_share, layer_count, 2, width_f)
    count_value = step_count[0].astype(jnp.float32)
    fix_one = 1.0 - jnp.power(jnp.float32(BETA_ONE), count_value)
    fix_two = 1.0 - jnp.power(jnp.float32(BETA_TWO), count_value)
    hidden_first_new, hidden_second_new, hidden_moves = adam_moments(
        hidden_grad, hidden_first, hidden_second, fix_one, fix_two
    )
    mlp_first_new, mlp_second_new, mlp_moves = adam_moments(
        mlp_grad, mlp_first, mlp_second, fix_one, fix_two
    )
    empty = (jnp.zeros(grad_hidden.shape, jnp.float32), jnp.zeros(grad_mlp.shape, jnp.float32))
    pieces = (
        lax.all_gather(hidden_moves.astype(jnp.bfloat16), "dp", axis=0, tiled=True).astype(
            jnp.float32
        ),
        lax.all_gather(mlp_moves.astype(jnp.bfloat16), "dp", axis=0, tiled=True).astype(
            jnp.float32
        ),
    )
    row_count = pieces[0].shape[0]
    picked = source_rows(row_count)
    cols_hidden = jnp.take(left_hidden, picked, axis=3)
    cols_mlp = jnp.take(left_mlp, picked, axis=3)
    back_hidden = empty[0] + jnp.einsum(
        "lkdc,clkx->lkdx", cols_hidden, pieces[0], precision=HIGHEST
    )
    back_mlp = empty[1] + jnp.einsum("lkdc,clkx->lkdx", cols_mlp, pieces[1], precision=HIGHEST)
    hidden_new = hidden_weights - MATRIX_RATE * (
        turn_right(back_hidden, hidden_blocks, True) + DECAY_RATE * hidden_weights
    )
    mlp_new = mlp_weights - MATRIX_RATE * (
        turn_right(back_mlp, mlp_blocks, True) + DECAY_RATE * mlp_weights
    )
    gain_local = jnp.stack(gain_list)
    bias_local = jnp.stack(bias_list)
    column_at = lax.axis_index("mp") * width_h
    bias_whole = jnp.zeros((layer_count, 2, width_h * lax.axis_size("mp")), jnp.float32)
    bias_whole = lax.dynamic_update_slice_in_dim(bias_whole, bias_local, column_at, 2)
    gain_grad, bias_summed = lax.psum((gain_local, bias_whole), ("dp", "mp"))
    bias_grad = lax.dynamic_slice_in_dim(bias_summed, column_at, width_h, 2)
    gain_first_new, gain_second_new, gain_moves = adam_moments(
        gain_grad, gain_first, gain_second, fix_one, fix_two
    )
    bias_first_new, bias_second_new, bias_moves = adam_moments(
        bias_grad, bias_first, bias_second, fix_one, fix_two
    )
    gain_new = norm_gains - GAIN_RATE * gain_moves
    bias_new = gate_bias - BIAS_RATE * bias_moves
    return (
        output,
        input_grad,
        hidden_grad,
        hidden_first_new,
        hidden_second_new[:, :, 2:],
        hidden_second_new[:, :, :2],
        hidden_new,
        mlp_grad,
        mlp_first_new,
        mlp_second_new,
        mlp_new,
        gain_grad,
        gain_first_new,
        gain_second_new,
        gain_new,
        bias_grad,
        bias_first_new,
        bias_second_new,
        bias_new,
    )


def solution(mesh):
    in_specs = (
        P("dp", "mp", None),
        P("dp", "mp", None),
        P("dp"),
        P(None, None, None, "mp"),
        P(None, None, None, "mp"),
        P(),
        P(None, None, "mp"),
        P(),
        P(None, None, "mp", None, None),
        P(None, None, "mp", None, None),
        P("dp", None, None, "mp"),
        P("dp", None, None, "mp"),
        P("dp", None, None, "mp"),
        P("dp", None, None, "mp"),
        P(),
        P(),
        P(None, None, "mp"),
        P(None, None, "mp"),
        P(),
        P(),
    )
    out_specs = (
        P("dp", "mp", None),
        P("dp", "mp", None),
        P("dp", None, None, "mp"),
        P("dp", None, None, "mp"),
        P("dp", None, None, "mp"),
        P("dp", None, None, "mp"),
        P(None, None, None, "mp"),
        P("dp", None, None, "mp"),
        P("dp", None, None, "mp"),
        P("dp", None, None, "mp"),
        P(None, None, None, "mp"),
        P(),
        P(),
        P(),
        P(),
        P(None, None, "mp"),
        P(None, None, "mp"),
        P(None, None, "mp"),
        P(None, None, "mp"),
    )
    return jax.shard_map(
        per_device, mesh=mesh, in_specs=in_specs, out_specs=out_specs, check_vma=False
    )
```

profile of v0, /device:TPU:0, one launch (start us, length us, event | category | flops | bytes accessed | tf_op | source)
XLA Modules:
  0.0 2653.6 jit_solution(502368849520886063)
XLA Ops:
  301.1 16.6 pad.292
  317.7 16.5 pad.293
  350.2 23.7 all-reduce.102.cloned.1.call-done
  388.1 20.3 fusion.123
  409.1 29.1 %all-reduce.104.cloned.1.call-done = f32[1,2048,512]{2,1,0:T(8,128)} async-done(((f32[1,2048,512]{2,1,0:T(8,128)}), f32[1,2048,512]{2,1,0:T(8,128)}) %all-reduce.104.cloned.1.call-update) | async-done | bytes 4194320 | tf_op jit(solution)/shard_map/psum | solution.py:70
  723.7 16.6 pad.314
  740.3 16.5 pad.315
  775.2 21.1 all-reduce.106.cloned.1.call-done
  806.5 25.1 fusion.32
  902.1 17.1 slice.1377
  919.2 16.7 slice.1384
  935.9 16.7 slice.1379
  974.7 32.8 %reverse.12 = f32[2048,512]{1,0:T(8,128)} reverse(f32[2048,512]{1,0:T(8,128)} %fusion.165), dimensions={0} | reverse | bytes 8388608 | tf_op jit(solution)/shard_map/reverse
  1227.5 16.5 pad.336
  1244.0 16.5 pad.337
  1266.9 32.8 %rev.16 = f32[1,2048,512]{2,1,0:T(8,128)} reverse(f32[1,2048,512]{2,1,0:T(8,128)} %add.1007), dimensions={1} | reverse | bytes 8388608 | tf_op jit(solution)/shard_map/jit(_flip)/rev | solution.py:43
  1328.3 23.2 gather_fusion.1
  1375.0 24.3 gather_fusion
  1456.1 17.1 slice.1467
  1473.2 16.7 slice.1474
  1489.9 16.6 slice.1469
  1543.1 24.9 fusion.23
  1653.1 32.6 %reverse.13 = f32[2048,512]{1,0:T(8,128)} reverse(f32[2048,512]{1,0:T(8,128)} %fusion.161), dimensions={0} | reverse | bytes 8388608 | tf_op jit(solution)/shard_map/reverse.4
  1922.7 16.6 pad.359
  1945.7 32.6 %rev.18 = f32[1,2048,512]{2,1,0:T(8,128)} reverse(f32[1,2048,512]{2,1,0:T(8,128)} %add.1045), dimensions={1} | reverse | bytes 8388608 | tf_op jit(solution)/shard_map/jit(_flip)/rev | solution.py:43
  2014.9 17.5 fusion.407
  2053.0 22.1 fusion.126
  2082.3 318.2 %reduce-scatter.2.cloned.1.call-done = f32[32,8192]{1,0:T(8,128)} async-done(((f32[512,8192]{1,0:T(8,128)}), f32[32,8192]{1,0:T(8,128)}) %reduce-scatter.2.cloned.1.call-update) | async-done | bytes 1048592 | tf_op jit(solution)/shard_map/reduce_scatter | solution.py:271
  2425.1 23.6 all-reduce.114.cloned.1.call-done
  2455.9 41.1 %all-reduce.92 = (f32[2,2,512]{2,1,0:T(2,128)S(1)}, f32[2,2,1024]{2,1,0:T(2,128)S(1)}) all-reduce(f32[2,2,512]{2,1,0:T(2,128)S(1)} %pad_maximum_fusion.43, f32[2,2,1024]{2,1,0:T(2,128)S(1)} %maximum_dynamic-update-slice_fusion), channel_id=1, replica_groups=mesh['dp'=16,'mp'=2] {'dp','mp'}, use_global_device_ids=true, to_apply=%region_22.26 | all-reduce | flops 6144 | bytes 49152 | tf_op jit(solution)/shard_map/psum | solution.py:322
  2507.1 22.1 all-gather.9.cloned.1.call-done
  2570.9 35.4 %all-gather.11.cloned.1.call-done = bf16[512,2,2,1024]{3,0,2,1:T(8,128)(2,1)} async-done(((bf16[32,2,2,1024]{3,0,2,1:T(8,128)(2,1)}), bf16[512,2,2,1024]{3,0,2,1:T(8,128)(2,1)}) %all-gather.11.cloned.1.call-update) | async-done | bytes 4194320 | tf_op jit(solution)/shard_map/all_gather | solution.py:299
  (1059 shorter events, 1615.2 us)
Async XLA Ops:
  7.2 1997.3 %copy-start = (f32[2,4,4,128,128]{4,3,2,1,0:T(8,128)S(1)}, f32[2,4,4,128,128]{4,3,2,1,0:T(8,128)}, u32[]{:S(2)}) copy-start(f32[2,4,4,128,128]{4,3,2,1,0:T(8,128)} %param.34) | copy-start | bytes 6291460
  7.2 15.7 all-gather.5.cloned.1.call-start
  8.0 365.9 %all-reduce.102.cloned.1.call-start = ((), (), s32[]{:S(2)}) async-start(), calls=%async_computation.2 | async-start | bytes 8388608 | tf_op jit(solution)/shard_map/psum | solution.py:70
  14.5 58.0 %copy-start.164 = (f32[1,1,512]{2,1,0:T(1,128)}, f32[1,1,512]{2,1,0:T(1,128)S(1)}, u32[]{:S(2)}) copy-start(f32[1,1,512]{2,1,0:T(1,128)S(1)} %get-tuple-element.202) | copy-start | bytes 6148
  25.0 47.5 %copy-start.110 = (f32[2048]{0:T(1024)}, f32[2048]{0:T(1024)S(1)}, u32[]{:S(2)}) copy-start(f32[2048]{0:T(1024)S(1)} %add_rsqrt_fusion.3) | copy-start | bytes 24580
  237.3 23.0 copy-start.78
  344.1 94.1 %all-reduce.104.cloned.1.call-start = ((), (), s32[]{:S(2)}) async-start(), calls=%async_computation.3 | async-start | bytes 8388608 | tf_op jit(solution)/shard_map/psum | solution.py:70
  408.5 358.9 %all-gather.7.cloned.1.call-start = ((), (), s32[]{:S(2)}) async-start(), calls=%async_computation.5 | async-start | bytes 3145728 | tf_op jit(solution)/shard_map/all_gather | solution.py:127
  409.1 34.0 %copy-start.128 = (f32[1,1,512]{2,1,0:T(1,128)S(1)}, f32[1,1,512]{2,1,0:T(1,128)}, u32[]{:S(2)}) copy-start(f32[1,1,512]{2,1,0:T(1,128)} %get-tuple-element.200) | copy-start | bytes 6148
  409.1 387.3 %all-reduce.106.cloned.1.call-start = ((), (), s32[]{:S(2)}) async-start(), calls=%async_computation.4 | async-start | bytes 8388608 | tf_op jit(solution)/shard_map/psum | solution.py:70
  766.6 192.4 %all-reduce.108.cloned.1.call-start = ((), (), s32[]{:S(2)}) async-start(), calls=%async_computation.6 | async-start | bytes 8388608 | tf_op jit(solution)/shard_map/psum | solution.py:74
  767.3 196.1 %copy-start.112 = (f32[2048]{0:T(1024)}, f32[2048]{0:T(1024)S(1)}, u32[]{:S(2)}) copy-start(f32[2048]{0:T(1024)S(1)} %fusion.254) | copy-start | bytes 24580
  802.6 28.9 %copy-start.44 = (f32[1,2048,512]{2,1,0:T(8,128)}, f32[1,2048,512]{2,1,0:T(8,128)S(1)}, u32[]{:S(2)}) copy-start(f32[1,2048,512]{2,1,0:T(8,128)S(1)} %broadcast_multiply_fusion) | copy-start | bytes 12582916
  841.3 690.7 %all-reduce.110.cloned.1.call-start = ((), (), s32[]{:S(2)}) async-start(), calls=%async_computation.7 | async-start | bytes 8388608 | tf_op jit(solution)/shard_map/psum | solution.py:74
  1163.6 23.0 copy-start.80
  1266.9 32.8 %copy-start.139 = (f32[1,1,512]{2,1,0:T(1,128)S(1)}, f32[1,1,512]{2,1,0:T(1,128)}, u32[]{:S(2)}) copy-start(f32[1,1,512]{2,1,0:T(1,128)} %get-tuple-element.207) | copy-start | bytes 6148
  1318.2 319.8 %all-reduce.112.cloned.1.call-start = ((), (), s32[]{:S(2)}) async-start(), calls=%async_computation.8 | async-start | bytes 8388608 | tf_op jit(solution)/shard_map/psum | solution.py:74
  1543.1 24.9 copy-start.36
  1577.1 823.5 %reduce-scatter.2.cloned.1.call-start = ((), (), s32[]{:S(2)}) async-start(), calls=%async_computation.9 | async-start | bytes 17825792 | tf_op jit(solution)/shard_map/reduce_scatter | solution.py:271
  1945.7 32.6 %copy-start.137 = (f32[1,1,512]{2,1,0:T(1,128)S(1)}, f32[1,1,512]{2,1,0:T(1,128)}, u32[]{:S(2)}) copy-start(f32[1,1,512]{2,1,0:T(1,128)} %copy-done.136) | copy-start | bytes 6148
  2052.9 395.8 %all-reduce.114.cloned.1.call-start = ((), (), s32[]{:S(2)}) async-start(), calls=%async_computation.12 | async-start | bytes 16777216 | tf_op jit(solution)/shard_map/psum | solution.py:70
  2081.6 447.7 %all-gather.9.cloned.1.call-start = ((), (), s32[]{:S(2)}) async-start(), calls=%async_computation.10 | async-start | bytes 4456448 | tf_op jit(solution)/shard_map/all_gather | solution.py:296
  2406.4 199.9 %all-gather.11.cloned.1.call-start = ((), (), s32[]{:S(2)}) async-start(), calls=%async_computation.11 | async-start | bytes 4456448 | tf_op jit(solution)/shard_map/all_gather | solution.py:299
  2454.0 43.1 %copy-start.125 = (f32[2,2,512]{2,1,0:T(2,128)S(1)}, f32[2,2,512]{2,1,0:T(2,128)}, u32[]{:S(2)}) copy-start(f32[2,2,512]{2,1,0:T(2,128)} %param.31) | copy-start | bytes 24580
  2454.0 43.1 %copy-start.127 = (f32[2,2,512]{2,1,0:T(2,128)S(1)}, f32[2,2,512]{2,1,0:T(2,128)}, u32[]{:S(2)}) copy-start(f32[2,2,512]{2,1,0:T(2,128)} %param.32) | copy-start | bytes 24580
  2454.0 43.1 %copy-start.186 = (f32[2,2,512]{2,1,0:T(2,128)S(1)}, f32[2,2,512]{2,1,0:T(2,128)}, u32[]{:S(2)}) copy-start(f32[2,2,512]{2,1,0:T(2,128)} %param.43) | copy-start | bytes 24580
  2454.0 43.1 %copy-start.187 = (f32[2,2,512]{2,1,0:T(2,128)S(1)}, f32[2,2,512]{2,1,0:T(2,128)}, u32[]{:S(2)}) copy-start(f32[2,2,512]{2,1,0:T(2,128)} %param.42) | copy-start | bytes 24580
  2454.0 43.1 %copy-start.188 = (f32[2,2,512]{2,1,0:T(2,128)S(1)}, f32[2,2,512]{2,1,0:T(2,128)}, u32[]{:S(2)}) copy-start(f32[2,2,512]{2,1,0:T(2,128)} %param.41) | copy-start | bytes 24580
  2454.0 43.1 %copy-start.189 = (f32[2,2,512]{2,1,0:T(2,128)S(1)}, f32[2,2,512]{2,1,0:T(2,128)}, u32[]{:S(2)}) copy-start(f32[2,2,512]{2,1,0:T(2,128)} %param.40) | copy-start | bytes 24580
  2454.1 43.7 %dynamic-slice-start.1 = ((f32[2048]{0:T(1024)}, s32[]{:T(128)}), f32[1024]{0:T(1024)S(1)}, s32[]{:S(2)}) async-start(f32[2048]{0:T(1024)} %copy-done.112, s32[]{:T(128)} %select_n.94), calls=%async_computation.16 | async-start | bytes 8704 | tf_op jit(solution)/shard_map/dynamic_slice | solution.py:66
  2455.9 45.8 %copy-start.71 = (f32[32,2,4,512]{3,0,2,1:T(8,128)S(1)}, f32[32,2,4,512]{3,0,2,1:T(8,128)}, u32[]{:S(2)}) copy-start(f32[32,2,4,512]{3,0,2,1:T(8,128)} %get-tuple-element.95) | copy-start | bytes 1572868
  2455.9 46.9 %copy-start.70 = (f32[32,2,4,512]{3,0,2,1:T(8,128)S(1)}, f32[32,2,4,512]{3,0,2,1:T(8,128)}, u32[]{:S(2)}) copy-start(f32[32,2,4,512]{3,0,2,1:T(8,128)} %get-tuple-element.94) | copy-start | bytes 1572868
  (180 other events, 1738.2 us)
Sparse Core Ops, SparseCore 0:
  9.6 13.2 all-gather.4
  344.2 29.5 all-reduce.101
  408.6 29.5 all-reduce.103
  439.6 11.7 all-gather.6
  766.7 29.5 all-reduce.105
  841.4 29.6 all-reduce.107
  1318.4 29.5 all-reduce.109
  1577.2 29.6 all-reduce.111
  2053.0 347.5 reduce-scatter.1
  2404.1 44.5 all-reduce.113
  2451.5 77.7 all-gather.8
  2531.9 74.4 all-gather.10
where the time goes:
time: 2700 us; the launch traced here: 2650 us
  local copies, waits for them, and re-layouts  1410 us (52%)
  waiting for transfers between devices  483 us (18%)
  other arithmetic  401 us (15%)
  matrix products  298 us (11%)
  blocking collectives  41.1 us (2%)
    slice x140, local copies, waits for them, and re-layouts, linear_scan(): lax.associative_scan(affine_combine, (jnp.flip(keep_next, 1), jnp.flip(dr...  474 us
    slice x134, local copies, waits for them, and re-layouts, linear_scan(): states = lax.associative_scan(affine_combine, (keep_rate, drive), axis=1)[1]  373 us
    reduce_scatter x1, waiting for transfers between devices, per_device(): lax.psum_scatter(jnp.concatenate([rot_hidden.reshape(row_share * lax.axis...  318 us
    pad x40, local copies, waits for them, and re-layouts, linear_scan(): lax.associative_scan(affine_combine, (jnp.flip(keep_next, 1), jnp.flip(dr...  109 us
    pad x40, local copies, waits for them, and re-layouts, linear_scan(): states = lax.associative_scan(affine_combine, (keep_rate, drive), axis=1)[1]  109 us
    psum x4, waiting for transfers between devices, collect_branch(): return lax.psum(branch_part, 'mp')  97.5 us
    mul x36, other arithmetic, affine_combine(): return (earlier[0] * later[0], later[0] * earlier[1] + later[1])  89.2 us
    dot_general x12, matrix products, forward_proj(): jnp.einsum('std,dx->stx', acts, weight, preferred_element_type=jnp.float32)  87.5 us
  transfers between devices with their start and end apart: 12, of which 8 were waited for; matrix products, arithmetic and copies ran while one was open for 32% of the time, Pallas kernels for 0%

commit v1 on v0

v1 whole, which is shorter than its diff:
```python
import functools
import jax
import jax.numpy as jnp
from jax import lax
from jax.experimental import pallas as pl
from jax.experimental.pallas import tpu as pltpu
from jax.sharding import PartitionSpec as P

NORM_EPS = 1e-05
BETA_ONE = 0.9
BETA_TWO = 0.95
ADAM_EPS = 1e-08
MATRIX_RATE = 0.08
GAIN_RATE = 0.5
BIAS_RATE = 4.0
DECAY_RATE = 0.01
BF = jnp.bfloat16
F32 = jnp.float32
SEG = 8
TILE_STEPS = 32
HC = 512
VMEM_LIMIT = 58 * 1024 * 1024
LOG2E = 1.4426950408889634


def dot_nn(a, b):
    return lax.dot_general(a, b, (((1,), (0,)), ((), ())), preferred_element_type=F32)


def dot_nt(a, b):
    return lax.dot_general(a, b, (((1,), (1,)), ((), ())), preferred_element_type=F32)


def dot_tn(a, b):
    return lax.dot_general(a, b, (((0,), (0,)), ((), ())), preferred_element_type=F32)


def recip(x):
    r = pl.reciprocal(x, approx=True)
    return r * (2.0 - x * r)


def rows_loop(count, size, body, init=None, unroll=1):
    def step(i, carry):
        return body(pl.ds(pl.multiple_of(i * size, size), size), carry)

    return lax.fori_loop(0, count // size, step, init, unroll=unroll)


def row_scale(values):
    return lax.rsqrt(jnp.mean(values * values, axis=-1, keepdims=True) + NORM_EPS)


def norm_stage(x_ref, gain, out_ref):
    def body(r, c):
        x = x_ref[r, :]
        out_ref[r, :] = (x * row_scale(x) * gain).astype(BF)
        return c

    rows_loop(x_ref.shape[0], 32, body, 0)


def gate_stage(nin_ref, bias_ref, w_refs, kbuf, state, outs):
    a_ref, loc_ref, prod_ref, cand_ref, wf_ref, wi_ref, q_ref = outs
    rows = nin_ref.shape[0]
    part = w_refs[0].shape[2]
    hc = min(HC, part)
    for j, w in enumerate(w_refs):
        for c0 in range(0, part, hc):
            cols = slice(j * part + c0, j * part + c0 + hc)
            n = nin_ref[...]
            for k in range(3):
                kbuf[k, :, :hc] = dot_nn(n, w[k, :, c0 : c0 + hc])
            bias_f = bias_ref[0:1, cols]
            bias_i = bias_ref[1:2, cols]

            def body(r, carry):
                loc, prod = carry
                kf = kbuf[0, r, :hc] + bias_f
                ki = kbuf[1, r, :hc] + bias_i
                kc = kbuf[2, r, :hc]
                tf = jnp.exp(-jnp.abs(kf))
                ti = jnp.exp(-jnp.abs(ki))
                tc = jnp.exp(-jnp.abs(kc))
                of, oi = 1.0 + tf, 1.0 + ti
                gap = jnp.minimum(ki, 0.0) - jnp.minimum(kf, 0.0)
                e = jnp.exp(-jnp.abs(gap))
                nf = jnp.where(gap < 0, of * e, of)
                ni = jnp.where(gap > 0, oi * e, oi)
                inv = recip(nf + ni)
                keep = ni * inv
                take = nf * inv
                sf = jnp.where(kf >= 0, tf, 1.0) * recip(of)
                si = jnp.where(ki >= 0, ti, 1.0) * recip(oi)
                sc = tc * recip(1.0 + tc)
                up = kc >= 0
                cand = jnp.where(up, kc + 0.5, sc)
                slope = jnp.where(up, 1.0, sc * (1.0 - sc))
                both = keep * take
                a_ref[r, cols] = keep
                cand_ref[r, cols] = cand.astype(BF)
                wf_ref[r, cols] = (both * sf).astype(BF)
                wi_ref[r, cols] = (both * si).astype(BF)
                q_ref[r, cols] = (take * slope).astype(BF)
                drive = take * cand
                loc0 = keep[:8] * loc + drive[:8]
                prod0 = keep[:8] * prod
                loc1 = keep[8:] * loc0 + drive[8:]
                prod1 = keep[8:] * prod0
                loc_ref[r, cols] = jnp.concatenate([loc0, loc1])
                prod_ref[r, cols] = jnp.concatenate([prod0, prod1])
                return loc1, prod1

            loc, prod = rows_loop(rows, 16, body, (state[0, :, cols], state[1, :, cols]))
            state[0, :, cols] = loc
            state[1, :, cols] = prod


def fold_forward(state, ends_ref, fin_ref, part):
    hidden = state.shape[2]
    ends_ref[...] = state[...]
    loc = state[0, 0:1, :]
    prod = state[1, 0:1, :]
    for s in range(1, SEG):
        loc = state[0, s : s + 1, :] + state[1, s : s + 1, :] * loc
        prod = state[1, s : s + 1, :] * prod
    n = hidden // part
    for j in range(n):
        src = slice(((j + 1) % n) * part, ((j + 1) % n) * part + part)
        fin_ref[0:1, j * part : (j + 1) * part] = loc[:, src]
        fin_ref[1:2, j * part : (j + 1) * part] = prod[:, src]


def fold_backward(state, ends_ref, fin_ref, part):
    hidden = state.shape[2]
    ends_ref[...] = state[...]
    mu = state[0, SEG - 1 : SEG, :]
    prod = state[1, SEG - 1 : SEG, :]
    for s in reversed(range(SEG - 1)):
        mu = state[0, s : s + 1, :] + state[1, s : s + 1, :] * mu
        prod = state[1, s : s + 1, :] * prod
    n = hidden // part
    for j in range(n):
        src = slice(((j - 1) % n) * part, ((j - 1) % n) * part + part)
        fin_ref[0:1, j * part : (j + 1) * part] = mu[:, src]
        fin_ref[1:2, j * part : (j + 1) * part] = prod[:, src]


def carry_forward(inc_ref, ends_ref, start, live):
    start[0:1, :] = inc_ref[0:1, :] * live
    for s in range(SEG - 1):
        start[s + 1 : s + 2, :] = (
            ends_ref[0, s : s + 1, :] + ends_ref[1, s : s + 1, :] * start[s : s + 1, :]
        )


def carry_backward(inc_ref, ends_ref, start, live):
    start[SEG - 1 : SEG, :] = inc_ref[0:1, :] * live
    for s in reversed(range(1, SEG)):
        start[s - 1 : s, :] = (
            ends_ref[0, s : s + 1, :] + ends_ref[1, s : s + 1, :] * start[s : s + 1, :]
        )


def state_stage(first, start, ins, hlow_ref, cf_ref, ci_ref):
    loc_ref, prod_ref, loc_before, prod_before, cand_ref, wf_ref, wi_ref = ins
    rows, hidden = loc_ref.shape
    hc = min(HC, hidden)
    for c0 in range(0, hidden, hc):
        cols = slice(c0, c0 + hc)
        c = start[:, cols]
        before = jnp.where(first, c, loc_before[:, cols] + prod_before[:, cols] * c)

        def body(r, before):
            loc = loc_ref[r, cols]
            prod = prod_ref[r, cols]
            h0 = loc[:8] + prod[:8] * c
            h1 = loc[8:] + prod[8:] * c
            hlow_ref[r, cols] = jnp.concatenate([h0, h1]).astype(BF)
            diff = cand_ref[r, cols].astype(F32) - jnp.concatenate([before, h0])
            cf_ref[r, cols] = (-wf_ref[r, cols].astype(F32) * diff).astype(BF)
            ci_ref[r, cols] = (wi_ref[r, cols].astype(F32) * diff).astype(BF)
            return h1

        rows_loop(rows, 16, body, before)


def mlp_stage(x_ref, hlow_ref, w_refs, m_refs, gain, kbuf, mid_ref, nmid_ref, act_ref, slope_ref, xn_ref):
    rows = x_ref.shape[0]
    part = w_refs[0].shape[2]
    total = x_ref[...]
    for j, w in enumerate(w_refs):
        total = total + dot_nt(hlow_ref[:, j * part : (j + 1) * part], w[0])
    mid_ref[...] = total
    norm_stage(mid_ref, gain, nmid_ref)
    wide = m_refs[0].shape[2]
    fc = min(HC, wide)
    xn_ref[...] = mid_ref[...]
    for j, m in enumerate(m_refs):
        for c0 in range(0, wide, fc):
            cols = slice(j * wide + c0, j * wide + c0 + fc)
            kbuf[0, :, :fc] = dot_nn(nmid_ref[...], m[0, :, c0 : c0 + fc])

            def body(r, c):
                pre = kbuf[0, r, :fc]
                size = jnp.abs(pre)
                t = recip(1.0 + size * (0.3275911 * 0.7071067811865476))
                bell = jnp.exp(pre * pre * -0.5)
                poly = (
                    (((1.061405429 * t - 1.453152027) * t + 1.421413741) * t - 0.284496736) * t
                    + 0.254829592
                ) * t
                tail = (0.5 * poly) * bell
                cdf = jnp.where(pre >= 0, 1.0 - tail, tail)
                act_ref[r, cols] = (pre * cdf).astype(BF)
                slope_ref[r, cols] = (cdf + pre * (bell * 0.3989422804014327)).astype(BF)
                return c

            rows_loop(rows, 16, body, 0)
        xn_ref[...] = xn_ref[...] + dot_nt(act_ref[:, j * wide : (j + 1) * wide], m[1])


def norm_back_stage(src_ref, gain, dn_ref, dx_ref, sums_ref, low_ref):
    def body(r, total):
        x = src_ref[r, :]
        scale = row_scale(x)
        unit = x * scale
        d = dn_ref[r, :]
        e = d * gain
        dx = dx_ref[r, :] + scale * (e - unit * jnp.mean(e * unit, axis=-1, keepdims=True))
        dx_ref[r, :] = dx
        if low_ref is not None:
            low_ref[r, :] = dx.astype(BF)
        g = d * unit
        return total + g[:8] + g[8:16] + g[16:24] + g[24:]

    sums_ref[...] = rows_loop(src_ref.shape[0], 32, body, sums_ref[...])


def mlp_back_stage(dx_ref, slope_ref, mid_ref, m_refs, gain, kbuf, dn_ref, dz_ref, dpre_ref, dout_ref, sums_ref):
    rows = dx_ref.shape[0]
    dz_ref[...] = dx_ref[...].astype(BF)
    wide = m_refs[0].shape[2]
    fc = min(HC, wide)
    total = None
    for j, m in enumerate(m_refs):
        for c0 in range(0, wide, fc):
            cols = slice(j * wide + c0, j * wide + c0 + fc)
            kbuf[0, :, :fc] = dot_nn(dz_ref[...], m[1, :, c0 : c0 + fc])

            def body(r, c):
                dpre_ref[r, cols] = (kbuf[0, r, :fc] * slope_ref[r, cols].astype(F32)).astype(BF)
                return c

            rows_loop(rows, 32, body, 0)
        term = dot_nt(dpre_ref[:, j * wide : (j + 1) * wide], m[0])
        if j == 0:
            dn_ref[...] = term
        else:
            dn_ref[...] = dn_ref[...] + term
    norm_back_stage(mid_ref, gain, dn_ref, dx_ref, sums_ref, dout_ref)


def adjoint_stage(dout_ref, w_refs, a_ref, kbuf, state, lam_ref, prod_ref):
    rows = dout_ref.shape[0]
    part = w_refs[0].shape[2]
    hc = min(HC, part)
    steps = rows // 16
    for j, w in enumerate(w_refs):
        for c0 in range(0, part, hc):
            cols = slice(j * part + c0, j * part + c0 + hc)
            kbuf[0, :, :hc] = dot_nn(dout_ref[...], w[0, :, c0 : c0 + hc])

            def body(i, carry):
                mu, prod = carry
                r = pl.ds(pl.multiple_of((steps - 1 - i) * 16, 16), 16)
                u = kbuf[0, r, :hc]
                a = a_ref[r, cols]
                lam1 = u[8:] + mu
                mu = a[8:] * lam1
                lam0 = u[:8] + mu
                mu = a[:8] * lam0
                prod0 = prod * a[8:]
                lam_ref[r, cols] = jnp.concatenate([lam0, lam1])
                prod_ref[r, cols] = jnp.concatenate([prod0, prod])
                return mu, prod0 * a[:8]

            mu, prod = lax.fori_loop(0, steps, body, (state[0, :, cols], state[1, :, cols]))
            state[0, :, cols] = mu
            state[1, :, cols] = prod


def keys_stage(start, lam_ref, prod_ref, cf_ref, ci_ref, q_ref, dkf_ref, dki_ref, dkc_ref, bias_ref):
    rows, hidden = lam_ref.shape
    hc = min(HC, hidden)
    for c0 in range(0, hidden, hc):
        cols = slice(c0, c0 + hc)
        c = jnp.concatenate([start[:, cols], start[:, cols]])

        def body(r, sums):
            lam = lam_ref[r, cols] + prod_ref[r, cols] * c
            df = (lam * cf_ref[r, cols].astype(F32)).astype(BF)
            di = (lam * ci_ref[r, cols].astype(F32)).astype(BF)
            dkf_ref[r, cols] = df
            dki_ref[r, cols] = di
            dkc_ref[r, cols] = (lam * q_ref[r, cols].astype(F32)).astype(BF)
            df, di = df.astype(F32), di.astype(F32)
            return sums[0] + df[:8] + df[8:], sums[1] + di[:8] + di[8:]

        sf, si = rows_loop(rows, 16, body, (bias_ref[0, :, cols], bias_ref[1, :, cols]))
        bias_ref[0, :, cols] = sf
        bias_ref[1, :, cols] = si


def keys_back_stage(dk_refs, w_refs, dn_ref):
    part = w_refs[0].shape[2]
    total = None
    for j, w in enumerate(w_refs):
        for k in range(3):
            term = dot_nt(dk_refs[k][:, j * part : (j + 1) * part], w[k])
            total = term if total is None else total + term
    dn_ref[...] = total


def spread(src_ref, dst, lanes):
    steps = src_ref.shape[1]
    for c in range(lanes.shape[0]):
        cols = slice(c * 128, c * 128 + 128)
        for s in range(SEG):
            lanes[c, pl.ds(s, steps, stride=SEG), :] = src_ref[s, :, cols].astype(F32)
        dst[:, cols] = lanes[c]


def gather_out(src, dst_ref, lanes):
    steps = dst_ref.shape[1]
    for c in range(lanes.shape[0]):
        cols = slice(c * 128, c * 128 + 128)
        lanes[c] = src[:, cols]
        for s in range(SEG):
            dst_ref[s, :, cols] = lanes[c, pl.ds(s, steps, stride=SEG), :]


def k_first(n_parts, in_ref, gain_ref, bias_ref, *refs):
    w = refs[:n_parts]
    xp, nin, a, loc, prod, cand, wf, wi, q, ends, fin, kbuf, state, lanes = refs[n_parts:]
    g = pl.program_id(0)

    @pl.when(g == 0)
    def _():
        state[0] = jnp.zeros_like(state[0])
        state[1] = jnp.ones_like(state[1])

    spread(in_ref, xp, lanes)
    norm_stage(xp, gain_ref[0:1, :], nin)
    gate_stage(nin, bias_ref, w, kbuf, state, (a, loc, prod, cand, wf, wi, q))

    @pl.when(g == pl.num_programs(0) - 1)
    def _():
        fold_forward(state, ends, fin, w[0].shape[2])


def k_middle(n_parts, info, inc, ends_in, x, loc, prod, loc_b, prod_b, cand, wf, wi, gain, gain_next, bias, *refs):
    wo = refs[:n_parts]
    m = refs[n_parts : 2 * n_parts]
    w = refs[2 * n_parts : 3 * n_parts]
    (hlow, cf, ci, mid, nmid, act, slope, xn, nin, a, loc_o, prod_o, cand_o, wf_o, wi_o, q_o, ends, fin) = refs[
        3 * n_parts : 3 * n_parts + 18
    ]
    kbuf, state, start = refs[3 * n_parts + 18 :]
    g = pl.program_id(0)

    @pl.when(g == 0)
    def _():
        state[0] = jnp.zeros_like(state[0])
        state[1] = jnp.ones_like(state[1])
        carry_forward(inc, ends_in, start, (info[1] > 0).astype(F32))

    state_stage(g == 0, start, (loc, prod, loc_b, prod_b, cand, wf, wi), hlow, cf, ci)
    mlp_stage(x, hlow, wo, m, gain[1:2, :], kbuf, mid, nmid, act, slope, xn)
    norm_stage(xn, gain_next[0:1, :], nin)
    gate_stage(nin, bias, w, kbuf, state, (a, loc_o, prod_o, cand_o, wf_o, wi_o, q_o))

    @pl.when(g == pl.num_programs(0) - 1)
    def _():
        fold_forward(state, ends, fin, w[0].shape[2])


def k_turn(n_parts, info, inc, ends_in, x, loc, prod, loc_b, prod_b, cand, wf, wi, a, gain, cot, *refs):
    wo = refs[:n_parts]
    m = refs[n_parts : 2 * n_parts]
    (hlow, cf, ci, nmid, act, out, dz, dpre, dout, dx, lam, prod_o, ends, fin, sums) = refs[
        2 * n_parts : 2 * n_parts + 15
    ]
    kbuf, state, start, mid, slope, xn, dn, lanes = refs[2 * n_parts + 15 :]
    g = pl.program_id(0)
    tile = pl.num_programs(0) - 1 - g
    rows = x.shape[0]
    steps_all = pl.num_programs(0) * (rows // SEG)

    @pl.when(g == 0)
    def _():
        state[0] = jnp.zeros_like(state[0])
        state[1] = jnp.ones_like(state[1])
        sums[...] = jnp.zeros_like(sums)
        carry_forward(inc, ends_in, start, (info[1] > 0).astype(F32))

    state_stage(tile == 0, start, (loc, prod, loc_b, prod_b, cand, wf, wi), hlow, cf, ci)
    mlp_stage(x, hlow, wo, m, gain[1:2, :], kbuf, mid, nmid, act, slope, xn)
    at = lax.broadcasted_iota(jnp.int32, (rows, 1), 0)
    place = info[1] * (SEG * steps_all) + (at % SEG) * steps_all + tile * (rows // SEG) + at // SEG
    mask = (place < info[0]).astype(F32)
    xn[...] = xn[...] * mask
    gather_out(xn, out, lanes)
    spread(cot, dx, lanes)
    dx[...] = dx[...] * mask
    mlp_back_stage(dx, slope, mid, m, gain[1:2, :], kbuf, dn, dz, dpre, dout, sums)
    adjoint_stage(dout, wo, a, kbuf, state, lam, prod_o)

    @pl.when(g == pl.num_programs(0) - 1)
    def _():
        fold_backward(state, ends, fin, wo[0].shape[2])


def k_return(n_parts, info, inc, ends_in, lam, prod, cf, ci, q, x, dx_in, mid, slope, a, gain, gain_prev, *refs):
    w = refs[:n_parts]
    m = refs[n_parts : 2 * n_parts]
    wo = refs[2 * n_parts : 3 * n_parts]
    (dkf, dki, dkc, dz, dpre, dout, dx, lam_o, prod_o, ends, fin, sums_in, sums_mid, bias) = refs[
        3 * n_parts : 3 * n_parts + 14
    ]
    kbuf, state, start, dn = refs[3 * n_parts + 14 :]
    g = pl.program_id(0)

    @pl.when(g == 0)
    def _():
        state[0] = jnp.zeros_like(state[0])
        state[1] = jnp.ones_like(state[1])
        sums_in[...] = jnp.zeros_like(sums_in)
        sums_mid[...] = jnp.zeros_like(sums_mid)
        bias[...] = jnp.zeros_like(bias)
        carry_backward(inc, ends_in, start, (info[1] < info[2] - 1).astype(F32))

    keys_stage(start, lam, prod, cf, ci, q, dkf, dki, dkc, bias)
    keys_back_stage((dkf, dki, dkc), w, dn)
    dx[...] = dx_in[...]
    norm_back_stage(x, gain[0:1, :], dn, dx, sums_in, None)
    mlp_back_stage(dx, slope, mid, m, gain_prev[1:2, :], kbuf, dn, dz, dpre, dout, sums_mid)
    adjoint_stage(dout, wo, a, kbuf, state, lam_o, prod_o)

    @pl.when(g == pl.num_programs(0) - 1)
    def _():
        fold_backward(state, ends, fin, wo[0].shape[2])


def k_last(n_parts, info, inc, ends_in, lam, prod, cf, ci, q, x, dx_in, gain, *refs):
    w = refs[:n_parts]
    dkf, dki, dkc, out, sums_in, bias = refs[n_parts : n_parts + 6]
    start, dn, dx, lanes = refs[n_parts + 6 :]
    g = pl.program_id(0)

    @pl.when(g == 0)
    def _():
        sums_in[...] = jnp.zeros_like(sums_in)
        bias[...] = jnp.zeros_like(bias)
        carry_backward(inc, ends_in, start, (info[1] < info[2] - 1).astype(F32))

    keys_stage(start, lam, prod, cf, ci, q, dkf, dki, dkc, bias)
    keys_back_stage((dkf, dki, dkc), w, dn)
    dx[...] = dx_in[...]
    norm_back_stage(x, gain[0:1, :], dn, dx, sums_in, None)
    gather_out(dx, out, lanes)


def k_grads(pairs, *refs):
    out = refs[-1]
    for k, (left, right) in enumerate(pairs):
        out[k] = dot_tn(refs[left][...], refs[right][...]).astype(BF)


def k_rotate(n_recv, share, owner, basis, blocks, own, *refs):
    recv = refs[:n_recv]
    out = refs[n_recv]
    order = blocks.shape[-1]
    total = own[0].astype(F32)
    for ref in recv:
        total = total + ref[0].astype(F32)
    low = total.astype(BF)
    turned = jnp.concatenate(
        [
            dot_nn(low[:, b * order : (b + 1) * order], blocks[0, b].astype(BF))
            for b in range(blocks.shape[1])
        ],
        axis=1,
    ).astype(BF)
    done = dot_tn(basis[0].astype(BF), turned).astype(BF)
    for b in range(done.shape[0] // share):
        at = pl.multiple_of(owner[b] * share, share)
        out[pl.ds(at, share), :] = done[b * share : (b + 1) * share, :]


def k_apply(share, owner, basis, blocks, moves, weight, out, sorted_moves):
    order = blocks.shape[-1]
    for b in range(moves.shape[0] // share):
        at = pl.multiple_of(owner[b] * share, share)
        sorted_moves[b * share : (b + 1) * share, :] = moves[pl.ds(at, share), :]
    back = dot_nn(basis[0].astype(BF), sorted_moves[...]).astype(BF)
    for b in range(blocks.shape[1]):
        cols = slice(b * order, (b + 1) * order)
        step = dot_nt(back[:, cols], blocks[0, b].astype(BF))
        old = weight[0, :, cols]
        out[0, :, cols] = old - MATRIX_RATE * (step + DECAY_RATE * old)


def adam_moments(grads, first, second, fix_one, fix_two):
    first = BETA_ONE * first + (1.0 - BETA_ONE) * grads
    second = BETA_TWO * second + (1.0 - BETA_TWO) * grads * grads
    moves = first / fix_one / (jnp.sqrt(second / fix_two) + ADAM_EPS)
    return (first, second, moves)


def params(parallel=False):
    return pltpu.CompilerParams(
        dimension_semantics=("arbitrary",), vmem_limit_bytes=VMEM_LIMIT
    )


def sds(*shape, dtype=F32):
    return jax.ShapeDtypeStruct(shape, dtype)


def per_device(
    inputs,
    cotangent,
    lengths,
    hidden_weights,
    mlp_weights,
    norm_gains,
    gate_bias,
    left_bases,
    hidden_blocks,
    mlp_blocks,
    hidden_first,
    hidden_second,
    mlp_first,
    mlp_second,
    gain_first,
    gain_second,
    bias_first,
    bias_second,
    step_count,
    row_owner,
):
    dp_count = lax.axis_size("dp")
    mp = lax.axis_size("mp")
    me = lax.axis_index("mp")
    tokens = inputs.shape[1]
    width = inputs.shape[2]
    part_h = hidden_weights.shape[3]
    part_f = mlp_weights.shape[3]
    hid = part_h * mp
    ff = part_f * mp
    layers = hidden_weights.shape[0]
    steps = tokens // SEG
    ts = min(TILE_STEPS, steps)
    tr = ts * SEG
    grid = steps // ts
    hc = min(HC, part_h)
    share = width // dp_count

    def from_peer(value, j):
        return lax.ppermute(value, "mp", [((m + j) % mp, m) for m in range(mp)])

    def to_next(value):
        return lax.ppermute(value, "mp", [(m, (m + 1) % mp) for m in range(mp)])

    def to_prev(value):
        return lax.ppermute(value, "mp", [((m + 1) % mp, m) for m in range(mp)])

    hid_parts, mlp_parts = [], []
    for l in range(layers):
        own = hidden_weights[l].astype(BF)
        hid_parts.append([own] + [from_peer(own, j) for j in range(1, mp)])
    for l in range(layers):
        own = mlp_weights[l].astype(BF)
        mlp_parts.append([own] + [from_peer(own, j) for j in range(1, mp)])
    bias_all = jnp.concatenate([gate_bias] + [from_peer(gate_bias, j) for j in range(1, mp)], axis=2)
    info = jnp.stack([lengths[0], me, jnp.int32(mp)]).astype(jnp.int32)

    def make_specs(order):
        def tile(cols):
            return pl.BlockSpec((tr, cols), lambda g: (order(g), 0))

        return tile

    def whole(*shape):
        return pl.BlockSpec(shape, lambda g: (0,) * len(shape), pipeline_mode=pl.Buffered(1))

    smem = pl.BlockSpec(memory_space=pltpu.SMEM)
    fwd = make_specs(lambda g: g)
    rev = make_specs(lambda g: grid - 1 - g)
    seg_fwd = pl.BlockSpec((SEG, ts, width), lambda g: (0, g, 0))
    seg_rev = pl.BlockSpec((SEG, ts, width), lambda g: (0, grid - 1 - g, 0))
    before_fwd = pl.BlockSpec((SEG, hid), lambda g: (jnp.maximum(g * ts - 1, 0), 0))
    before_rev = pl.BlockSpec((SEG, hid), lambda g: (jnp.maximum((grid - 1 - g) * ts - 1, 0), 0))
    gates_spec = pl.BlockSpec((3, width, part_h), lambda g: (0, 0, 0), pipeline_mode=pl.Buffered(1))
    wout_spec = pl.BlockSpec((1, width, part_h), lambda g: (3, 0, 0), pipeline_mode=pl.Buffered(1))
    mlp_spec = whole(2, width, part_f)
    gain_spec = whole(2, width)
    bias_spec = whole(2, hid)
    ends_spec = pl.BlockSpec((2, SEG, hid), lambda g: (0, 0, 0))
    fin_spec = pl.BlockSpec((2, hid), lambda g: (0, 0))
    sums_spec = pl.BlockSpec((SEG, width), lambda g: (0, 0))
    bsum_spec = pl.BlockSpec((2, SEG, hid), lambda g: (0, 0, 0))
    kbuf = pltpu.VMEM((3, tr, HC), F32)
    state = pltpu.VMEM((2, SEG, hid), F32)
    start = pltpu.VMEM((SEG, hid), F32)
    row_f32 = pltpu.VMEM((tr, width), F32)
    lanes = pltpu.VMEM((width // 128, tr, 128), F32)

    t_w = sds(tokens, width)
    t_wb = sds(tokens, width, dtype=BF)
    t_h = sds(tokens, hid)
    t_hb = sds(tokens, hid, dtype=BF)
    t_fb = sds(tokens, ff, dtype=BF)
    ends_s = sds(2, SEG, hid)
    fin_s = sds(2, hid)
    sums_s = sds(SEG, width)
    bsum_s = sds(2, SEG, hid)

    def cost(matmul_cols, elems):
        return pl.CostEstimate(
            flops=2 * tokens * width * matmul_cols,
            bytes_accessed=elems,
            transcendentals=0,
        )

    def chain(fin, send, shift, live):
        carry = send(fin)
        for _ in range(mp - 2):
            known = jnp.roll(carry[0:1] * live, shift, axis=1)
            carry = send(jnp.concatenate([fin[0:1] + fin[1:2] * known, fin[1:2]]))
        return carry

    def chain_forward(fin):
        return chain(fin, to_next, -part_h, (me > 0).astype(F32))

    def chain_backward(fin):
        return chain(fin, to_prev, part_h, (me < mp - 1).astype(F32))

    seg_in = inputs.reshape(SEG, steps, width)
    seg_cot = cotangent.reshape(SEG, steps, width)
    saved = []
    f1_out_specs = lambda t: [t(width), t(hid), t(hid), t(hid), t(hid), t(hid), t(hid), t(hid), ends_spec, fin_spec]
    f1_out_shapes = [t_wb, t_h, t_h, t_h, t_hb, t_hb, t_hb, t_hb, ends_s, fin_s]
    outs = pl.pallas_call(
        functools.partial(k_first, mp),
        grid=(grid,),
        in_specs=[seg_fwd, gain_spec, bias_spec] + [gates_spec] * mp,
        out_specs=[fwd(width)] + f1_out_specs(fwd),
        out_shape=[t_w] + f1_out_shapes,
        scratch_shapes=[kbuf, state, lanes],
        compiler_params=params(),
        cost_estimate=cost(3 * hid, 24 * 2**20),
        name="gates_first",
    )(seg_in, norm_gains[0], bias_all[0], *hid_parts[0])
    x, gate = outs[0], outs[1:]
    xs = [x]
    for l in range(layers - 1):
        nin, a, loc, prod, cand, wf, wi, q, ends, fin = gate
        inc = chain_forward(fin)
        outs = pl.pallas_call(
            functools.partial(k_middle, mp),
            grid=(grid,),
            in_specs=[smem, fin_spec, ends_spec, fwd(width), fwd(hid), fwd(hid), before_fwd, before_fwd]
            + [fwd(hid)] * 3
            + [gain_spec, gain_spec, bias_spec]
            + [wout_spec] * mp
            + [mlp_spec] * mp
            + [gates_spec] * mp,
            out_specs=[fwd(hid)] * 3 + [fwd(width)] * 2 + [fwd(ff)] * 2 + [fwd(width)] + f1_out_specs(fwd),
            out_shape=[t_hb] * 3 + [t_w, t_wb, t_fb, t_fb, t_w] + f1_out_shapes,
            scratch_shapes=[kbuf, state, start],
            compiler_params=params(),
            cost_estimate=cost(4 * hid + 2 * ff, 60 * 2**20),
            name="block_forward",
        )(
            info, inc, ends, xs[l], loc, prod, loc, prod, cand, wf, wi,
            norm_gains[l], norm_gains[l + 1], bias_all[l + 1],
            *hid_parts[l], *mlp_parts[l], *hid_parts[l + 1],
        )
        hlow, cf, ci, mid, nmid, act, slope, xn = outs[:8]
        saved.append((nin, a, q, hlow, cf, ci, mid, nmid, act, slope))
        xs.append(xn)
        gate = outs[8:]
    top = layers - 1
    nin, a, loc, prod, cand, wf, wi, q, ends, fin = gate
    inc = chain_forward(fin)
    outs = pl.pallas_call(
        functools.partial(k_turn, mp),
        grid=(grid,),
        in_specs=[smem, fin_spec, ends_spec, rev(width), rev(hid), rev(hid), before_rev, before_rev]
        + [rev(hid)] * 4
        + [gain_spec, seg_rev]
        + [wout_spec] * mp
        + [mlp_spec] * mp,
        out_specs=[rev(hid)] * 3
        + [rev(width), rev(ff), seg_rev, rev(width), rev(ff), rev(width), rev(width), rev(hid), rev(hid)]
        + [ends_spec, fin_spec, sums_spec],
        out_shape=[t_hb] * 3
        + [t_wb, t_fb, sds(SEG, steps, width), t_wb, t_fb, t_wb, t_w, t_h, t_h, ends_s, fin_s, sums_s],
        scratch_shapes=[kbuf, state, start, row_f32, pltpu.VMEM((tr, ff), BF), row_f32, row_f32, lanes],
        compiler_params=params(),
        cost_estimate=cost(2 * hid + 4 * ff, 60 * 2**20),
        name="block_turn",
    )(
        info, inc, ends, xs[top], loc, prod, loc, prod, cand, wf, wi, a, norm_gains[top], seg_cot,
        *hid_parts[top], *mlp_parts[top],
    )
    hlow, cf, ci, nmid, act, output, dz, dpre, dout, dx, lam, rprod, ends, fin, sums_mid = outs
    output = output.reshape(1, tokens, width)
    saved.append((nin, a, q, hlow, cf, ci, None, nmid, act, None))

    def weight_grads(pairs, lefts, rights, part, wide, block):
        count = len(pairs)
        per = wide // block
        in_specs = [pl.BlockSpec((tokens, width), lambda g: (0, 0), pipeline_mode=pl.Buffered(1)) for _ in lefts]
        in_specs += [pl.BlockSpec((tokens, block), lambda g: (0, part * per + g)) for _ in rights]
        return pl.pallas_call(
            functools.partial(k_grads, pairs),
            grid=(per,),
            in_specs=in_specs,
            out_specs=pl.BlockSpec((count, width, block), lambda g: (0, 0, g)),
            out_shape=sds(count, width, wide, dtype=BF),
            compiler_params=params(),
            cost_estimate=cost(count * wide, tokens * wide * count * 2),
            name="weight_grads",
        )(*lefts, *rights)

    def reduce_parts(pairs, lefts, rights, wide):
        block = min(256, wide)
        others = []
        for j in range(1, mp):
            sent = weight_grads(pairs, lefts, rights, j, wide, block)
            others.append(lax.ppermute(sent, "mp", [(m, (m + j) % mp) for m in range(mp)]))
        return weight_grads(pairs, lefts, rights, 0, wide, block), others

    def rotate(own, others, basis, blocks):
        count, _, wide = own.shape
        block = min(512, wide)
        per = wide // block
        nb = block // blocks.shape[-1]
        order = blocks.shape[-1]
        piece = pl.BlockSpec((1, width, block), lambda g: (g // per, 0, g % per))
        return pl.pallas_call(
            functools.partial(k_rotate, mp - 1, share),
            grid=(count * per,),
            in_specs=[
                smem,
                pl.BlockSpec((1, width, width), lambda g: (g // per, 0, 0)),
                pl.BlockSpec((1, nb, order, order), lambda g: (g // per, g % per, 0, 0)),
            ]
            + [piece] * mp,
            out_specs=pl.BlockSpec((width, block), lambda g: (0, g)),
            out_shape=sds(width, count * wide, dtype=BF),
            compiler_params=params(),
            cost_estimate=cost(count * wide // 2, width * wide * count * 8),
            name="rotate",
        )(row_owner, basis, blocks, own, *others)

    def apply_moves(moves, basis, blocks, weight):
        count, _, wide = weight.shape
        block = min(512, wide)
        per = wide // block
        order = blocks.shape[-1]
        nb = block // order
        piece = pl.BlockSpec((1, width, block), lambda g: (g // per, 0, g % per))
        return pl.pallas_call(
            functools.partial(k_apply, share),
            grid=(count * per,),
            in_specs=[
                smem,
                pl.BlockSpec((1, width, width), lambda g: (g // per, 0, 0)),
                pl.BlockSpec((1, nb, order, order), lambda g: (g // per, g % per, 0, 0)),
                pl.BlockSpec((width, block), lambda g: (0, g)),
                piece,
            ],
            out_specs=piece,
            out_shape=sds(count, width, wide),
            scratch_shapes=[pltpu.VMEM((width, block), BF)],
            compiler_params=params(),
            cost_estimate=cost(count * wide // 2, width * wide * count * 10),
            name="apply_moves",
        )(row_owner, basis, blocks, moves, weight)

    count_value = step_count[0].astype(F32)
    fix_one = 1.0 - jnp.power(jnp.float32(BETA_ONE), count_value)
    fix_two = 1.0 - jnp.power(jnp.float32(BETA_TWO), count_value)

    def finish(own, others, basis, blocks, first, second, weight):
        count, _, wide = own.shape
        rotated = rotate(own, others, basis, blocks)
        mine = lax.psum_scatter(rotated, "dp", scatter_dimension=0, tiled=True)
        grad = mine.astype(F32).reshape(share, count, wide)
        first, second, moves = adam_moments(grad, first, second, fix_one, fix_two)
        moves = moves.astype(BF).reshape(share, count * wide)
        moves = lax.all_gather(moves, "dp", axis=0, tiled=True)
        return grad, first, second, apply_moves(moves, basis, blocks, weight)

    def all_sum(value):
        step = 1
        while step < dp_count:
            value = value + lax.ppermute(value, "dp", [(i, i ^ step) for i in range(dp_count)])
            step *= 2
        return value

    hid_done = [None] * layers
    mlp_done = [None] * layers
    small = [None] * layers
    for l in reversed(range(layers)):
        nin, a, q, hlow, cf, ci, mid, nmid, act, slope = saved[l]
        inc = chain_backward(fin)
        mlp_own, mlp_others = reduce_parts(((0, 2), (1, 3)), (nmid, dz), (dpre, act), part_f)
        mlp_done[l] = finish(
            mlp_own, mlp_others, left_bases[l, 4:], mlp_blocks[l], mlp_first[:, l], mlp_second[:, l], mlp_weights[l]
        )
        if l > 0:
            below = saved[l - 1]
            outs = pl.pallas_call(
                functools.partial(k_return, mp),
                grid=(grid,),
                in_specs=[smem, fin_spec, ends_spec]
                + [rev(hid)] * 5
                + [rev(width)] * 3
                + [rev(ff), rev(hid), gain_spec, gain_spec]
                + [gates_spec] * mp
                + [mlp_spec] * mp
                + [wout_spec] * mp,
                out_specs=[rev(hid)] * 3
                + [rev(width), rev(ff), rev(width), rev(width), rev(hid), rev(hid)]
                + [ends_spec, fin_spec, sums_spec, sums_spec, bsum_spec],
                out_shape=[t_hb] * 3
                + [t_wb, t_fb, t_wb, t_w, t_h, t_h, ends_s, fin_s, sums_s, sums_s, bsum_s],
                scratch_shapes=[kbuf, state, start, row_f32],
                compiler_params=params(),
                cost_estimate=cost(4 * hid + 2 * ff, 60 * 2**20),
                name="block_return",
            )(
                info, inc, ends, lam, rprod, cf, ci, q, xs[l], dx, below[6], below[9], below[1],
                norm_gains[l], norm_gains[l - 1],
                *hid_parts[l], *mlp_parts[l - 1], *hid_parts[l - 1],
            )
            dkf, dki, dkc, dz, dpre, dout_next, dx, lam, rprod, ends, fin, sums_in, sums_next, bsum = outs
        else:
            outs = pl.pallas_call(
                functools.partial(k_last, mp),
                grid=(grid,),
                in_specs=[smem, fin_spec, ends_spec]
                + [rev(hid)] * 5
                + [rev(width)] * 2
                + [gain_spec]
                + [gates_spec] * mp,
                out_specs=[rev(hid)] * 3 + [seg_rev, sums_spec, bsum_spec],
                out_shape=[t_hb] * 3 + [sds(SEG, steps, width), sums_s, bsum_s],
                scratch_shapes=[start, row_f32, row_f32, lanes],
                compiler_params=params(),
                cost_estimate=cost(3 * hid, 30 * 2**20),
                name="block_last",
            )(info, inc, ends, lam, rprod, cf, ci, q, xs[l], dx, norm_gains[l], *hid_parts[l])
            dkf, dki, dkc, input_grad, sums_in, bsum = outs
            dout_next, sums_next = None, None
        hid_own, hid_others = reduce_parts(
            ((0, 2), (0, 3), (0, 4), (1, 5)), (nin, dout), (dkf, dki, dkc, hlow), part_h
        )
        hid_done[l] = finish(
            hid_own, hid_others, left_bases[l, :4], hidden_blocks[l], hidden_first[:, l], hidden_second[:, l],
            hidden_weights[l],
        )
        gains = jnp.stack([sums_in.sum(0), sums_mid.sum(0)])
        biases = bsum.sum(1)
        vector = jnp.concatenate([gains.reshape(-1), biases[:, :part_h].reshape(-1)])
        total = vector
        for j in range(1, mp):
            sent = jnp.concatenate([gains.reshape(-1), biases[:, j * part_h : (j + 1) * part_h].reshape(-1)])
            total = total + lax.ppermute(sent, "mp", [(m, (m + j) % mp) for m in range(mp)])
        total = all_sum(total.reshape(-1, 128)).reshape(-1)
        small[l] = (total[: 2 * width].reshape(2, width), total[2 * width :].reshape(2, part_h))
        dout, sums_mid = dout_next, sums_next
    input_grad = input_grad.reshape(1, tokens, width)
    hidden_grad, hidden_first_new, hidden_second_new = (
        jnp.stack([hid_done[l][i] for l in range(layers)], axis=1) for i in range(3)
    )
    mlp_grad, mlp_first_new, mlp_second_new = (
        jnp.stack([mlp_done[l][i] for l in range(layers)], axis=1) for i in range(3)
    )
    hidden_new = jnp.stack([hid_done[l][3] for l in range(layers)])
    mlp_new = jnp.stack([mlp_done[l][3] for l in range(layers)])
    gain_grad = jnp.stack([small[l][0] for l in range(layers)])
    bias_grad = jnp.stack([small[l][1] for l in range(layers)])
    gain_first_new, gain_second_new, gain_moves = adam_moments(
        gain_grad, gain_first, gain_second, fix_one, fix_two
    )
    bias_first_new, bias_second_new, bias_moves = adam_moments(
        bias_grad, bias_first, bias_second, fix_one, fix_two
    )
    gain_new = norm_gains - GAIN_RATE * gain_moves
    bias_new = gate_bias - BIAS_RATE * bias_moves
    return (
        output,
        input_grad,
        hidden_grad,
        hidden_first_new,
        hidden_second_new[:, :, 2:],
        hidden_second_new[:, :, :2],
        hidden_new,
        mlp_grad,
        mlp_first_new,
        mlp_second_new,
        mlp_new,
        gain_grad,
        gain_first_new,
        gain_second_new,
        gain_new,
        bias_grad,
        bias_first_new,
        bias_second_new,
        bias_new,
    )


def solution(mesh):
    in_specs = (
        P("dp", "mp", None),
        P("dp", "mp", None),
        P("dp"),
        P(None, None, None, "mp"),
        P(None, None, None, "mp"),
        P(),
        P(None, None, "mp"),
        P(),
        P(None, None, "mp", None, None),
        P(None, None, "mp", None, None),
        P("dp", None, None, "mp"),
        P("dp", None, None, "mp"),
        P("dp", None, None, "mp"),
        P("dp", None, None, "mp"),
        P(),
        P(),
        P(None, None, "mp"),
        P(None, None, "mp"),
        P(),
        P(),
    )
    out_specs = (
        P("dp", "mp", None),
        P("dp", "mp", None),
        P("dp", None, None, "mp"),
        P("dp", None, None, "mp"),
        P("dp", None, None, "mp"),
        P("dp", None, None, "mp"),
        P(None, None, None, "mp"),
        P("dp", None, None, "mp"),
        P("dp", None, None, "mp"),
        P("dp", None, None, "mp"),
        P(None, None, None, "mp"),
        P(),
        P(),
        P(),
        P(),
        P(None, None, "mp"),
        P(None, None, "mp"),
        P(None, None, "mp"),
        P(None, None, "mp"),
    )
    return jax.shard_map(
        per_device, mesh=mesh, in_specs=in_specs, out_specs=out_specs, check_vma=False
    )
```

time: 2700 us -> 786 us (0.29); the launches traced: 2650 us -> 776 us
  local copies, waits for them, and re-layouts: 1410 us -> 54.2 us
  other arithmetic: 401 us -> 41.7 us
  Pallas kernels: 0 us -> 299 us
  matrix products: 298 us -> 0 us
  waiting for transfers between devices: 483 us -> 352 us
  blocking collectives: 41.1 us -> 0 us
    slice x282 -> x2, local copies, waits for them, and re-layouts: 869 us -> 0.01 us  [per_device(): total[2 * width:].reshape(2, part_h)]
    pallas_call x0 -> x21, Pallas kernels: none -> 299 us  [the longest x1 54.2 us: per_device(): pl.pallas_call(functools.partial(k_middle, mp), grid=(grid,), in_specs=[s...]
    dot_general x36 -> x0, matrix products: 298 us -> none  [the longest x12 87.5 us: forward_proj(): jnp.einsum('std,dx->stx', acts, weight, preferred_element_type=jnp.float32)]
    pad x80 -> x0, local copies, waits for them, and re-layouts: 218 us -> none  [the longest x40 109 us: linear_scan(): lax.associative_scan(affine_combine, (jnp.flip(keep_next, 1), jnp.flip(dr...]
    reduce_scatter x1 -> x4, waiting for transfers between devices: 318 us -> 179 us  [finish(): mine = lax.psum_scatter(rotated, 'dp', scatter_dimension=0, tiled=True)]
    add x91 -> x8, other arithmetic: 106 us -> 4.34 us  [all_sum(): value + lax.ppermute(value, 'dp', [(i, i ^ step) for i in range(dp_count)])]
    mul x41 -> x2, other arithmetic: 103 us -> 3.43 us  [adam_moments(): second = BETA_TWO * second + (1.0 - BETA_TWO) * grads * grads]
    all_gather x4, waiting for transfers between devices: 65.4 us -> 165 us  [finish(): moves = lax.all_gather(moves, 'dp', axis=0, tiled=True)]
  transfers between devices with their start and end apart: 12 -> 31, of which waited for: 8 -> 16; matrix products, arithmetic and copies ran while one was open for 32% -> 10% of each run, Pallas kernels for 0% -> 29%
where the time goes in v1:
time: 786 us; the launch traced here: 776 us
  waiting for transfers between devices  352 us (45%)
  Pallas kernels  299 us (38%)
  local copies, waits for them, and re-layouts  54.2 us (7%)
  other arithmetic  41.7 us (5%)
  between operations  16.6 us (2%)
  starting transfers between devices  12.2 us (2%)
    reduce_scatter x4, waiting for transfers between devices, finish(): mine = lax.psum_scatter(rotated, 'dp', scatter_dimension=0, tiled=True)  179 us
    all_gather x4, waiting for transfers between devices, finish(): moves = lax.all_gather(moves, 'dp', axis=0, tiled=True)  165 us
    pallas_call x1, Pallas kernels, per_device(): pl.pallas_call(functools.partial(k_middle, mp), grid=(grid,), in_specs=[s...  54.2 us
    pallas_call x1, Pallas kernels, per_device(): pl.pallas_call(functools.partial(k_turn, mp), grid=(grid,), in_specs=[sme...  52.7 us
    pallas_call x8, Pallas kernels, weight_grads(): pl.pallas_call(functools.partial(k_grads, pairs), grid=(per,), in_specs=i...  50.6 us
    pallas_call x1, Pallas kernels, per_device(): pl.pallas_call(functools.partial(k_return, mp), grid=(grid,), in_specs=[s...  41.3 us
    pallas_call x4, Pallas kernels, apply_moves(): pl.pallas_call(functools.partial(k_apply, share), grid=(count * per,), in...  30.5 us
    pallas_call x4, Pallas kernels, rotate(): pl.pallas_call(functools.partial(k_rotate, mp - 1, share), grid=(count *...  26.2 us
  transfers between devices with their start and end apart: 31, of which 16 were waited for; matrix products, arithmetic and copies ran while one was open for 10% of the time, Pallas kernels for 29%

profile of v1, /device:TPU:0, one launch (start us, length us, event | category | flops | bytes accessed | tf_op | source)
XLA Modules:
  0.0 776.0 jit_solution(623403685929412881)
XLA Ops:
  20.6 24.6 %gates_first.1 = (f32[1024,512]{1,0:T(8,128)}, bf16[1024,512]{1,0:T(8,128)(2,1)}, f32[1024,1024]{1,0:T(8,128)}, f32[1024,1024]{1,0:T(8,128)}, f32[1024,1024]{1,0...) custom-call(bf16[8,128,512]{2,1,0:T(8,128)(2,1)} %bitcast.168, ...), custom_call_target="tpu_custom_call" | custom-call | flops 3221225472 | bytes 25165824 | tf_op jit(solution)/shard_map/gates_first/pallas_call | solution.py:655
  47.3 54.2 %block_forward.1 = (bf16[1024,1024]{1,0:T(8,128)(2,1)}, bf16[1024,1024]{1,0:T(8,128)(2,1)}, bf16[1024,1024]{1,0:T(8,128)(2,1)}, f32[1024,512]{1,0:T(8,128)}, bf1...) custom-call(s32[3]{0:T(128)} %pad_add_fusion.info, ...), custom_call_target="tpu_custom_call" | custom-call | flops 8589934592 | bytes 62914560 | tf_op jit(solution)/shard_map/block_forward/pallas_call | solution.py:671
  103.5 52.7 %block_turn.1 = (bf16[1024,1024]{1,0:T(8,128)(2,1)}, bf16[1024,1024]{1,0:T(8,128)(2,1)}, bf16[1024,1024]{1,0:T(8,128)(2,1)}, bf16[1024,512]{1,0:T(8,128)(2,1)}, ...) custom-call(s32[3]{0:T(128)} %pad_add_fusion.info, ...), custom_call_target="tpu_custom_call" | custom-call | flops 10737418240 | bytes 62914560 | tf_op jit(solution)/shard_map/block_turn/pallas_call | solution.py:698
  156.2 6.7 weight_grads.15
  169.3 6.5 weight_grads.14.own
  177.1 6.5 rotate.7
  186.0 41.3 %block_return.1 = (bf16[1024,1024]{1,0:T(8,128)(2,1)}, bf16[1024,1024]{1,0:T(8,128)(2,1)}, bf16[1024,1024]{1,0:T(8,128)(2,1)}, bf16[1024,512]{1,0:T(8,128)(2,1)}...) custom-call(s32[3]{0:T(128)} %pad_add_fusion.info, ...), custom_call_target="tpu_custom_call" | custom-call | flops 8589934592 | bytes 62914560 | tf_op jit(solution)/shard_map/block_return/pallas_call | solution.py:828
  227.3 6.5 weight_grads.13
  234.2 6.5 weight_grads.12.own
  242.0 6.5 rotate.6
  248.5 6.2 weight_grads.11
  256.7 7.9 %slice_bitcast_fusion.1 = (f32[4,512,512]{2,1,0:T(8,128)}, f32[4,512,512]{2,1,0:T(8,128)}) fusion(f32[2,6,512,512]{3,2,1,0:T(8,128)} %param.27), kind=kLoop, calls=%fused_computation.3 | loop fusion | bytes 16777216 | tf_op jit(solution)/shard_map/squeeze | solution.py:875
  264.6 6.0 weight_grads.10.own
  271.9 6.7 rotate.5
  281.0 19.2 %block_last.1 = (bf16[1024,1024]{1,0:T(8,128)(2,1)}, bf16[1024,1024]{1,0:T(8,128)(2,1)}, bf16[1024,1024]{1,0:T(8,128)(2,1)}, f32[8,128,512]{2,1,0:T(8,128)}, f32[8,512]{1,0:T(8,128)}, /*index=5*/f32[2,8,1024]{2,1,0:T(8,128)}) custom-call(s32[3]{0:T(128)} %pad_add_fusion.info, f32[2,1024]{1,0:T(2,128)} %copy-done.28, ...), custom_call_target="tpu_custom_call" | custom-call | flops 3221225472 | bytes 31457280 | tf_op jit(solution)/shard_map/block_last/pallas_call | solution.py:854
  300.2 6.1 weight_grads.9
  306.5 6.1 weight_grads.8.own
  313.9 6.6 rotate.4
  322.6 24.4 %reduce-scatter.9.cloned.1.call-done = bf16[32,2048]{1,0:T(8,128)(2,1)} async-done(((bf16[512,2048]{1,0:T(8,128)(2,1)}), bf16[32,2048]{1,0:T(8,128)(2,1)}) %reduce-scatter.9.cloned.1.call-update) | async-done | bytes 131088 | tf_op jit(solution)/shard_map/reduce_scatter | solution.py:802
  351.5 76.0 %reduce-scatter.7.cloned.1.call-done = bf16[32,2048]{1,0:T(8,128)(2,1)} async-done(((bf16[512,2048]{1,0:T(8,128)(2,1)}), bf16[32,2048]{1,0:T(8,128)(2,1)}) %reduce-scatter.7.cloned.1.call-update) | async-done | bytes 131088 | tf_op jit(solution)/shard_map/reduce_scatter | solution.py:802
  428.5 78.6 %reduce-scatter.5.cloned.1.call-done = bf16[32,2048]{1,0:T(8,128)(2,1)} async-done(((bf16[512,2048]{1,0:T(8,128)(2,1)}), bf16[32,2048]{1,0:T(8,128)(2,1)}) %reduce-scatter.5.cloned.1.call-update) | async-done | bytes 131088 | tf_op jit(solution)/shard_map/reduce_scatter | solution.py:802
  530.7 9.0 %slice_bitcast_fusion.4 = (f32[2,512,1024]{2,1,0:T(8,128)}, f32[2,512,1024]{2,1,0:T(8,128)}) fusion(f32[2,2,512,1024]{3,2,1,0:T(8,128)} %param.24), kind=kLoop, calls=%fused_computation.6 | loop fusion | bytes 16777216 | tf_op jit(solution)/shard_map/squeeze | solution.py:584
  559.1 8.7 %all-gather.9.cloned.1.call-done.moves = bf16[512,2048]{1,0:T(8,128)(2,1)} async-done(((bf16[32,2048]{1,0:T(8,128)(2,1)}), bf16[512,2048]{1,0:T(8,128)(2,1)}) %all-gather.9.cloned.1.call-update) | async-done | bytes 2097168 | tf_op jit(solution)/shard_map/all_gather | solution.py:806
  567.9 7.4 apply_moves.6
  575.3 54.6 %all-gather.11.cloned.1.call-done.moves = bf16[512,2048]{1,0:T(8,128)(2,1)} async-done(((bf16[32,2048]{1,0:T(8,128)(2,1)}), bf16[512,2048]{1,0:T(8,128)(2,1)}) %all-gather.11.cloned.1.call-update) | async-done | bytes 2097168 | tf_op jit(solution)/shard_map/all_gather | solution.py:806
  629.9 7.6 apply_moves.7
  637.5 7.3 pad_maximum_fusion.1
  644.8 47.2 %all-gather.5.cloned.1.call-done.moves = bf16[512,2048]{1,0:T(8,128)(2,1)} async-done(((bf16[32,2048]{1,0:T(8,128)(2,1)}), bf16[512,2048]{1,0:T(8,128)(2,1)}) %all-gather.5.cloned.1.call-update) | async-done | bytes 2097168 | tf_op jit(solution)/shard_map/all_gather | solution.py:806
  692.0 7.6 apply_moves.4
  699.7 54.6 %all-gather.7.cloned.1.call-done.moves = bf16[512,2048]{1,0:T(8,128)(2,1)} async-done(((bf16[32,2048]{1,0:T(8,128)(2,1)}), bf16[512,2048]{1,0:T(8,128)(2,1)}) %all-gather.7.cloned.1.call-update) | async-done | bytes 2097168 | tf_op jit(solution)/shard_map/all_gather | solution.py:806
  754.2 7.9 %apply_moves.5 = f32[4,512,512]{2,1,0:T(8,128)} custom-call(s32[16]{0:T(128)} %owner.15, f32[4,512,512]{2,1,0:T(8,128)} %get-tuple-element.156.basis, f32[4,4,128,128]{3,2,1,0:T(8,128)} %get-tuple-element.168.blocks, bf16[512,2048]{1,0:T(8,128)(2,1)} %all-gather.7.cloned.1.call-done.moves, f32[4,512,512]{2,1,0:T(8,128)} %get-tuple-element.160.weight), custom_call_target="tpu_custom_call" | custom-call | flops 1073741824 | bytes 10485760 | tf_op jit(solution)/shard_map/apply_moves/pallas_call | solution.py:777
  762.1 6.6 pad_maximum_fusion
  (218 shorter events, 85.2 us)
Async XLA Ops:
  7.2 314.3 %reduce-scatter.11.cloned.1.call-start = ((), (), s32[]{:S(2)}) async-start(), calls=%async_computation.9 | async-start | bytes 2228224 | tf_op jit(solution)/shard_map/reduce_scatter | solution.py:802
  12.8 7.8 %collective-permute-start.1 = (bf16[4,512,512]{2,1,0:T(8,128)(2,1)S(1)}, bf16[4,512,512]{2,1,0:T(8,128)(2,1)}, u32[]{:S(2)}, u32[]{:S(2)}) collective-permute-start(bf16[4,512,512]{2,1,0:T(8,128)(2,1)S(1)} %get-tuple-element.164.refs_0_.refs_4_), channel_id=1, source_target_pairs={{1,0},{0,1},{3,2},{2,3},{5,4},{4,5},{7,6},{6,7},{9,8},{8,9},{11,10... | collective-permute-start | bytes 6291464 | tf_op jit(solution)/shard_map/ppermute | solution.py:571
  13.3 32.8 %collective-permute-start.4 = (bf16[4,512,512]{2,1,0:T(8,128)(2,1)}, bf16[4,512,512]{2,1,0:T(8,128)(2,1)}, u32[]{:S(2)}, u32[]{:S(2)}) collective-permute-start(bf16[4,512,512]{2,1,0:T(8,128)(2,1)} %get-tuple-element.163.refs_4_.refs_0_), channel_id=1, source_target_pairs={{1,0},{0,1},{3,2},{2,3},{5,4},{4,5},{7,6},{6,7},{9,8},{8,9},{11,10... | collective-permute-start | bytes 6291464 | tf_op jit(solution)/shard_map/ppermute | solution.py:571
  16.5 29.5 %collective-permute-start.3 = (bf16[2,512,1024]{2,1,0:T(8,128)(2,1)}, bf16[2,512,1024]{2,1,0:T(8,128)(2,1)}, u32[]{:S(2)}, u32[]{:S(2)}) collective-permute-start(bf16[2,512,1024]{2,1,0:T(8,128)(2,1)} %get-tuple-element.162.refs_2_), channel_id=1, source_target_pairs={{1,0},{0,1},{3,2},{2,3},{5,4},{4,5},{7,6},{6,7},{9,8},{8,9},{11,10... | collective-permute-start | bytes 6291464 | tf_op jit(solution)/shard_map/ppermute | solution.py:571
  16.9 84.7 %collective-permute-start.6 = (bf16[2,512,1024]{2,1,0:T(8,128)(2,1)}, bf16[2,512,1024]{2,1,0:T(8,128)(2,1)}, u32[]{:S(2)}, u32[]{:S(2)}) collective-permute-start(bf16[2,512,1024]{2,1,0:T(8,128)(2,1)} %get-tuple-element.161.refs_2_), channel_id=1, source_target_pairs={{1,0},{0,1},{3,2},{2,3},{5,4},{4,5},{7,6},{6,7},{9,8},{8,9},{11,10... | collective-permute-start | bytes 6291464 | tf_op jit(solution)/shard_map/ppermute | solution.py:571
  17.0 3.0 collective-permute-start
  45.2 1.4 collective-permute-start.2
  101.4 1.4 collective-permute-start.5
  162.9 12.9 %collective-permute-start.12 = (bf16[2,512,1024]{2,1,0:T(8,128)(2,1)}, bf16[2,512,1024]{2,1,0:T(8,128)(2,1)S(1)}, u32[]{:S(2)}, u32[]{:S(2)}) collective-permute-start(bf16[2,512,1024]{2,1,0:T(8,128)(2,1)} %weight_grads.15), channel_id=1, source_target_pairs={{0,1},{1,0},{2,3},{3,2},{4,5},{5,4},{6,7},{7,6},{8,9},{9,8},{10,11... | collective-permute-start | bytes 6291464 | tf_op jit(solution)/shard_map/ppermute | solution.py:744
  183.6 163.5 %reduce-scatter.9.cloned.1.call-start = ((), (), s32[]{:S(2)}) async-start(), calls=%async_computation.8 | async-start | bytes 2228224 | tf_op jit(solution)/shard_map/reduce_scatter | solution.py:802
  184.3 1.2 collective-permute-start.7
  233.9 6.8 collective-permute-start.11
  248.5 178.9 %reduce-scatter.7.cloned.1.call-start = ((), (), s32[]{:S(2)}) async-start(), calls=%async_computation.5 | async-start | bytes 2228224 | tf_op jit(solution)/shard_map/reduce_scatter | solution.py:802
  254.7 15.9 %collective-permute-start.10 = (bf16[4,512,512]{2,1,0:T(8,128)(2,1)}, bf16[4,512,512]{2,1,0:T(8,128)(2,1)S(1)}, u32[]{:S(2)}, u32[]{:S(2)}) collective-permute-start(bf16[4,512,512]{2,1,0:T(8,128)(2,1)} %weight_grads.11), channel_id=1, source_target_pairs={{0,1},{1,0},{2,3},{3,2},{4,5},{5,4},{6,7},{7,6},{8,9},{9,8},{10,11... | collective-permute-start | bytes 6291464 | tf_op jit(solution)/shard_map/ppermute | solution.py:744
  278.6 228.5 %reduce-scatter.5.cloned.1.call-start = ((), (), s32[]{:S(2)}) async-start(), calls=%async_computation.4 | async-start | bytes 2228224 | tf_op jit(solution)/shard_map/reduce_scatter | solution.py:802
  279.3 1.2 collective-permute-start.8
  306.3 6.3 collective-permute-start.9
  320.5 27.7 %copy-start.12 = (f32[32,2,2,1024]{3,2,1,0:T(2,128)S(1)}, f32[32,2,2,1024]{3,2,1,0:T(2,128)}, u32[]{:S(2)}) copy-start(f32[32,2,2,1024]{3,2,1,0:T(2,128)} %param.32) | copy-start | bytes 1572868
  320.6 247.3 %all-gather.9.cloned.1.call-start = ((), (), s32[]{:S(2)}) async-start(), calls=%async_computation.10 | async-start | bytes 2228224 | tf_op jit(solution)/shard_map/all_gather | solution.py:806
  350.3 279.6 %all-gather.11.cloned.1.call-start = ((), (), s32[]{:S(2)}) async-start(), calls=%async_computation.11 | async-start | bytes 2228224 | tf_op jit(solution)/shard_map/all_gather | solution.py:806
  351.4 340.6 %all-gather.5.cloned.1.call-start = ((), (), s32[]{:S(2)}) async-start(), calls=%async_computation.6 | async-start | bytes 2228224 | tf_op jit(solution)/shard_map/all_gather | solution.py:806
  511.7 242.5 %all-gather.7.cloned.1.call-start = ((), (), s32[]{:S(2)}) async-start(), calls=%async_computation.7 | async-start | bytes 2228224 | tf_op jit(solution)/shard_map/all_gather | solution.py:806
  515.6 1.4 collective-permute-start.18
  517.6 4.7 collective-permute-start.19
  521.8 1.3 collective-permute-start.13
  523.0 3.7 collective-permute-start.20
  523.7 5.3 collective-permute-start.14
  528.0 11.8 %collective-permute-start.21 = (f32[16,128]{1,0:T(8,128)}, f32[16,128]{1,0:T(8,128)}, u32[]{:S(2)}, u32[]{:S(2)}) collective-permute-start(f32[16,128]{1,0:T(8,128)} %fusion.49), channel_id=1, source_target_pairs={{0,8},{2,10},{4,12},{6,14},{8,0},{10,2},{12,4},{14,6},{16,24},{18,... | collective-permute-start | bytes 24584 | tf_op jit(solution)/shard_map/ppermute | solution.py:812
  529.9 12.4 %collective-permute-start.15 = (f32[16,128]{1,0:T(8,128)S(1)}, f32[16,128]{1,0:T(8,128)S(1)}, u32[]{:S(2)}, u32[]{:S(2)}) collective-permute-start(f32[16,128]{1,0:T(8,128)S(1)} %fusion.48), channel_id=1, source_target_pairs={{0,4},{2,6},{4,0},{6,2},{8,12},{10,14},{12,8},{14,10},{16,20},{18,... | collective-permute-start | bytes 24584 | tf_op jit(solution)/shard_map/ppermute | solution.py:812
  540.5 10.2 %collective-permute-start.22 = (f32[16,128]{1,0:T(8,128)S(1)}, f32[16,128]{1,0:T(8,128)S(1)}, u32[]{:S(2)}, u32[]{:S(2)}) collective-permute-start(f32[16,128]{1,0:T(8,128)S(1)} %add.156), channel_id=1, source_target_pairs={{0,16},{2,18},{4,20},{6,22},{8,24},{10,26},{12,28},{14,30},{16,0},... | collective-permute-start | bytes 24584 | tf_op jit(solution)/shard_map/ppermute | solution.py:812
  543.1 4.6 collective-permute-start.16
  547.7 4.6 collective-permute-start.17
  (39 other events, 239.0 us)
Sparse Core Ops, SparseCore 0:
  183.7 83.3 reduce-scatter.10
  269.4 77.6 reduce-scatter.8
  349.4 78.0 reduce-scatter.6
  429.5 77.5 reduce-scatter.4
  509.8 58.0 all-gather.8
  570.5 59.3 all-gather.10
  632.7 59.3 all-gather.4
  694.8 59.3 all-gather.6

commit v2 on v1

--- a/solution.py
+++ b/solution.py
@@ -477,38 +477,220 @@
         out[k] = dot_tn(refs[left][...], refs[right][...]).astype(BF)
 
 
-def k_rotate(n_recv, share, owner, basis, blocks, own, *refs):
-    recv = refs[:n_recv]
-    out = refs[n_recv]
+def digits_place(relative, stages):
+    place = None
+    for low, count in stages:
+        digit = (relative >> low) & ((1 << count) - 1)
+        place = digit if place is None else (place << count) + digit
+    return place
+
+
+def turn_blocks(value, blocks, inverse):
     order = blocks.shape[-1]
-    total = own[0].astype(F32)
-    for ref in recv:
-        total = total + ref[0].astype(F32)
-    low = total.astype(BF)
-    turned = jnp.concatenate(
+    dot = dot_nt if inverse else dot_nn
+    return jnp.concatenate(
         [
-            dot_nn(low[:, b * order : (b + 1) * order], blocks[0, b].astype(BF))
-            for b in range(blocks.shape[1])
+            dot(value[:, b * order : (b + 1) * order], blocks[0, 0, b].astype(BF))
+            for b in range(blocks.shape[2])
         ],
         axis=1,
-    ).astype(BF)
-    done = dot_tn(basis[0].astype(BF), turned).astype(BF)
-    for b in range(done.shape[0] // share):
-        at = pl.multiple_of(owner[b] * share, share)
-        out[pl.ds(at, share), :] = done[b * share : (b + 1) * share, :]
-
-
-def k_apply(share, owner, basis, blocks, moves, weight, out, sorted_moves):
-    order = blocks.shape[-1]
-    for b in range(moves.shape[0] // share):
-        at = pl.multiple_of(owner[b] * share, share)
-        sorted_moves[b * share : (b + 1) * share, :] = moves[pl.ds(at, share), :]
-    back = dot_nn(basis[0].astype(BF), sorted_moves[...]).astype(BF)
-    for b in range(blocks.shape[1]):
-        cols = slice(b * order, (b + 1) * order)
-        step = dot_nt(back[:, cols], blocks[0, b].astype(BF))
-        old = weight[0, :, cols]
-        out[0, :, cols] = old - MATRIX_RATE * (step + DECAY_RATE * old)
+    )
+
+
+def k_rotate(plan, per_source, who, basis, *refs):
+    n_src = len(plan.sources)
+    blocks = refs[:n_src]
+    grads = refs[n_src : n_src * (1 + per_source)]
+    n_out = sum(plan.firsts)
+    outs = refs[n_src * (1 + per_source) :][:n_out]
+    bufs = refs[n_src * (1 + per_source) + n_out : -1]
+    done = refs[-1]
+    g = pl.program_id(0)
+    share = plan.share
+    for at in range(n_src):
+
+        @pl.when((g >= plan.begins[at]) & (g < plan.begins[at + 1]))
+        def _(at=at):
+            mine = grads[at * per_source : (at + 1) * per_source]
+            total = mine[0][0].astype(F32)
+            for ref in mine[1:]:
+                total = total + ref[0].astype(F32)
+            turned = turn_blocks(total.astype(BF), blocks[at], False).astype(BF)
+            done[:, : plan.blocks[at]] = dot_tn(basis[0, 0].astype(BF), turned).astype(BF)
+
+    count = done.shape[0] // share
+    relative = [who[b] ^ who[count] for b in range(count)]
+    for chunk, runs in enumerate(plan.runs):
+
+        @pl.when(g == chunk)
+        def _(runs=runs):
+            for stream, src, dst, wide in runs:
+                for b in range(count):
+                    at = digits_place(relative[b], plan.stages[stream]) * share
+                    bufs[stream][pl.ds(pl.multiple_of(at, share), share), dst : dst + wide] = done[
+                        b * share : (b + 1) * share, src : src + wide
+                    ]
+
+    @pl.when(g == pl.num_programs(0) - 1)
+    def _():
+        at = 0
+        for stream, pieces in enumerate(plan.firsts):
+            rows = done.shape[0] // pieces
+            for r in range(pieces):
+                outs[at][...] = bufs[stream][r * rows : (r + 1) * rows, :]
+                at += 1
+
+
+def sum_pieces(refs):
+    total = refs[0][...].astype(F32)
+    for ref in refs[1:]:
+        total = total + ref[...].astype(F32)
+    return total
+
+
+def k_combine(n_in, n_out, *refs):
+    i, o = 0, sum(n_in)
+    for take, give in zip(n_in, n_out):
+        total = sum_pieces(refs[i : i + take]).astype(BF)
+        rows = total.shape[0] // give
+        for r in range(give):
+            refs[o + r][...] = total[r * rows : (r + 1) * rows, :]
+        i += take
+        o += give
+
+
+def k_adam(plan, splits, n_alias, fix, *refs):
+    n_in = sum(plan.lasts)
+    n_src = len(plan.sources)
+    pieces = refs[:n_in]
+    olds = refs[n_in : n_in + 2 * n_src]
+    outs = refs[n_in + 2 * n_src + n_alias :]
+    bufs = refs[len(refs) - n_src :]
+    moves_o = outs[sum(2 + len(split) for split in splits) :][: len(plan.stages)]
+    sums, i = [], 0
+    for take in plan.lasts:
+        sums.append(sum_pieces(pieces[i : i + take]))
+        i += take
+    o = 0
+    for at, split in enumerate(splits):
+        grad_o, first_o = outs[o : o + 2]
+        second_o = outs[o + 2 : o + 2 + len(split)]
+        o += 2 + len(split)
+        first, second = olds[2 * at : 2 * at + 2]
+        for chunk in range(plan.begins[at], plan.begins[at + 1]):
+            kind, base = plan.where(at, chunk)
+            for stream, src, dst, wide in plan.runs[chunk]:
+                grad_o[:, 0, kind, base + src : base + src + wide] = sums[stream][:, dst : dst + wide]
+        grad = grad_o[...]
+        one = BETA_ONE * first[...] + (1.0 - BETA_ONE) * grad
+        two = BETA_TWO * second[...] + (1.0 - BETA_TWO) * grad * grad
+        first_o[...] = one
+        for ref, (lo, hi) in zip(second_o, split):
+            ref[...] = two[:, :, lo:hi, :]
+        bufs[at][...] = one * fix[0] / (jnp.sqrt(two * fix[1]) + ADAM_EPS)
+        for chunk in range(plan.begins[at], plan.begins[at + 1]):
+            kind, base = plan.where(at, chunk)
+            for stream, src, dst, wide in plan.runs[chunk]:
+                moves_o[stream][:, dst : dst + wide] = bufs[at][
+                    :, 0, kind, base + src : base + src + wide
+                ].astype(BF)
+
+
+def k_apply(plan, n_alias, who, basis, *refs):
+    n_src = len(plan.sources)
+    n_in = sum(plan.firsts)
+    blocks = refs[:n_src]
+    weights = refs[n_src : 2 * n_src]
+    pieces = refs[2 * n_src : 2 * n_src + n_in]
+    outs = refs[2 * n_src + n_in + n_alias :][:n_src]
+    bufs = refs[2 * n_src + n_in + n_alias + n_src : -1]
+    moves = refs[-1]
+    g = pl.program_id(0)
+    share = plan.share
+    width = basis.shape[2]
+    count = width // share
+
+    @pl.when(g == 0)
+    def _():
+        at = 0
+        for stream, n in enumerate(plan.firsts):
+            rows = width // n
+            for r in range(n):
+                bufs[stream][r * rows : (r + 1) * rows, :] = pieces[at][...]
+                at += 1
+
+    relative = [who[b] ^ who[count] for b in range(count)]
+    for chunk, runs in enumerate(plan.runs):
+
+        @pl.when(g == chunk)
+        def _(runs=runs):
+            for stream, src, dst, wide in runs:
+                for b in range(count):
+                    at = digits_place(relative[b], plan.stages[stream]) * share
+                    moves[b * share : (b + 1) * share, src : src + wide] = bufs[stream][
+                        pl.ds(pl.multiple_of(at, share), share), dst : dst + wide
+                    ]
+
+    for at in range(n_src):
+
+        @pl.when((g >= plan.begins[at]) & (g < plan.begins[at + 1]))
+        def _(at=at):
+            wide = plan.blocks[at]
+            back = dot_nn(basis[0, 0].astype(BF), moves[:, :wide]).astype(BF)
+            step = turn_blocks(back, blocks[at], True)
+            old = weights[at][0, 0]
+            outs[at][0, 0] = old - MATRIX_RATE * (step + DECAY_RATE * old)
+
+
+class Plan:
+    def __init__(self, dp_count, width, sources):
+        bits = dp_count.bit_length() - 1
+        plane, rest = (0, 2), (2, bits - 2)
+        orders = [[plane, rest], [rest, plane]]
+        self.share = width // dp_count
+        self.sources = sources
+        self.blocks = [min(512, wide) for _, _, wide in sources]
+        self.pers = [wide // block for (_, _, wide), block in zip(sources, self.blocks)]
+        self.begins = [0]
+        for (_, count, _), per in zip(sources, self.pers):
+            self.begins.append(self.begins[-1] + count * per)
+        chunks = self.begins[-1]
+        named = []
+        for at, block in enumerate(self.blocks):
+            for chunk in range(self.begins[at], self.begins[at + 1]):
+                lanes = block // 128
+                cut = lanes - (1 if chunk % 3 else 2)
+                named.append([0 if lane < max(cut, 1) else 1 for lane in range(lanes)])
+        used = sorted({stream for row in named for stream in row})
+        self.stages = [orders[stream] for stream in used]
+        self.cols = [0] * len(used)
+        self.runs = []
+        for row in named:
+            runs = []
+            for lane, stream in enumerate(row):
+                at = used.index(stream)
+                if runs and runs[-1][0] == at:
+                    runs[-1][3] += 128
+                else:
+                    runs.append([at, lane * 128, self.cols[at], 128])
+                self.cols[at] += 128
+            self.runs.append(runs)
+        self.firsts = [1 << stages[0][1] for stages in self.stages]
+        self.lasts = [1 << stages[-1][1] for stages in self.stages]
+
+    def where(self, at, chunk):
+        local = chunk - self.begins[at]
+        return local // self.pers[at], local % self.pers[at] * self.blocks[at]
+
+    def local(self, at, g):
+        return jnp.clip(g - self.begins[at], 0, self.begins[at + 1] - self.begins[at] - 1)
+
+    def basis_at(self, g):
+        index = None
+        for at, (base, _, _) in enumerate(self.sources):
+            here = base + self.local(at, g) // self.pers[at]
+            index = here if index is None else jnp.where(g < self.begins[at], index, here)
+        return index
 
 
 def adam_moments(grads, first, second, fix_one, fix_two):
@@ -744,67 +926,168 @@
             others.append(lax.ppermute(sent, "mp", [(m, (m + j) % mp) for m in range(mp)]))
         return weight_grads(pairs, lefts, rights, 0, wide, block), others
 
-    def rotate(own, others, basis, blocks):
-        count, _, wide = own.shape
-        block = min(512, wide)
-        per = wide // block
-        nb = block // blocks.shape[-1]
-        order = blocks.shape[-1]
-        piece = pl.BlockSpec((1, width, block), lambda g: (g // per, 0, g % per))
-        return pl.pallas_call(
-            functools.partial(k_rotate, mp - 1, share),
-            grid=(count * per,),
-            in_specs=[
-                smem,
-                pl.BlockSpec((1, width, width), lambda g: (g // per, 0, 0)),
-                pl.BlockSpec((1, nb, order, order), lambda g: (g // per, g % per, 0, 0)),
-            ]
-            + [piece] * mp,
-            out_specs=pl.BlockSpec((width, block), lambda g: (0, g)),
-            out_shape=sds(width, count * wide, dtype=BF),
-            compiler_params=params(),
-            cost_estimate=cost(count * wide // 2, width * wide * count * 8),
-            name="rotate",
-        )(row_owner, basis, blocks, own, *others)
-
-    def apply_moves(moves, basis, blocks, weight):
-        count, _, wide = weight.shape
-        block = min(512, wide)
-        per = wide // block
-        order = blocks.shape[-1]
-        nb = block // order
-        piece = pl.BlockSpec((1, width, block), lambda g: (g // per, 0, g % per))
-        return pl.pallas_call(
-            functools.partial(k_apply, share),
-            grid=(count * per,),
-            in_specs=[
-                smem,
-                pl.BlockSpec((1, width, width), lambda g: (g // per, 0, 0)),
-                pl.BlockSpec((1, nb, order, order), lambda g: (g // per, g % per, 0, 0)),
-                pl.BlockSpec((width, block), lambda g: (0, g)),
-                piece,
-            ],
-            out_specs=piece,
-            out_shape=sds(count, width, wide),
-            scratch_shapes=[pltpu.VMEM((width, block), BF)],
-            compiler_params=params(),
-            cost_estimate=cost(count * wide // 2, width * wide * count * 10),
-            name="apply_moves",
-        )(row_owner, basis, blocks, moves, weight)
-
+    dp_me = lax.axis_index("dp")
+    who = jnp.concatenate([row_owner, dp_me[None].astype(jnp.int32)])
     count_value = step_count[0].astype(F32)
     fix_one = 1.0 - jnp.power(jnp.float32(BETA_ONE), count_value)
     fix_two = 1.0 - jnp.power(jnp.float32(BETA_TWO), count_value)
-
-    def finish(own, others, basis, blocks, first, second, weight):
-        count, _, wide = own.shape
-        rotated = rotate(own, others, basis, blocks)
-        mine = lax.psum_scatter(rotated, "dp", scatter_dimension=0, tiled=True)
-        grad = mine.astype(F32).reshape(share, count, wide)
-        first, second, moves = adam_moments(grad, first, second, fix_one, fix_two)
-        moves = moves.astype(BF).reshape(share, count * wide)
-        moves = lax.all_gather(moves, "dp", axis=0, tiled=True)
-        return grad, first, second, apply_moves(moves, basis, blocks, weight)
+    fix = jnp.stack([1.0 / fix_one, 1.0 / fix_two])
+    vmem = pl.BlockSpec(memory_space=pltpu.VMEM)
+    hbm = pl.BlockSpec(memory_space=pl.ANY)
+
+    def exchange(value, stage):
+        low, count = stage
+        return [
+            lax.ppermute(value, "dp", [(i, i ^ (r << low)) for i in range(dp_count)])
+            for r in range(1, 1 << count)
+        ]
+
+    def source_spec(plan, at, shape, tail):
+        return pl.BlockSpec(shape, lambda g: tail(plan.local(at, g) // plan.pers[at], plan.local(at, g) % plan.pers[at]))
+
+    def rotate(plan, l, grads, blocks):
+        basis_spec = pl.BlockSpec((1, 1, width, width), lambda g: (l, plan.basis_at(g), 0, 0))
+        specs, flat = [], []
+        for at, one in enumerate(blocks):
+            order = one.shape[-1]
+            nb = plan.blocks[at] // order
+            specs.append(source_spec(plan, at, (1, 1, nb, order, order), lambda k, c: (l, k, c, 0, 0)))
+        for at, ones in enumerate(grads):
+            for one in ones:
+                specs.append(source_spec(plan, at, (1, width, plan.blocks[at]), lambda k, c: (k, 0, c)))
+                flat.append(one)
+        out_shapes = [
+            sds(width // n, cols, dtype=BF) for n, cols in zip(plan.firsts, plan.cols) for _ in range(n)
+        ]
+        outs = pl.pallas_call(
+            functools.partial(k_rotate, plan, mp),
+            grid=(plan.begins[-1],),
+            in_specs=[smem, basis_spec] + specs,
+            out_specs=[pl.BlockSpec(o.shape, lambda g: (0, 0)) for o in out_shapes],
+            out_shape=out_shapes,
+            scratch_shapes=[pltpu.VMEM((width, cols), BF) for cols in plan.cols]
+            + [pltpu.VMEM((width, max(plan.blocks)), BF)],
+            compiler_params=params(),
+            cost_estimate=cost(2 * sum(plan.cols), 16 * 2**20),
+            name="rotate",
+        )(who, left_bases, *blocks, *flat)
+        pieces, at = [], 0
+        for n in plan.firsts:
+            pieces.append(outs[at : at + n])
+            at += n
+        return pieces
+
+    def scatter_stage(plan, pieces, at):
+        held = []
+        for stages, mine in zip(plan.stages, pieces):
+            low, count = stages[at]
+            got = [
+                lax.ppermute(mine[r], "dp", [(i, i ^ (r << low)) for i in range(dp_count)])
+                for r in range(1, 1 << count)
+            ]
+            held.append([mine[0]] + got)
+        return held
+
+    def combine(plan, held, at):
+        flat = [v for one in held for v in one]
+        n_in = [len(one) for one in held]
+        n_out = [1 << stages[at + 1][1] for stages in plan.stages]
+        shapes = [
+            sds(one[0].shape[0] // n, one[0].shape[1], dtype=BF) for one, n in zip(held, n_out) for _ in range(n)
+        ]
+        outs = pl.pallas_call(
+            functools.partial(k_combine, n_in, n_out),
+            in_specs=[vmem] * len(flat),
+            out_specs=[vmem] * len(shapes),
+            out_shape=shapes,
+            compiler_params=pltpu.CompilerParams(vmem_limit_bytes=VMEM_LIMIT),
+            cost_estimate=pl.CostEstimate(flops=0, bytes_accessed=6 * 2**20, transcendentals=0),
+            name="combine",
+        )(*flat)
+        pieces, i = [], 0
+        for n in n_out:
+            pieces.append(outs[i : i + n])
+            i += n
+        return pieces
+
+    def adam(plan, l, held, olds, splits, before):
+        flat = [v for one in held for v in one]
+        out_specs, shapes, in_specs, bufs = [], [], [], []
+        for (_, count, wide), split in zip(plan.sources, splits):
+            for lo, hi in ((0, count),) * 2 + split:
+                out_specs.append(pl.BlockSpec((share, 1, hi - lo, wide), lambda g: (0, l, 0, 0)))
+                shapes.append(sds(share, layers, hi - lo, wide))
+            in_specs += [pl.BlockSpec((share, 1, count, wide), lambda g: (0, l, 0, 0))] * 2
+            bufs.append(pltpu.VMEM((share, 1, count, wide), F32))
+        n_state = len(shapes)
+        before = before or ()
+        outs = pl.pallas_call(
+            functools.partial(k_adam, plan, splits, len(before)),
+            grid=(1,),
+            in_specs=[smem] + [vmem] * len(flat) + in_specs + [hbm] * len(before),
+            out_specs=out_specs + [vmem] * len(plan.cols),
+            out_shape=shapes + [sds(share, cols, dtype=BF) for cols in plan.cols],
+            scratch_shapes=bufs,
+            input_output_aliases={1 + len(flat) + len(olds) + i: i for i in range(len(before))},
+            compiler_params=pltpu.CompilerParams(vmem_limit_bytes=VMEM_LIMIT),
+            cost_estimate=pl.CostEstimate(flops=0, bytes_accessed=8 * 2**20, transcendentals=0),
+            name="adam",
+        )(fix, *flat, *olds, *before)
+        return tuple(outs[:n_state]), outs[n_state:]
+
+    def gather_moves(plan, moves):
+        flat = []
+        for stages, value in zip(plan.stages, moves):
+            for stage in reversed(stages[1:]):
+                value = jnp.concatenate([value] + exchange(value, stage), axis=0)
+            flat += [value] + exchange(value, stages[0])
+        return flat
+
+    def apply_moves(plan, l, flat, blocks, weights, before):
+        basis_spec = pl.BlockSpec((1, 1, width, width), lambda g: (l, plan.basis_at(g), 0, 0))
+        block_specs, specs = [], []
+        for at, one in enumerate(blocks):
+            order = one.shape[-1]
+            nb = plan.blocks[at] // order
+            block_specs.append(source_spec(plan, at, (1, 1, nb, order, order), lambda k, c: (l, k, c, 0, 0)))
+            specs.append(source_spec(plan, at, (1, 1, width, plan.blocks[at]), lambda k, c: (l, k, 0, c)))
+        before = before or ()
+        ins = 2 + 2 * len(blocks) + len(flat)
+        return tuple(
+            pl.pallas_call(
+                functools.partial(k_apply, plan, len(before)),
+                grid=(plan.begins[-1],),
+                in_specs=[smem, basis_spec]
+                + block_specs
+                + specs
+                + [whole(*v.shape) for v in flat]
+                + [hbm] * len(before),
+                out_specs=specs,
+                out_shape=[sds(*w.shape) for w in weights],
+                scratch_shapes=[pltpu.VMEM((width, cols), BF) for cols in plan.cols]
+                + [pltpu.VMEM((width, max(plan.blocks)), BF)],
+                input_output_aliases={ins + i: i for i in range(len(before))},
+                compiler_params=params(),
+                cost_estimate=cost(2 * sum(plan.cols), 24 * 2**20),
+                name="apply_moves",
+            )(who, left_bases, *blocks, *weights, *flat, *before)
+        )
+
+    plan = Plan(dp_count, width, ((4, 2, part_f), (0, 4, part_h)))
+    olds = (mlp_first, mlp_second, hidden_first, hidden_second)
+    splits = (((0, 2),), ((0, 2), (2, 4)))
+
+    def finish(l, grads, before):
+        state, new = before or (None, None)
+        blocks = (mlp_blocks, hidden_blocks)
+        pieces = rotate(plan, l, grads, blocks)
+        stages = len(plan.stages[0])
+        for at in range(stages - 1):
+            pieces = combine(plan, scatter_stage(plan, pieces, at), at)
+        held = scatter_stage(plan, pieces, stages - 1)
+        state, moves = adam(plan, l, held, olds, splits, state)
+        flat = gather_moves(plan, moves)
+        return state, apply_moves(plan, l, flat, blocks, (mlp_weights, hidden_weights), new)
 
     def all_sum(value):
         step = 1
@@ -813,16 +1096,12 @@
             step *= 2
         return value
 
-    hid_done = [None] * layers
-    mlp_done = [None] * layers
+    done = None
     small = [None] * layers
     for l in reversed(range(layers)):
         nin, a, q, hlow, cf, ci, mid, nmid, act, slope = saved[l]
         inc = chain_backward(fin)
         mlp_own, mlp_others = reduce_parts(((0, 2), (1, 3)), (nmid, dz), (dpre, act), part_f)
-        mlp_done[l] = finish(
-            mlp_own, mlp_others, left_bases[l, 4:], mlp_blocks[l], mlp_first[:, l], mlp_second[:, l], mlp_weights[l]
-        )
         if l > 0:
             below = saved[l - 1]
             outs = pl.pallas_call(
@@ -871,10 +1150,7 @@
         hid_own, hid_others = reduce_parts(
             ((0, 2), (0, 3), (0, 4), (1, 5)), (nin, dout), (dkf, dki, dkc, hlow), part_h
         )
-        hid_done[l] = finish(
-            hid_own, hid_others, left_bases[l, :4], hidden_blocks[l], hidden_first[:, l], hidden_second[:, l],
-            hidden_weights[l],
-        )
+        done = finish(l, ([mlp_own] + mlp_others, [hid_own] + hid_others), done)
         gains = jnp.stack([sums_in.sum(0), sums_mid.sum(0)])
         biases = bsum.sum(1)
         vector = jnp.concatenate([gains.reshape(-1), biases[:, :part_h].reshape(-1)])
@@ -886,14 +1162,9 @@
         small[l] = (total[: 2 * width].reshape(2, width), total[2 * width :].reshape(2, part_h))
         dout, sums_mid = dout_next, sums_next
     input_grad = input_grad.reshape(1, tokens, width)
-    hidden_grad, hidden_first_new, hidden_second_new = (
-        jnp.stack([hid_done[l][i] for l in range(layers)], axis=1) for i in range(3)
-    )
-    mlp_grad, mlp_first_new, mlp_second_new = (
-        jnp.stack([mlp_done[l][i] for l in range(layers)], axis=1) for i in range(3)
-    )
-    hidden_new = jnp.stack([hid_done[l][3] for l in range(layers)])
-    mlp_new = jnp.stack([mlp_done[l][3] for l in range(layers)])
+    state, (mlp_new, hidden_new) = done
+    mlp_grad, mlp_first_new, mlp_second_new = state[:3]
+    hidden_grad, hidden_first_new, gate_second_new, hidden_second_new = state[3:]
     gain_grad = jnp.stack([small[l][0] for l in range(layers)])
     bias_grad = jnp.stack([small[l][1] for l in range(layers)])
     gain_first_new, gain_second_new, gain_moves = adam_moments(
@@ -909,8 +1180,8 @@
         input_grad,
         hidden_grad,
         hidden_first_new,
-        hidden_second_new[:, :, 2:],
-        hidden_second_new[:, :, :2],
+        hidden_second_new,
+        gate_second_new,
         hidden_new,
         mlp_grad,
         mlp_first_new,

time: 786 us -> 551 us (0.70)
  waiting for transfers between devices: 352 us -> 96.7 us
  starting transfers between devices: 12.2 us -> 103 us
  local copies, waits for them, and re-layouts: 54.2 us -> 17.9 us
  other arithmetic: 41.7 us -> 8.83 us
  Pallas kernels: 299 us -> 315 us
  between operations: 16.6 us -> 3.08 us
    reduce_scatter x4 -> x0, waiting for transfers between devices: 179 us -> none  [finish(): mine = lax.psum_scatter(rotated, 'dp', scatter_dimension=0, tiled=True)]
    all_gather x4 -> x0, waiting for transfers between devices: 165 us -> none  [finish(): moves = lax.all_gather(moves, 'dp', axis=0, tiled=True)]
    ppermute x0 -> x48, starting transfers between devices: none -> 86.1 us  [the longest x24 51.4 us: exchange(): lax.ppermute(value, 'dp', [(i, i ^ r << low) for i in range(dp_count)])]
    ppermute x0 -> x48, waiting for transfers between devices: none -> 84.1 us  [the longest x24 54.2 us: exchange(): lax.ppermute(value, 'dp', [(i, i ^ r << low) for i in range(dp_count)])]
    squeeze x6 -> x0, local copies, waits for them, and re-layouts: 29.2 us -> none  [the longest x1 9.04 us: per_device(): own = mlp_weights[l].astype(BF)]
    pallas_call x8, Pallas kernels: 56.7 us -> 73 us  [the longest x2 31.7 us: apply_moves(): pl.pallas_call(functools.partial(k_apply, plan, len(before)), grid=(plan....]
    another operation x8 -> x3, other arithmetic: 19.9 us -> 5.2 us  [the longest x1 7.3 us: per_device(): mlp_new = jnp.stack([mlp_done[l][3] for l in range(layers)])]
  transfers between devices with their start and end apart: 31 -> 71, of which waited for: 16 -> 21; matrix products, arithmetic and copies ran while one was open for 10% -> 2% of each run, Pallas kernels for 29% -> 45%
where the time goes in v2:
time: 551 us; the launch traced here: 545 us
  Pallas kernels  315 us (57%)
  starting transfers between devices  103 us (19%)
  waiting for transfers between devices  96.7 us (18%)
  local copies, waits for them, and re-layouts  17.9 us (3%)
  other arithmetic  8.83 us (2%)
    ppermute x24, waiting for transfers between devices, exchange(): lax.ppermute(value, 'dp', [(i, i ^ r << low) for i in range(dp_count)])  54.2 us
    pallas_call x1, Pallas kernels, per_device(): pl.pallas_call(functools.partial(k_middle, mp), grid=(grid,), in_specs=[s...  54.1 us
    pallas_call x1, Pallas kernels, per_device(): pl.pallas_call(functools.partial(k_turn, mp), grid=(grid,), in_specs=[sme...  52.7 us
    ppermute x24, starting transfers between devices, exchange(): lax.ppermute(value, 'dp', [(i, i ^ r << low) for i in range(dp_count)])  51.4 us
    pallas_call x8, Pallas kernels, weight_grads(): pl.pallas_call(functools.partial(k_grads, pairs), grid=(per,), in_specs=i...  50.6 us
    pallas_call x1, Pallas kernels, per_device(): pl.pallas_call(functools.partial(k_return, mp), grid=(grid,), in_specs=[s...  41.3 us
    ppermute x24, starting transfers between devices, scatter_stage(): lax.ppermute(mine[r], 'dp', [(i, i ^ r << low) for i in range(dp_count)])  34.7 us
    pallas_call x2, Pallas kernels, apply_moves(): pl.pallas_call(functools.partial(k_apply, plan, len(before)), grid=(plan....  31.7 us
  transfers between devices with their start and end apart: 71, of which 21 were waited for; matrix products, arithmetic and copies ran while one was open for 2% of the time, Pallas kernels for 45%

profile of v2, /device:TPU:0, one launch (start us, length us, event | category | flops | bytes accessed | tf_op | source)
XLA Modules:
  0.0 544.8 jit_solution(6223503581457632194)
XLA Ops:
  0.7 3.9 convert.8
  17.5 24.8 %gates_first.1 = (f32[1024,512]{1,0:T(8,128)}, bf16[1024,512]{1,0:T(8,128)(2,1)}, f32[1024,1024]{1,0:T(8,128)}, f32[1024,1024]{1,0:T(8,128)}, f32[1024,1024]{1,0...) custom-call(bf16[8,128,512]{2,1,0:T(8,128)(2,1)} %bitcast.81, ...), custom_call_target="tpu_custom_call" | custom-call | flops 3221225472 | bytes 25165824 | tf_op jit(solution)/shard_map/gates_first/pallas_call | solution.py:837
  44.4 54.1 %block_forward.1 = (bf16[1024,1024]{1,0:T(8,128)(2,1)}, bf16[1024,1024]{1,0:T(8,128)(2,1)}, bf16[1024,1024]{1,0:T(8,128)(2,1)}, f32[1024,512]{1,0:T(8,128)}, bf1...) custom-call(s32[3]{0:T(128)} %pad_add_fusion.info, ...), custom_call_target="tpu_custom_call" | custom-call | flops 8589934592 | bytes 62914560 | tf_op jit(solution)/shard_map/block_forward/pallas_call | solution.py:853
  100.5 52.7 %block_turn.1 = (bf16[1024,1024]{1,0:T(8,128)(2,1)}, bf16[1024,1024]{1,0:T(8,128)(2,1)}, bf16[1024,1024]{1,0:T(8,128)(2,1)}, bf16[1024,512]{1,0:T(8,128)(2,1)}, ...) custom-call(s32[3]{0:T(128)} %pad_add_fusion.info, ...), custom_call_target="tpu_custom_call" | custom-call | flops 10737418240 | bytes 62914560 | tf_op jit(solution)/shard_map/block_turn/pallas_call | solution.py:880
  153.6 6.5 %weight_grads.13 = bf16[2,512,1024]{2,1,0:T(8,128)(2,1)} custom-call(bf16[1024,512]{1,0:T(8,128)(2,1)} %get-tuple-element.201.refs_0_, bf16[1024,512]{1,0:T(8,128)(2,1)} %get-tuple-element.202.refs_1_, bf16[1024,2048]{1,0:T(8,128)(2,1)} %get-tuple-element.203.refs_2_, bf16[1024,2048]{1,0:T(8,128)(2,1)} %get-tuple-element.204.refs_3_), custom_call_target="tpu_custom_call" | custom-call | flops 2147483648 | bytes 4194304 | tf_op jit(solution)/shard_map/weight_grads/pallas_call | solution.py:910
  160.2 6.7 %weight_grads.12.refs_2_ = bf16[2,512,1024]{2,1,0:T(8,128)(2,1)} custom-call(bf16[1024,512]{1,0:T(8,128)(2,1)} %get-tuple-element.201.refs_0_, bf16[1024,512]{1,0:T(8,128)(2,1)} %get-tuple-element.202.refs_1_, bf16[1024,2048]{1,0:T(8,128)(2,1)} %get-tuple-element.203.refs_2_, bf16[1024,2048]{1,0:T(8,128)(2,1)} %get-tuple-element.204.refs_3_), custom_call_target="tpu_custom_call" | custom-call | flops 2147483648 | bytes 4194304 | tf_op jit(solution)/shard_map/weight_grads/pallas_call | solution.py:910
  167.6 41.3 %block_return.1 = (bf16[1024,1024]{1,0:T(8,128)(2,1)}, bf16[1024,1024]{1,0:T(8,128)(2,1)}, bf16[1024,1024]{1,0:T(8,128)(2,1)}, bf16[1024,512]{1,0:T(8,128)(2,1)}...) custom-call(s32[3]{0:T(128)} %pad_add_fusion.info, ...), custom_call_target="tpu_custom_call" | custom-call | flops 8589934592 | bytes 62914560 | tf_op jit(solution)/shard_map/block_return/pallas_call | solution.py:1107
  208.9 6.6 %weight_grads.9 = bf16[2,512,1024]{2,1,0:T(8,128)(2,1)} custom-call(bf16[1024,512]{1,0:T(8,128)(2,1)} %get-tuple-element.175.refs_0_, bf16[1024,512]{1,0:T(8,128)(2,1)} %get-tuple-element.176.refs_1_, bf16[1024,2048]{1,0:T(8,128)(2,1)} %get-tuple-element.177.refs_2_, bf16[1024,2048]{1,0:T(8,128)(2,1)} %get-tuple-element.178.refs_3_), custom_call_target="tpu_custom_call" | custom-call | flops 2147483648 | bytes 4194304 | tf_op jit(solution)/shard_map/weight_grads/pallas_call | solution.py:910
  215.5 6.6 %weight_grads.8.refs_2_ = bf16[2,512,1024]{2,1,0:T(8,128)(2,1)} custom-call(bf16[1024,512]{1,0:T(8,128)(2,1)} %get-tuple-element.175.refs_0_, bf16[1024,512]{1,0:T(8,128)(2,1)} %get-tuple-element.176.refs_1_, bf16[1024,2048]{1,0:T(8,128)(2,1)} %get-tuple-element.177.refs_2_, bf16[1024,2048]{1,0:T(8,128)(2,1)} %get-tuple-element.178.refs_3_), custom_call_target="tpu_custom_call" | custom-call | flops 2147483648 | bytes 4194304 | tf_op jit(solution)/shard_map/weight_grads/pallas_call | solution.py:910
  222.6 6.1 %weight_grads.15 = bf16[4,512,512]{2,1,0:T(8,128)(2,1)} custom-call(bf16[1024,512]{1,0:T(8,128)(2,1)} %get-tuple-element.205.refs_0_, bf16[1024,512]{1,0:T(8,128)(2,1)} %get-tuple-element.206.refs_1_, bf16[1024,1024]{1,0:T(8,128)(2,1)} %get-tuple-element.207.refs_2_, bf16[1024,1024]{1,0:T(8,128)(2,1)} %get-tuple-element.208.refs_3_, ...), custom_call_target="tpu_custom_call" | custom-call | flops 2147483648 | bytes 4194304 | tf_op jit(solution)/shard_map/weight_grads/pallas_call | solution.py:910
  228.7 6.1 %weight_grads.14.refs_4_ = bf16[4,512,512]{2,1,0:T(8,128)(2,1)} custom-call(bf16[1024,512]{1,0:T(8,128)(2,1)} %get-tuple-element.205.refs_0_, bf16[1024,512]{1,0:T(8,128)(2,1)} %get-tuple-element.206.refs_1_, bf16[1024,1024]{1,0:T(8,128)(2,1)} %get-tuple-element.207.refs_2_, bf16[1024,1024]{1,0:T(8,128)(2,1)} %get-tuple-element.208.refs_3_, ...), custom_call_target="tpu_custom_call" | custom-call | flops 2147483648 | bytes 4194304 | tf_op jit(solution)/shard_map/weight_grads/pallas_call | solution.py:910
  239.0 18.9 %block_last.1 = (bf16[1024,1024]{1,0:T(8,128)(2,1)}, bf16[1024,1024]{1,0:T(8,128)(2,1)}, bf16[1024,1024]{1,0:T(8,128)(2,1)}, f32[8,128,512]{2,1,0:T(8,128)}, f32[8,512]{1,0:T(8,128)}, /*index=5*/f32[2,8,1024]{2,1,0:T(8,128)}) custom-call(s32[3]{0:T(128)} %pad_add_fusion.info, f32[2,1024]{1,0:T(2,128)} %copy-done.46, ...), custom_call_target="tpu_custom_call" | custom-call | flops 3221225472 | bytes 31457280 | tf_op jit(solution)/shard_map/block_last/pallas_call | solution.py:1133
  259.6 6.1 %weight_grads.11 = bf16[4,512,512]{2,1,0:T(8,128)(2,1)} custom-call(bf16[1024,512]{1,0:T(8,128)(2,1)} %get-tuple-element.179.refs_0_, bf16[1024,512]{1,0:T(8,128)(2,1)} %get-tuple-element.180.refs_1_, bf16[1024,1024]{1,0:T(8,128)(2,1)} %get-tuple-element.181.refs_2_, bf16[1024,1024]{1,0:T(8,128)(2,1)} %get-tuple-element.182.refs_3_, ...), custom_call_target="tpu_custom_call" | custom-call | flops 2147483648 | bytes 4194304 | tf_op jit(solution)/shard_map/weight_grads/pallas_call | solution.py:910
  282.4 6.0 %weight_grads.10.refs_4_ = bf16[4,512,512]{2,1,0:T(8,128)(2,1)} custom-call(bf16[1024,512]{1,0:T(8,128)(2,1)} %get-tuple-element.179.refs_0_, bf16[1024,512]{1,0:T(8,128)(2,1)} %get-tuple-element.180.refs_1_, bf16[1024,1024]{1,0:T(8,128)(2,1)} %get-tuple-element.181.refs_2_, bf16[1024,1024]{1,0:T(8,128)(2,1)} %get-tuple-element.182.refs_3_, ...), custom_call_target="tpu_custom_call" | custom-call | flops 2147483648 | bytes 4194304 | tf_op jit(solution)/shard_map/weight_grads/pallas_call | solution.py:910
  291.4 13.5 %rotate.3 = (bf16[128,2688]{1,0:T(8,128)(2,1)}, bf16[128,2688]{1,0:T(8,128)(2,1)}, bf16[128,2688]{1,0:T(8,128)(2,1)}, bf16[128,2688]{1,0:T(8,128)(2,1)}, bf16[12...) custom-call(s32[17]{0:T(128)} %pad_add_fusion.1.who, ...), custom_call_target="tpu_custom_call" | custom-call | flops 8589934592 | bytes 16777216 | tf_op jit(solution)/shard_map/rotate/pallas_call | solution.py:962
  310.0 13.6 %rotate.2 = (bf16[128,2688]{1,0:T(8,128)(2,1)}, bf16[128,2688]{1,0:T(8,128)(2,1)}, bf16[128,2688]{1,0:T(8,128)(2,1)}, bf16[128,2688]{1,0:T(8,128)(2,1)}, bf16[12...) custom-call(s32[17]{0:T(128)} %pad_add_fusion.1.who, ...), custom_call_target="tpu_custom_call" | custom-call | flops 8589934592 | bytes 16777216 | tf_op jit(solution)/shard_map/rotate/pallas_call | solution.py:962
  329.7 3.9 collective-permute-done.30.refs_7_
  352.0 11.2 %collective-permute-done.15.refs_6_ = bf16[128,1408]{1,0:T(8,128)(2,1)} collective-permute-done((bf16[128,1408]{1,0:T(8,128)(2,1)}, bf16[128,1408]{1,0:T(8,128)(2,1)}, u32[]{:S(2)}, u32[]{:S(2)}) %collective-permute-start.15) | collective-permute-done | bytes 360480 | tf_op jit(solution)/shard_map/ppermute | solution.py:985
  366.8 7.1 %collective-permute-done.12.refs_2_ = bf16[128,2688]{1,0:T(8,128)(2,1)S(1)} collective-permute-done((bf16[128,2688]{1,0:T(8,128)(2,1)}, bf16[128,2688]{1,0:T(8,128)(2,1)S(1)}, u32[]{:S(2)}, u32[]{:S(2)}) %collective-permute-start.12) | collective-permute-done | bytes 688160 | tf_op jit(solution)/shard_map/ppermute | solution.py:985
  373.9 4.3 collective-permute-start.33
  404.4 10.2 %collective-permute-start.50 = (bf16[32,2688]{1,0:T(8,128)(2,1)}, bf16[32,2688]{1,0:T(8,128)(2,1)S(1)}, u32[]{:S(2)}, u32[]{:S(2)}) collective-permute-start(bf16[32,2688]{1,0:T(8,128)(2,1)} %get-tuple-element.240), channel_id=1, source_target_pairs={{0,16},{2,18},{4,20},{6,22},{8,24},{10,26},{12,28},{14,30},{16,0},... | collective-permute-start | bytes 516104 | tf_op jit(solution)/shard_map/ppermute | solution.py:941
  414.6 3.9 adam.3
  423.4 4.5 collective-permute-done.43
  428.3 4.4 collective-permute-done.44
  442.7 18.7 %collective-permute-done.38 = bf16[32,2688]{1,0:T(8,128)(2,1)S(1)} collective-permute-done((bf16[32,2688]{1,0:T(8,128)(2,1)}, bf16[32,2688]{1,0:T(8,128)(2,1)S(1)}, u32[]{:S(2)}, u32[]{:S(2)}) %collective-permute-start.38) | collective-permute-done | bytes 172064 | tf_op jit(solution)/shard_map/ppermute | solution.py:941
  462.6 7.1 %collective-permute-start.58 = (bf16[128,1408]{1,0:T(8,128)(2,1)S(1)}, bf16[128,1408]{1,0:T(8,128)(2,1)S(1)}, u32[]{:S(2)}, u32[]{:S(2)}) collective-permute-start(bf16[128,1408]{1,0:T(8,128)(2,1)S(1)} %constant_dynamic-update-slice_fusion.14.refs_8_), channel_id=1, source_target_pairs={{0,8},{2,10},{4,12},{6,14},{8,0},{10,2},{12,4},{14,6},{16,24},{18,... | collective-permute-start | bytes 1081352 | tf_op jit(solution)/shard_map/ppermute | solution.py:941
  469.7 7.4 %collective-permute-done.59.refs_10_ = bf16[128,1408]{1,0:T(8,128)(2,1)S(1)} collective-permute-done((bf16[128,1408]{1,0:T(8,128)(2,1)S(1)}, bf16[128,1408]{1,0:T(8,128)(2,1)S(1)}, u32[]{:S(2)}, u32[]{:S(2)}) %collective-permute-start.59) | collective-permute-done | bytes 360480 | tf_op jit(solution)/shard_map/ppermute | solution.py:941
  477.1 6.7 %collective-permute-done.58.refs_9_ = bf16[128,1408]{1,0:T(8,128)(2,1)S(1)} collective-permute-done((bf16[128,1408]{1,0:T(8,128)(2,1)S(1)}, bf16[128,1408]{1,0:T(8,128)(2,1)S(1)}, u32[]{:S(2)}, u32[]{:S(2)}) %collective-permute-start.58) | collective-permute-done | bytes 360480 | tf_op jit(solution)/shard_map/ppermute | solution.py:941
  488.5 11.9 %collective-permute-start.46 = (bf16[128,1408]{1,0:T(8,128)(2,1)S(1)}, bf16[128,1408]{1,0:T(8,128)(2,1)}, u32[]{:S(2)}, u32[]{:S(2)}) collective-permute-start(bf16[128,1408]{1,0:T(8,128)(2,1)S(1)} %constant_dynamic-update-slice_fusion.6.refs_8_), channel_id=1, source_target_pairs={{0,8},{2,10},{4,12},{6,14},{8,0},{10,2},{12,4},{14,6},{16,24},{18,... | collective-permute-start | bytes 1081352 | tf_op jit(solution)/shard_map/ppermute | solution.py:941
  504.1 15.9 %apply_moves.2 = (f32[2,2,512,1024]{3,2,1,0:T(8,128)}, f32[2,4,512,512]{3,2,1,0:T(8,128)}) custom-call(s32[17]{0:T(128)} %pad_add_fusion.1.who, f32[2,6,512,512]{3,2,1,0:T(8,128)} %basis.7, f32[2,2,8,128,128]{4,3,2,1,0:T(8,128)} %refs_0_.7, f32[2,4,4,128,128]{4,3,2,1,0:T(8,128)} %refs_1_.7, f32[2,2,512,1024]{3,2,1,0:T(8,128)} %refs_2_.3, ...), custom_call_target="tpu_custom_call" | custom-call | flops 8589934592 | bytes 25165824 | tf_op jit(solution)/shard_map/apply_moves/pallas_call | solution.py:1057
  520.0 7.7 %collective-permute-done.41.refs_6_ = bf16[128,2688]{1,0:T(8,128)(2,1)S(1)} collective-permute-done((bf16[128,2688]{1,0:T(8,128)(2,1)S(1)}, bf16[128,2688]{1,0:T(8,128)(2,1)S(1)}, u32[]{:S(2)}, u32[]{:S(2)}) %collective-permute-start.41) | collective-permute-done | bytes 688160 | tf_op jit(solution)/shard_map/ppermute | solution.py:941
  528.8 15.8 %apply_moves.3 = (f32[2,2,512,1024]{3,2,1,0:T(8,128)}, f32[2,4,512,512]{3,2,1,0:T(8,128)}) custom-call(s32[17]{0:T(128)} %pad_add_fusion.1.who, f32[2,6,512,512]{3,2,1,0:T(8,128)} %basis.7, f32[2,2,8,128,128]{4,3,2,1,0:T(8,128)} %refs_0_.7, f32[2,4,4,128,128]{4,3,2,1,0:T(8,128)} %refs_1_.7, ...), custom_call_target="tpu_custom_call", output_to_operand_aliasing={{0}: (14, {}), {1}: (15, {})} | custom-call | flops 8589934592 | bytes 25165824 | tf_op jit(solution)/shard_map/apply_moves/pallas_call | solution.py:1057
  (315 shorter events, 127.9 us)
Async XLA Ops:
  6.6 36.7 %collective-permute-start.4 = (bf16[4,512,512]{2,1,0:T(8,128)(2,1)}, bf16[4,512,512]{2,1,0:T(8,128)(2,1)}, u32[]{:S(2)}, u32[]{:S(2)}) collective-permute-start(bf16[4,512,512]{2,1,0:T(8,128)(2,1)} %get-tuple-element.263.refs_4_.refs_0_), channel_id=1, source_target_pairs={{1,0},{0,1},{3,2},{2,3},{5,4},{4,5},{7,6},{6,7},{9,8},{8,9},{11,10... | collective-permute-start | bytes 6291464 | tf_op jit(solution)/shard_map/ppermute | solution.py:753
  12.6 30.7 %collective-permute-start.3 = (bf16[2,512,1024]{2,1,0:T(8,128)(2,1)}, bf16[2,512,1024]{2,1,0:T(8,128)(2,1)}, u32[]{:S(2)}, u32[]{:S(2)}) collective-permute-start(bf16[2,512,1024]{2,1,0:T(8,128)(2,1)} %get-tuple-element.262.refs_2_), channel_id=1, source_target_pairs={{1,0},{0,1},{3,2},{2,3},{5,4},{4,5},{7,6},{6,7},{9,8},{8,9},{11,10... | collective-permute-start | bytes 6291464 | tf_op jit(solution)/shard_map/ppermute | solution.py:753
  13.1 86.4 %collective-permute-start.6 = (bf16[2,512,1024]{2,1,0:T(8,128)(2,1)}, bf16[2,512,1024]{2,1,0:T(8,128)(2,1)}, u32[]{:S(2)}, u32[]{:S(2)}) collective-permute-start(bf16[2,512,1024]{2,1,0:T(8,128)(2,1)} %get-tuple-element.261.refs_2_), channel_id=1, source_target_pairs={{1,0},{0,1},{3,2},{2,3},{5,4},{4,5},{7,6},{6,7},{9,8},{8,9},{11,10... | collective-permute-start | bytes 6291464 | tf_op jit(solution)/shard_map/ppermute | solution.py:753
  166.8 124.3 %collective-permute-start.23 = (bf16[2,512,1024]{2,1,0:T(8,128)(2,1)S(1)}, bf16[2,512,1024]{2,1,0:T(8,128)(2,1)}, u32[]{:S(2)}, u32[]{:S(2)}) collective-permute-start(bf16[2,512,1024]{2,1,0:T(8,128)(2,1)S(1)} %copy-done.2), channel_id=1, source_target_pairs={{0,1},{1,0},{2,3},{3,2},{4,5},{5,4},{6,7},{7,6},{8,9},{9,8},{10,11... | collective-permute-start | bytes 6291464 | tf_op jit(solution)/shard_map/ppermute | solution.py:926
  235.0 56.4 %collective-permute-start.24 = (bf16[4,512,512]{2,1,0:T(8,128)(2,1)}, bf16[4,512,512]{2,1,0:T(8,128)(2,1)}, u32[]{:S(2)}, u32[]{:S(2)}) collective-permute-start(bf16[4,512,512]{2,1,0:T(8,128)(2,1)} %weight_grads.15), channel_id=1, source_target_pairs={{0,1},{1,0},{2,3},{3,2},{4,5},{5,4},{6,7},{7,6},{8,9},{9,8},{10,11... | collective-permute-start | bytes 6291464 | tf_op jit(solution)/shard_map/ppermute | solution.py:926
  235.3 72.6 %collective-permute-start.9 = (bf16[2,512,1024]{2,1,0:T(8,128)(2,1)}, bf16[2,512,1024]{2,1,0:T(8,128)(2,1)}, u32[]{:S(2)}, u32[]{:S(2)}) collective-permute-start(bf16[2,512,1024]{2,1,0:T(8,128)(2,1)} %weight_grads.9), channel_id=1, source_target_pairs={{0,1},{1,0},{2,3},{3,2},{4,5},{5,4},{6,7},{7,6},{8,9},{9,8},{10,11... | collective-permute-start | bytes 6291464 | tf_op jit(solution)/shard_map/ppermute | solution.py:926
  235.5 30.7 %collective-permute-start.67 = (f32[16,128]{1,0:T(8,128)S(1)}, f32[16,128]{1,0:T(8,128)S(1)}, u32[]{:S(2)}, u32[]{:S(2)}) collective-permute-start(f32[16,128]{1,0:T(8,128)S(1)} %fusion.1), channel_id=1, source_target_pairs={{0,2},{2,0},{4,6},{6,4},{8,10},{10,8},{12,14},{14,12},{16,18},{18,... | collective-permute-start | bytes 24584 | tf_op jit(solution)/shard_map/ppermute | solution.py:1095
  265.7 42.8 %collective-permute-start.10 = (bf16[4,512,512]{2,1,0:T(8,128)(2,1)}, bf16[4,512,512]{2,1,0:T(8,128)(2,1)S(1)}, u32[]{:S(2)}, u32[]{:S(2)}) collective-permute-start(bf16[4,512,512]{2,1,0:T(8,128)(2,1)} %weight_grads.11), channel_id=1, source_target_pairs={{0,1},{1,0},{2,3},{3,2},{4,5},{5,4},{6,7},{7,6},{8,9},{9,8},{10,11... | collective-permute-start | bytes 6291464 | tf_op jit(solution)/shard_map/ppermute | solution.py:926
  291.1 32.5 %collective-permute-start.65 = (f32[16,128]{1,0:T(8,128)S(1)}, f32[16,128]{1,0:T(8,128)S(1)}, u32[]{:S(2)}, u32[]{:S(2)}) collective-permute-start(f32[16,128]{1,0:T(8,128)S(1)} %add.51), channel_id=1, source_target_pairs={{0,16},{2,18},{4,20},{6,22},{8,24},{10,26},{12,28},{14,30},{16,0},... | collective-permute-start | bytes 24584 | tf_op jit(solution)/shard_map/ppermute | solution.py:1095
  304.9 20.2 %collective-permute-start.28 = (bf16[128,1408]{1,0:T(8,128)(2,1)}, bf16[128,1408]{1,0:T(8,128)(2,1)S(1)}, u32[]{:S(2)}, u32[]{:S(2)}) collective-permute-start(bf16[128,1408]{1,0:T(8,128)(2,1)} %get-tuple-element.216), channel_id=1, source_target_pairs={{0,8},{2,10},{4,12},{6,14},{8,0},{10,2},{12,4},{14,6},{16,24},{18,... | collective-permute-start | bytes 1081352 | tf_op jit(solution)/shard_map/ppermute | solution.py:985
  305.3 20.7 %collective-permute-start.29 = (bf16[128,1408]{1,0:T(8,128)(2,1)}, bf16[128,1408]{1,0:T(8,128)(2,1)}, u32[]{:S(2)}, u32[]{:S(2)}) collective-permute-start(bf16[128,1408]{1,0:T(8,128)(2,1)} %get-tuple-element.217), channel_id=1, source_target_pairs={{0,16},{2,18},{4,20},{6,22},{8,24},{10,26},{12,28},{14,30},{16,0},... | collective-permute-start | bytes 1081352 | tf_op jit(solution)/shard_map/ppermute | solution.py:985
  307.9 31.6 %collective-permute-start.25 = (bf16[128,2688]{1,0:T(8,128)(2,1)}, bf16[128,2688]{1,0:T(8,128)(2,1)S(1)}, u32[]{:S(2)}, u32[]{:S(2)}) collective-permute-start(bf16[128,2688]{1,0:T(8,128)(2,1)} %get-tuple-element.212), channel_id=1, source_target_pairs={{0,2},{2,0},{4,6},{6,4},{8,10},{10,8},{12,14},{14,12},{16,18},{18,... | collective-permute-start | bytes 2064392 | tf_op jit(solution)/shard_map/ppermute | solution.py:985
  308.5 32.5 %collective-permute-start.26 = (bf16[128,2688]{1,0:T(8,128)(2,1)}, bf16[128,2688]{1,0:T(8,128)(2,1)S(1)}, u32[]{:S(2)}, u32[]{:S(2)}) collective-permute-start(bf16[128,2688]{1,0:T(8,128)(2,1)} %get-tuple-element.213), channel_id=1, source_target_pairs={{0,4},{2,6},{4,0},{6,2},{8,12},{10,14},{12,8},{14,10},{16,20},{18,... | collective-permute-start | bytes 2064392 | tf_op jit(solution)/shard_map/ppermute | solution.py:985
  334.3 30.9 %collective-permute-start.11 = (bf16[128,2688]{1,0:T(8,128)(2,1)}, bf16[128,2688]{1,0:T(8,128)(2,1)S(1)}, u32[]{:S(2)}, u32[]{:S(2)}) collective-permute-start(bf16[128,2688]{1,0:T(8,128)(2,1)} %get-tuple-element.186), channel_id=1, source_target_pairs={{0,2},{2,0},{4,6},{6,4},{8,10},{10,8},{12,14},{14,12},{16,18},{18,... | collective-permute-start | bytes 2064392 | tf_op jit(solution)/shard_map/ppermute | solution.py:985
  338.0 35.8 %collective-permute-start.12 = (bf16[128,2688]{1,0:T(8,128)(2,1)}, bf16[128,2688]{1,0:T(8,128)(2,1)S(1)}, u32[]{:S(2)}, u32[]{:S(2)}) collective-permute-start(bf16[128,2688]{1,0:T(8,128)(2,1)} %get-tuple-element.187), channel_id=1, source_target_pairs={{0,4},{2,6},{4,0},{6,2},{8,12},{10,14},{12,8},{14,10},{16,20},{18,... | collective-permute-start | bytes 2064392 | tf_op jit(solution)/shard_map/ppermute | solution.py:985
  339.5 34.3 %collective-permute-start.13 = (bf16[128,2688]{1,0:T(8,128)(2,1)}, bf16[128,2688]{1,0:T(8,128)(2,1)S(1)}, u32[]{:S(2)}, u32[]{:S(2)}) collective-permute-start(bf16[128,2688]{1,0:T(8,128)(2,1)} %get-tuple-element.188), channel_id=1, source_target_pairs={{0,6},{2,4},{4,2},{6,0},{8,14},{10,12},{12,10},{14,8},{16,22},{18,... | collective-permute-start | bytes 2064392 | tf_op jit(solution)/shard_map/ppermute | solution.py:985
  341.0 22.2 %collective-permute-start.15 = (bf16[128,1408]{1,0:T(8,128)(2,1)}, bf16[128,1408]{1,0:T(8,128)(2,1)}, u32[]{:S(2)}, u32[]{:S(2)}) collective-permute-start(bf16[128,1408]{1,0:T(8,128)(2,1)} %get-tuple-element.191), channel_id=1, source_target_pairs={{0,16},{2,18},{4,20},{6,22},{8,24},{10,26},{12,28},{14,30},{16,0},... | collective-permute-start | bytes 1081352 | tf_op jit(solution)/shard_map/ppermute | solution.py:985
  400.0 23.1 %collective-permute-start.57 = (bf16[32,1408]{1,0:T(8,128)(2,1)}, bf16[32,1408]{1,0:T(8,128)(2,1)S(1)}, u32[]{:S(2)}, u32[]{:S(2)}) collective-permute-start(bf16[32,1408]{1,0:T(8,128)(2,1)} %get-tuple-element.241), channel_id=1, source_target_pairs={{0,6},{2,4},{4,2},{6,0},{8,14},{10,12},{12,10},{14,8},{16,22},{18,... | collective-permute-start | bytes 270344 | tf_op jit(solution)/shard_map/ppermute | solution.py:941
  403.6 35.8 %collective-permute-start.51 = (bf16[32,2688]{1,0:T(8,128)(2,1)}, bf16[32,2688]{1,0:T(8,128)(2,1)S(1)}, u32[]{:S(2)}, u32[]{:S(2)}) collective-permute-start(bf16[32,2688]{1,0:T(8,128)(2,1)} %get-tuple-element.240), channel_id=1, source_target_pairs={{0,24},{2,26},{4,28},{6,30},{8,16},{10,18},{12,20},{14,22},{16,8},... | collective-permute-start | bytes 516104 | tf_op jit(solution)/shard_map/ppermute | solution.py:941
  404.4 32.8 %collective-permute-start.50 = (bf16[32,2688]{1,0:T(8,128)(2,1)}, bf16[32,2688]{1,0:T(8,128)(2,1)S(1)}, u32[]{:S(2)}, u32[]{:S(2)}) collective-permute-start(bf16[32,2688]{1,0:T(8,128)(2,1)} %get-tuple-element.240), channel_id=1, source_target_pairs={{0,16},{2,18},{4,20},{6,22},{8,24},{10,26},{12,28},{14,30},{16,0},... | collective-permute-start | bytes 516104 | tf_op jit(solution)/shard_map/ppermute | solution.py:941
  434.7 26.7 %collective-permute-start.38 = (bf16[32,2688]{1,0:T(8,128)(2,1)}, bf16[32,2688]{1,0:T(8,128)(2,1)S(1)}, u32[]{:S(2)}, u32[]{:S(2)}) collective-permute-start(bf16[32,2688]{1,0:T(8,128)(2,1)} %get-tuple-element.238), channel_id=1, source_target_pairs={{0,16},{2,18},{4,20},{6,22},{8,24},{10,26},{12,28},{14,30},{16,0},... | collective-permute-start | bytes 516104 | tf_op jit(solution)/shard_map/ppermute | solution.py:941
  436.2 25.1 %collective-permute-start.37 = (bf16[32,2688]{1,0:T(8,128)(2,1)}, bf16[32,2688]{1,0:T(8,128)(2,1)S(1)}, u32[]{:S(2)}, u32[]{:S(2)}) collective-permute-start(bf16[32,2688]{1,0:T(8,128)(2,1)} %get-tuple-element.238), channel_id=1, source_target_pairs={{0,8},{2,10},{4,12},{6,14},{8,0},{10,2},{12,4},{14,6},{16,24},{18,... | collective-permute-start | bytes 516104 | tf_op jit(solution)/shard_map/ppermute | solution.py:941
  437.2 25.3 %collective-permute-start.60 = (bf16[128,1408]{1,0:T(8,128)(2,1)S(1)}, bf16[128,1408]{1,0:T(8,128)(2,1)S(1)}, u32[]{:S(2)}, u32[]{:S(2)}) collective-permute-start(bf16[128,1408]{1,0:T(8,128)(2,1)S(1)} %constant_dynamic-update-slice_fusion.14.refs_8_), channel_id=1, source_target_pairs={{0,24},{2,26},{4,28},{6,30},{8,16},{10,18},{12,20},{14,22},{16,8},... | collective-permute-start | bytes 1081352 | tf_op jit(solution)/shard_map/ppermute | solution.py:941
  439.4 37.7 %collective-permute-start.59 = (bf16[128,1408]{1,0:T(8,128)(2,1)S(1)}, bf16[128,1408]{1,0:T(8,128)(2,1)S(1)}, u32[]{:S(2)}, u32[]{:S(2)}) collective-permute-start(bf16[128,1408]{1,0:T(8,128)(2,1)S(1)} %constant_dynamic-update-slice_fusion.14.refs_8_), channel_id=1, source_target_pairs={{0,16},{2,18},{4,20},{6,22},{8,24},{10,26},{12,28},{14,30},{16,0},... | collective-permute-start | bytes 1081352 | tf_op jit(solution)/shard_map/ppermute | solution.py:941
  442.0 58.4 %collective-permute-start.54 = (bf16[128,2688]{1,0:T(8,128)(2,1)S(1)}, bf16[128,2688]{1,0:T(8,128)(2,1)S(1)}, u32[]{:S(2)}, u32[]{:S(2)}) collective-permute-start(bf16[128,2688]{1,0:T(8,128)(2,1)S(1)} %constant_dynamic-update-slice_fusion.10.refs_4_), channel_id=1, source_target_pairs={{0,6},{2,4},{4,2},{6,0},{8,14},{10,12},{12,10},{14,8},{16,22},{18,... | collective-permute-start | bytes 2064392 | tf_op jit(solution)/shard_map/ppermute | solution.py:941
  461.4 39.8 %collective-permute-start.53 = (bf16[128,2688]{1,0:T(8,128)(2,1)S(1)}, bf16[128,2688]{1,0:T(8,128)(2,1)S(1)}, u32[]{:S(2)}, u32[]{:S(2)}) collective-permute-start(bf16[128,2688]{1,0:T(8,128)(2,1)S(1)} %constant_dynamic-update-slice_fusion.10.refs_4_), channel_id=1, source_target_pairs={{0,4},{2,6},{4,0},{6,2},{8,12},{10,14},{12,8},{14,10},{16,20},{18,... | collective-permute-start | bytes 2064392 | tf_op jit(solution)/shard_map/ppermute | solution.py:941
  461.4 41.8 %collective-permute-start.52 = (bf16[128,2688]{1,0:T(8,128)(2,1)S(1)}, bf16[128,2688]{1,0:T(8,128)(2,1)S(1)}, u32[]{:S(2)}, u32[]{:S(2)}) collective-permute-start(bf16[128,2688]{1,0:T(8,128)(2,1)S(1)} %constant_dynamic-update-slice_fusion.10.refs_4_), channel_id=1, source_target_pairs={{0,2},{2,0},{4,6},{6,4},{8,10},{10,8},{12,14},{14,12},{16,18},{18,... | collective-permute-start | bytes 2064392 | tf_op jit(solution)/shard_map/ppermute | solution.py:941
  462.6 21.3 %collective-permute-start.58 = (bf16[128,1408]{1,0:T(8,128)(2,1)S(1)}, bf16[128,1408]{1,0:T(8,128)(2,1)S(1)}, u32[]{:S(2)}, u32[]{:S(2)}) collective-permute-start(bf16[128,1408]{1,0:T(8,128)(2,1)S(1)} %constant_dynamic-update-slice_fusion.14.refs_8_), channel_id=1, source_target_pairs={{0,8},{2,10},{4,12},{6,14},{8,0},{10,2},{12,4},{14,6},{16,24},{18,... | collective-permute-start | bytes 1081352 | tf_op jit(solution)/shard_map/ppermute | solution.py:941
  483.8 36.1 %collective-permute-start.47 = (bf16[128,1408]{1,0:T(8,128)(2,1)S(1)}, bf16[128,1408]{1,0:T(8,128)(2,1)}, u32[]{:S(2)}, u32[]{:S(2)}) collective-permute-start(bf16[128,1408]{1,0:T(8,128)(2,1)S(1)} %constant_dynamic-update-slice_fusion.6.refs_8_), channel_id=1, source_target_pairs={{0,16},{2,18},{4,20},{6,22},{8,24},{10,26},{12,28},{14,30},{16,0},... | collective-permute-start | bytes 1081352 | tf_op jit(solution)/shard_map/ppermute | solution.py:941
  488.5 31.5 %collective-permute-start.46 = (bf16[128,1408]{1,0:T(8,128)(2,1)S(1)}, bf16[128,1408]{1,0:T(8,128)(2,1)}, u32[]{:S(2)}, u32[]{:S(2)}) collective-permute-start(bf16[128,1408]{1,0:T(8,128)(2,1)S(1)} %constant_dynamic-update-slice_fusion.6.refs_8_), channel_id=1, source_target_pairs={{0,8},{2,10},{4,12},{6,14},{8,0},{10,2},{12,4},{14,6},{16,24},{18,... | collective-permute-start | bytes 1081352 | tf_op jit(solution)/shard_map/ppermute | solution.py:941
  501.2 26.5 %collective-permute-start.41 = (bf16[128,2688]{1,0:T(8,128)(2,1)S(1)}, bf16[128,2688]{1,0:T(8,128)(2,1)S(1)}, u32[]{:S(2)}, u32[]{:S(2)}) collective-permute-start(bf16[128,2688]{1,0:T(8,128)(2,1)S(1)} %constant_dynamic-update-slice_fusion.2.refs_4_), channel_id=1, source_target_pairs={{0,4},{2,6},{4,0},{6,2},{8,12},{10,14},{12,8},{14,10},{16,20},{18,... | collective-permute-start | bytes 2064392 | tf_op jit(solution)/shard_map/ppermute | solution.py:941
  503.2 24.5 %collective-permute-start.40 = (bf16[128,2688]{1,0:T(8,128)(2,1)S(1)}, bf16[128,2688]{1,0:T(8,128)(2,1)S(1)}, u32[]{:S(2)}, u32[]{:S(2)}) collective-permute-start(bf16[128,2688]{1,0:T(8,128)(2,1)S(1)} %constant_dynamic-update-slice_fusion.2.refs_4_), channel_id=1, source_target_pairs={{0,2},{2,0},{4,6},{6,4},{8,10},{10,8},{12,14},{14,12},{16,18},{18,... | collective-permute-start | bytes 2064392 | tf_op jit(solution)/shard_map/ppermute | solution.py:941
  (98 other events, 1290.9 us)

commit v3 on v2

v3 whole, which is shorter than its diff:
```python
import functools
import jax
import jax.numpy as jnp
from jax import lax
from jax.experimental import pallas as pl
from jax.experimental.pallas import tpu as pltpu
from jax.sharding import PartitionSpec as P

NORM_EPS = 1e-05
BETA_ONE = 0.9
BETA_TWO = 0.95
ADAM_EPS = 1e-08
MATRIX_RATE = 0.08
GAIN_RATE = 0.5
BIAS_RATE = 4.0
DECAY_RATE = 0.01
BF = jnp.bfloat16
F32 = jnp.float32
SEG = 8
TILE_STEPS = 32
HC = 512
VMEM_LIMIT = 58 * 1024 * 1024
LOG2E = 1.4426950408889634


def dot_nn(a, b):
    return lax.dot_general(a, b, (((1,), (0,)), ((), ())), preferred_element_type=F32)


def dot_nt(a, b):
    return lax.dot_general(a, b, (((1,), (1,)), ((), ())), preferred_element_type=F32)


def dot_tn(a, b):
    return lax.dot_general(a, b, (((0,), (0,)), ((), ())), preferred_element_type=F32)


def recip(x):
    r = pl.reciprocal(x, approx=True)
    return r * (2.0 - x * r)


def row_blocks(count, size):
    return [slice(at, at + size) for at in range(0, count, size)]


def row_scale(values):
    return lax.rsqrt(jnp.mean(values * values, axis=-1, keepdims=True) + NORM_EPS)


def norm_stage(x_ref, gain, out_ref):
    for r in row_blocks(x_ref.shape[0], 32):
        x = x_ref[r, :]
        out_ref[r, :] = (x * row_scale(x) * gain).astype(BF)


def column_chunks(parts, wide):
    step = min(HC, wide)
    return [(j, c0, j * wide + c0, step) for j in range(parts) for c0 in range(0, wide, step)]


def gate_stage(nin_ref, bias_ref, w_refs, kbuf, state, outs):
    take_ref, loc_ref, prod_ref, cand_ref, wf_ref, wi_ref, q_ref = outs
    for turn, (j, c0, at, wide) in enumerate(column_chunks(len(w_refs), w_refs[0].shape[2])):
        slot = turn % 2
        for k in range(3):
            kbuf[slot, k, :, :wide] = dot_nn(nin_ref[...], w_refs[j][k, :, c0 : c0 + wide])
        cols = slice(at, at + wide)
        bias_f, bias_i = bias_ref[0:1, cols], bias_ref[1:2, cols]
        loc, prod = state[0, :, cols], state[1, :, cols]
        for r in row_blocks(nin_ref.shape[0], 16):
            kf = kbuf[slot, 0, r, :wide] + bias_f
            ki = kbuf[slot, 1, r, :wide] + bias_i
            kc = kbuf[slot, 2, r, :wide]
            tf = jnp.exp(-jnp.abs(kf))
            ti = jnp.exp(-jnp.abs(ki))
            tc = jnp.exp(-jnp.abs(kc))
            gap = jnp.minimum(ki, 0.0) - jnp.minimum(kf, 0.0)
            e = jnp.exp(-jnp.abs(gap))
            ef = jnp.where(gap < 0, e, 1.0)
            ei = jnp.where(gap > 0, e, 1.0)
            nf, ni = ef + ef * tf, ei + ei * ti
            inv = recip(nf + ni)
            keep = ni * inv
            take = nf * inv
            sf = ef * jnp.where(kf >= 0, tf, 1.0)
            si = ei * jnp.where(ki >= 0, ti, 1.0)
            sc = tc * recip(1.0 + tc)
            up = kc >= 0
            cand = jnp.where(up, kc + 0.5, sc)
            slope = jnp.where(up, 1.0, sc - sc * sc)
            take_ref[r, cols] = take.astype(BF)
            cand_ref[r, cols] = cand.astype(BF)
            wf_ref[r, cols] = (keep * inv * sf).astype(BF)
            wi_ref[r, cols] = (take * inv * si).astype(BF)
            q_ref[r, cols] = (take * slope).astype(BF)
            drive = take * cand
            loc0 = keep[:8] * loc + drive[:8]
            prod0 = keep[:8] * prod
            loc = keep[8:] * loc0 + drive[8:]
            prod = keep[8:] * prod0
            loc_ref[r, cols] = jnp.concatenate([loc0, loc]).astype(BF)
            prod_ref[r, cols] = jnp.concatenate([prod0, prod]).astype(BF)
        state[0, :, cols] = loc
        state[1, :, cols] = prod


def fold(state, ends_ref, fin_ref, part, backward):
    hidden = state.shape[2]
    ends_ref[...] = state[...]
    order = list(reversed(range(SEG))) if backward else list(range(SEG))
    value = state[0, order[0] : order[0] + 1, :]
    prod = state[1, order[0] : order[0] + 1, :]
    for s in order[1:]:
        value = state[0, s : s + 1, :] + state[1, s : s + 1, :] * value
        prod = state[1, s : s + 1, :] * prod
    n = hidden // part
    for j in range(n):
        at = ((j - 1) % n if backward else (j + 1) % n) * part
        fin_ref[0:1, j * part : (j + 1) * part] = value[:, at : at + part]
        fin_ref[1:2, j * part : (j + 1) * part] = prod[:, at : at + part]


def carry_forward(inc_ref, ends_ref, start, live):
    start[0:1, :] = inc_ref[0:1, :] * live
    for s in range(SEG - 1):
        start[s + 1 : s + 2, :] = (
            ends_ref[0, s : s + 1, :] + ends_ref[1, s : s + 1, :] * start[s : s + 1, :]
        )


def carry_backward(inc_ref, ends_ref, start, live):
    start[SEG - 1 : SEG, :] = inc_ref[0:1, :] * live
    for s in reversed(range(1, SEG)):
        start[s - 1 : s, :] = (
            ends_ref[0, s : s + 1, :] + ends_ref[1, s : s + 1, :] * start[s : s + 1, :]
        )


def state_stage(start, loc_ref, prod_ref, hlow_ref):
    rows, hidden = loc_ref.shape
    for _, _, at, wide in column_chunks(1, hidden):
        cols = slice(at, at + wide)
        c = jnp.concatenate([start[:, cols], start[:, cols]])
        for r in row_blocks(rows, 16):
            hlow_ref[r, cols] = (loc_ref[r, cols].astype(F32) + prod_ref[r, cols].astype(F32) * c).astype(BF)


def mlp_stage(x_ref, hlow_ref, w_refs, m_refs, gain, kbuf, mid_ref, nmid_ref, act_ref, slope_ref):
    part = w_refs[0].shape[2]
    total = x_ref[...]
    for j, w in enumerate(w_refs):
        total = total + dot_nt(hlow_ref[:, j * part : (j + 1) * part], w[0])
    mid_ref[...] = total
    norm_stage(mid_ref, gain, nmid_ref)
    wide = m_refs[0].shape[2]
    total = mid_ref[...]
    for turn, (j, c0, at, step) in enumerate(column_chunks(len(m_refs), wide)):
        slot = turn % 2
        kbuf[slot, 0, :, :step] = dot_nn(nmid_ref[...], m_refs[j][0, :, c0 : c0 + step])
        cols = slice(at, at + step)
        acts = []
        for r in row_blocks(x_ref.shape[0], 16):
            pre = kbuf[slot, 0, r, :step]
            t = recip(1.0 + jnp.abs(pre) * (0.3275911 * 0.7071067811865476))
            bell = jnp.exp(pre * pre * -0.5)
            poly = (
                (((0.5307027145 * t - 0.7265760135) * t + 0.7107068705) * t - 0.142248368) * t
                + 0.127414796
            ) * t
            tail = poly * bell
            cdf = jnp.where(pre >= 0, 1.0 - tail, tail)
            acts.append((pre * cdf).astype(BF))
            slope_ref[r, cols] = (cdf + pre * (bell * 0.3989422804014327)).astype(BF)
        acts = jnp.concatenate(acts)
        act_ref[:, cols] = acts
        total = total + dot_nt(acts, m_refs[j][1, :, c0 : c0 + step])
    return total


def norm_back_stage(src_ref, gain, dn_ref, dx_ref, sums_ref, low_ref):
    sums = sums_ref[...]
    for r in row_blocks(src_ref.shape[0], 32):
        x = src_ref[r, :]
        scale = row_scale(x)
        unit = x * scale
        d = dn_ref[r, :]
        e = d * gain
        dx = dx_ref[r, :] + scale * (e - unit * jnp.mean(e * unit, axis=-1, keepdims=True))
        dx_ref[r, :] = dx
        if low_ref is not None:
            low_ref[r, :] = dx.astype(BF)
        g = d * unit
        sums = sums + ((g[:8] + g[8:16]) + (g[16:24] + g[24:]))
    sums_ref[...] = sums


def mlp_back_stage(dx_ref, slope_ref, mid_ref, m_refs, gain, dn_ref, dz_ref, dpre_ref, dout_ref, sums_ref):
    dz_ref[...] = dx_ref[...].astype(BF)
    wide = m_refs[0].shape[2]
    for j, c0, at, step in column_chunks(len(m_refs), wide):
        cols = slice(at, at + step)
        dact = dot_nn(dz_ref[...], m_refs[j][1, :, c0 : c0 + step])
        dpre_ref[:, cols] = (dact * slope_ref[:, cols].astype(F32)).astype(BF)
    total = None
    for j, m in enumerate(m_refs):
        term = dot_nt(dpre_ref[:, j * wide : (j + 1) * wide], m[0])
        total = term if total is None else total + term
    dn_ref[...] = total
    norm_back_stage(mid_ref, gain, dn_ref, dx_ref, sums_ref, dout_ref)


def adjoint_stage(dout_ref, w_refs, take_ref, kbuf, state, lam_ref, prod_ref):
    for turn, (j, c0, at, wide) in enumerate(column_chunks(len(w_refs), w_refs[0].shape[2])):
        slot = turn % 2
        kbuf[slot, 0, :, :wide] = dot_nn(dout_ref[...], w_refs[j][0, :, c0 : c0 + wide])
        cols = slice(at, at + wide)
        mu, prod = state[0, :, cols], state[1, :, cols]
        for r in reversed(row_blocks(dout_ref.shape[0], 16)):
            u = kbuf[slot, 0, r, :wide]
            keep = 1.0 - take_ref[r, cols].astype(F32)
            lam1 = u[8:] + mu
            lam0 = u[:8] + keep[8:] * lam1
            mu = keep[:8] * lam0
            prod0 = prod * keep[8:]
            lam_ref[r, cols] = jnp.concatenate([lam0, lam1]).astype(BF)
            prod_ref[r, cols] = jnp.concatenate([prod0, prod]).astype(BF)
            prod = prod0 * keep[:8]
        state[0, :, cols] = mu
        state[1, :, cols] = prod


def keys_stage(first, mu_in, h_in, ins, dk_refs, bias_ref):
    lam_ref, prod_ref, hlow_ref, hbefore_ref, cand_ref, wf_ref, wi_ref, q_ref = ins
    dkf_ref, dki_ref, dkc_ref = dk_refs
    rows, hidden = lam_ref.shape
    for _, _, at, wide in column_chunks(1, hidden):
        cols = slice(at, at + wide)
        c = jnp.concatenate([mu_in[:, cols], mu_in[:, cols]])
        before = jnp.where(first, h_in[:, cols], hbefore_ref[:, cols].astype(F32)[8:])
        sum_f, sum_i = bias_ref[0, :, cols], bias_ref[1, :, cols]
        for r in row_blocks(rows, 16):
            lam = lam_ref[r, cols].astype(F32) + prod_ref[r, cols].astype(F32) * c
            h = hlow_ref[r, cols].astype(F32)
            diff = lam * (cand_ref[r, cols].astype(F32) - jnp.concatenate([before, h[:8]]))
            before = h[8:]
            df = (-(diff * wf_ref[r, cols].astype(F32))).astype(BF)
            di = (diff * wi_ref[r, cols].astype(F32)).astype(BF)
            dkf_ref[r, cols] = df
            dki_ref[r, cols] = di
            dkc_ref[r, cols] = (lam * q_ref[r, cols].astype(F32)).astype(BF)
            df, di = df.astype(F32), di.astype(F32)
            sum_f = sum_f + (df[:8] + df[8:])
            sum_i = sum_i + (di[:8] + di[8:])
        bias_ref[0, :, cols] = sum_f
        bias_ref[1, :, cols] = sum_i


def keys_back_stage(dk_refs, w_refs, dn_ref):
    part = w_refs[0].shape[2]
    total = None
    for j, w in enumerate(w_refs):
        for k in range(3):
            term = dot_nt(dk_refs[k][:, j * part : (j + 1) * part], w[k])
            total = term if total is None else total + term
    dn_ref[...] = total


def spread(src_ref, dst, lanes):
    steps = src_ref.shape[1]
    for c in range(lanes.shape[0]):
        cols = slice(c * 128, c * 128 + 128)
        for s in range(SEG):
            lanes[c, pl.ds(s, steps, stride=SEG), :] = src_ref[s, :, cols].astype(F32)
        dst[:, cols] = lanes[c]


def gather_out(src, dst_ref, lanes):
    steps = dst_ref.shape[1]
    for c in range(lanes.shape[0]):
        cols = slice(c * 128, c * 128 + 128)
        lanes[c] = src[:, cols]
        for s in range(SEG):
            dst_ref[s, :, cols] = lanes[c, pl.ds(s, steps, stride=SEG), :]


def reset(state):
    state[0] = jnp.zeros_like(state[0])
    state[1] = jnp.ones_like(state[1])


def k_cast(*refs):
    half = len(refs) // 2
    for src, dst in zip(refs[:half], refs[half:]):
        dst[...] = src[0].astype(BF)


def k_first(n_parts, in_ref, gain_ref, bias_ref, *refs):
    w = refs[:n_parts]
    xp, nin = refs[n_parts : n_parts + 2]
    gates = refs[n_parts + 2 : n_parts + 9]
    ends, fin, kbuf, state, lanes = refs[n_parts + 9 :]
    g = pl.program_id(0)

    @pl.when(g == 0)
    def _():
        reset(state)

    spread(in_ref, xp, lanes)
    norm_stage(xp, gain_ref[0:1, :], nin)
    gate_stage(nin, bias_ref, w, kbuf, state, gates)

    @pl.when(g == pl.num_programs(0) - 1)
    def _():
        fold(state, ends, fin, w[0].shape[2], False)


def k_middle(n_parts, info, inc, ends_in, x, loc, prod, gain, gain_next, bias, *refs):
    wo = refs[:n_parts]
    m = refs[n_parts : 2 * n_parts]
    w = refs[2 * n_parts : 3 * n_parts]
    hlow, start, mid, nmid, act, slope, xn, nin = refs[3 * n_parts : 3 * n_parts + 8]
    gates = refs[3 * n_parts + 8 : 3 * n_parts + 15]
    ends, fin, kbuf, state = refs[3 * n_parts + 15 :]
    g = pl.program_id(0)

    @pl.when(g == 0)
    def _():
        reset(state)
        carry_forward(inc, ends_in, start, (info[1] > 0).astype(F32))

    state_stage(start, loc, prod, hlow)
    xn[...] = mlp_stage(x, hlow, wo, m, gain[1:2, :], kbuf, mid, nmid, act, slope)
    norm_stage(xn, gain_next[0:1, :], nin)
    gate_stage(nin, bias, w, kbuf, state, gates)

    @pl.when(g == pl.num_programs(0) - 1)
    def _():
        fold(state, ends, fin, w[0].shape[2], False)


def k_turn(n_parts, info, inc, ends_in, x, loc, prod, take, gain, cot, *refs):
    wo = refs[:n_parts]
    m = refs[n_parts : 2 * n_parts]
    (hlow, start, nmid, act, out, dz, dpre, dout, dx, lam, prod_o, ends, fin, sums) = refs[
        2 * n_parts : 2 * n_parts + 14
    ]
    kbuf, state, mid, slope, dn, lanes, out_lanes = refs[2 * n_parts + 14 :]
    g = pl.program_id(0)
    tile = pl.num_programs(0) - 1 - g
    rows = x.shape[0]
    steps_all = pl.num_programs(0) * (rows // SEG)

    @pl.when(g == 0)
    def _():
        reset(state)
        sums[...] = jnp.zeros_like(sums)
        carry_forward(inc, ends_in, start, (info[1] > 0).astype(F32))

    state_stage(start, loc, prod, hlow)
    top = mlp_stage(x, hlow, wo, m, gain[1:2, :], kbuf, mid, nmid, act, slope)
    at = lax.broadcasted_iota(jnp.int32, (rows, 1), 0)
    place = info[1] * (SEG * steps_all) + (at % SEG) * steps_all + tile * (rows // SEG) + at // SEG
    mask = (place < info[0]).astype(F32)
    gather_out(top * mask, out, out_lanes)

    @pl.when(g >= 0)
    def _():
        spread(cot, dx, lanes)
        dx[...] = dx[...] * mask
        mlp_back_stage(dx, slope, mid, m, gain[1:2, :], dn, dz, dpre, dout, sums)
        adjoint_stage(dout, wo, take, kbuf, state, lam, prod_o)

    @pl.when(g == pl.num_programs(0) - 1)
    def _():
        fold(state, ends, fin, wo[0].shape[2], True)


def k_return(n_parts, info, inc, ends_in, h_in, *refs):
    keys = refs[:8]
    x, dx_in, mid, slope, take, gain, gain_prev = refs[8:15]
    refs = refs[15:]
    w = refs[:n_parts]
    m = refs[n_parts : 2 * n_parts]
    wo = refs[2 * n_parts : 3 * n_parts]
    (dkf, dki, dkc, dz, dpre, dout, dx, lam_o, prod_o, ends, fin, sums_in, sums_mid, bias) = refs[
        3 * n_parts : 3 * n_parts + 14
    ]
    kbuf, state, start, dn = refs[3 * n_parts + 14 :]
    g = pl.program_id(0)
    last = pl.num_programs(0) - 1

    @pl.when(g == 0)
    def _():
        reset(state)
        sums_in[...] = jnp.zeros_like(sums_in)
        sums_mid[...] = jnp.zeros_like(sums_mid)
        bias[...] = jnp.zeros_like(bias)
        carry_backward(inc, ends_in, start, (info[1] < info[2] - 1).astype(F32))

    keys_stage(g == last, start, h_in, keys, (dkf, dki, dkc), bias)
    keys_back_stage((dkf, dki, dkc), w, dn)
    dx[...] = dx_in[...]
    norm_back_stage(x, gain[0:1, :], dn, dx, sums_in, None)
    mlp_back_stage(dx, slope, mid, m, gain_prev[1:2, :], dn, dz, dpre, dout, sums_mid)
    adjoint_stage(dout, wo, take, kbuf, state, lam_o, prod_o)

    @pl.when(g == last)
    def _():
        fold(state, ends, fin, wo[0].shape[2], True)


def k_last(n_parts, n_after, *refs):
    info, inc, ends_in, h_in = refs[n_after : n_after + 4]
    refs = refs[n_after + 4 :]
    keys = refs[:8]
    x, dx_in, gain = refs[8:11]
    w = refs[11 : 11 + n_parts]
    dkf, dki, dkc, out, sums_in, bias = refs[11 + n_parts : 17 + n_parts]
    start, dn, dx, lanes = refs[17 + n_parts :]
    g = pl.program_id(0)
    last = pl.num_programs(0) - 1

    @pl.when(g == 0)
    def _():
        sums_in[...] = jnp.zeros_like(sums_in)
        bias[...] = jnp.zeros_like(bias)
        carry_backward(inc, ends_in, start, (info[1] < info[2] - 1).astype(F32))

    keys_stage(g == last, start, h_in, keys, (dkf, dki, dkc), bias)
    keys_back_stage((dkf, dki, dkc), w, dn)
    dx[...] = dx_in[...]
    norm_back_stage(x, gain[0:1, :], dn, dx, sums_in, None)
    gather_out(dx, out, lanes)


def k_grads(pairs, n_after, *refs):
    refs = refs[n_after:]
    out = refs[-1]
    for k, (left, right) in enumerate(pairs):
        out[k] = dot_tn(refs[left][...], refs[right][...]).astype(BF)


def place_of(owner, me, stages):
    if stages is None:
        return owner
    relative = owner ^ me
    place = None
    for low, count in stages:
        digit = (relative >> low) & ((1 << count) - 1)
        place = digit if place is None else (place << count) + digit
    return place


def turn_blocks(value, blocks, inverse):
    order = blocks.shape[-1]
    dot = dot_nt if inverse else dot_nn
    return jnp.concatenate(
        [
            dot(value[:, b * order : (b + 1) * order], blocks[0, 0, b].astype(BF))
            for b in range(blocks.shape[2])
        ],
        axis=1,
    )


def k_rotate(plan, n_recv, pairs, n_after, who, basis, *refs):
    refs = refs[n_after:]
    n_src = len(plan.sources)
    n_left, n_right = 1 + max(p[0] for p in pairs), len(pairs)
    blocks = refs[:n_src]
    recv = refs[n_src : n_src * (1 + n_recv)]
    refs = refs[n_src * (1 + n_recv) :]
    lefts, rights = refs[:n_left], refs[n_left : n_left + n_right]
    refs = refs[n_left + n_right :]
    n_out = sum(plan.firsts)
    outs, bufs = refs[:n_out], refs[n_out:]
    g = pl.program_id(0)
    share = plan.share
    width = basis.shape[2]
    count = width // share
    for chunk, runs in enumerate(plan.runs):
        at, pair = plan.source_of[chunk], pairs[plan.matrix_of[chunk]]

        @pl.when(g == chunk)
        def _(runs=runs, at=at, pair=pair):
            total = dot_tn(lefts[pair[0]][...], rights[pair[1]][...])
            for ref in recv[at * n_recv : (at + 1) * n_recv]:
                total = total + ref[0].astype(F32)
            turned = turn_blocks(total.astype(BF), blocks[at], False).astype(BF)
            done = dot_tn(basis[0, 0].astype(BF), turned).astype(BF)
            for b in range(count):
                for stream, src, dst, wide in runs:
                    row = place_of(who[b], who[count], plan.stages[stream]) * share
                    bufs[stream][pl.ds(pl.multiple_of(row, share), share), dst : dst + wide] = done[
                        b * share : (b + 1) * share, src : src + wide
                    ]

    @pl.when(g == pl.num_programs(0) - 1)
    def _():
        at = 0
        for stream, pieces in enumerate(plan.firsts):
            rows = width // pieces
            for r in range(pieces):
                outs[at][...] = bufs[stream][r * rows : (r + 1) * rows, :]
                at += 1


def sum_pieces(refs):
    total = refs[0][...].astype(F32)
    for ref in refs[1:]:
        total = total + ref[...].astype(F32)
    return total


def k_combine(n_in, n_out, n_after, n_small, *refs):
    refs = refs[n_after:]
    if n_small:
        at = sum(n_in)
        refs[-1][...] = refs[at][...] + refs[at + 1][...]
        refs = refs[:at] + refs[at + 2 : -1]
    i, o = 0, sum(n_in)
    for take, give in zip(n_in, n_out):
        total = sum_pieces(refs[i : i + take]).astype(BF)
        rows = total.shape[0] // give
        for r in range(give):
            refs[o + r][...] = total[r * rows : (r + 1) * rows, :]
        i += take
        o += give


def k_join(n_in, n_after, *refs):
    refs = refs[n_after:]
    outs = refs[sum(n_in) :]
    i = 0
    for out, take in zip(outs, n_in):
        rows = refs[i].shape[0]
        for r in range(take):
            out[r * rows : (r + 1) * rows, :] = refs[i + r][...]
        i += take


def k_adam(plan, spread_plan, splits, n_alias, fix, *refs):
    n_in = sum(plan.lasts)
    n_src = len(plan.sources)
    pieces = refs[:n_in]
    olds = refs[n_in : n_in + 2 * n_src]
    outs = refs[n_in + 2 * n_src + n_alias :]
    bufs = refs[len(refs) - n_src :]
    moves_o = outs[sum(2 + len(split) for split in splits) :][: len(spread_plan.stages)]
    sums, i = [], 0
    for take in plan.lasts:
        sums.append(sum_pieces(pieces[i : i + take]))
        i += take
    o = 0
    for at, split in enumerate(splits):
        grad_o, first_o = outs[o : o + 2]
        second_o = outs[o + 2 : o + 2 + len(split)]
        o += 2 + len(split)
        first, second = olds[2 * at : 2 * at + 2]
        for chunk in range(plan.begins[at], plan.begins[at + 1]):
            kind, base = plan.where(at, chunk)
            for stream, src, dst, wide in plan.runs[chunk]:
                grad_o[:, 0, kind, base + src : base + src + wide] = sums[stream][:, dst : dst + wide]
        grad = grad_o[...]
        one = BETA_ONE * first[...] + (1.0 - BETA_ONE) * grad
        two = BETA_TWO * second[...] + (1.0 - BETA_TWO) * grad * grad
        first_o[...] = one
        for ref, (lo, hi) in zip(second_o, split):
            ref[...] = two[:, :, lo:hi, :]
        bufs[at][...] = one * fix[0] / (jnp.sqrt(two * fix[1]) + ADAM_EPS)
        for chunk in range(plan.begins[at], plan.begins[at + 1]):
            kind, base = plan.where(at, chunk)
            for stream, src, dst, wide in spread_plan.runs[chunk]:
                moves_o[stream][:, dst : dst + wide] = bufs[at][
                    :, 0, kind, base + src : base + src + wide
                ].astype(BF)


def k_apply(plan, n_alias, who, basis, *refs):
    n_src = len(plan.sources)
    n_in = sum(plan.firsts)
    blocks = refs[:n_src]
    weights = refs[n_src : 2 * n_src]
    pieces = refs[2 * n_src : 2 * n_src + n_in]
    outs = refs[2 * n_src + n_in + n_alias :][:n_src]
    bufs = refs[2 * n_src + n_in + n_alias + n_src : -1]
    moves = refs[-1]
    g = pl.program_id(0)
    share = plan.share
    width = basis.shape[2]
    count = width // share

    @pl.when(g == 0)
    def _():
        at = 0
        for stream, n in enumerate(plan.firsts):
            rows = width // n
            for r in range(n):
                bufs[stream][r * rows : (r + 1) * rows, :] = pieces[at][...]
                at += 1

    for chunk, runs in enumerate(plan.runs):

        @pl.when(g == chunk)
        def _(runs=runs):
            for stream, src, dst, wide in runs:
                for b in range(count):
                    at = place_of(who[b], who[count], plan.stages[stream]) * share
                    moves[b * share : (b + 1) * share, src : src + wide] = bufs[stream][
                        pl.ds(pl.multiple_of(at, share), share), dst : dst + wide
                    ]

    for at in range(n_src):

        @pl.when((g >= plan.begins[at]) & (g < plan.begins[at + 1]))
        def _(at=at):
            wide = plan.blocks[at]
            back = dot_nn(basis[0, 0].astype(BF), moves[:, :wide]).astype(BF)
            step = turn_blocks(back, blocks[at], True)
            old = weights[at][0, 0]
            outs[at][0, 0] = old - MATRIX_RATE * (step + DECAY_RATE * old)


class Plan:
    def __init__(self, dp_count, width, sources, staged=True):
        bits = dp_count.bit_length() - 1
        x, y, z, rest = (0, 1), (1, 1), (2, 1), (3, bits - 3)
        orders = [[x, y, z, rest], [y, x, z, rest], [z, rest, x, y]]
        self.share = width // dp_count
        self.sources = sources
        self.blocks = [min(512, wide) for _, _, wide in sources]
        self.pers = [wide // block for (_, _, wide), block in zip(sources, self.blocks)]
        self.begins = [0]
        for (_, count, _), per in zip(sources, self.pers):
            self.begins.append(self.begins[-1] + count * per)
        self.source_of, self.matrix_of = [], []
        matrices = 0
        for at, (_, count, _) in enumerate(sources):
            for k in range(count):
                self.source_of += [at] * self.pers[at]
                self.matrix_of += [matrices + k] * self.pers[at]
            matrices += count
        named = []
        for at, block in enumerate(self.blocks):
            for chunk in range(self.begins[at], self.begins[at + 1]):
                named.append([0 if not staged else 2 if lane == 3 else chunk % 2 for lane in range(block // 128)])
        used = sorted({stream for row in named for stream in row})
        self.stages = [orders[stream] if staged else None for stream in used]
        self.cols = [0] * len(used)
        self.runs = []
        for row in named:
            runs = []
            for lane, stream in enumerate(row):
                at = used.index(stream)
                if runs and runs[-1][0] == at:
                    runs[-1][3] += 128
                else:
                    runs.append([at, lane * 128, self.cols[at], 128])
                self.cols[at] += 128
            self.runs.append(runs)
        self.firsts = [1 << stages[0][1] if staged else 1 for stages in self.stages]
        self.lasts = [1 << stages[-1][1] if staged else 1 for stages in self.stages]

    def where(self, at, chunk):
        local = chunk - self.begins[at]
        return local // self.pers[at], local % self.pers[at] * self.blocks[at]

    def local(self, at, g):
        return jnp.clip(g - self.begins[at], 0, self.begins[at + 1] - self.begins[at] - 1)

    def basis_at(self, g):
        index = None
        for at, (base, _, _) in enumerate(self.sources):
            here = base + self.local(at, g) // self.pers[at]
            index = here if index is None else jnp.where(g < self.begins[at], index, here)
        return index


def k_small(*refs):
    gains, biases = refs[-2:]
    for l in range(gains.shape[0]):
        sums_in, sums_mid, bias = refs[3 * l : 3 * l + 3]
        gains[l, 0:1, :] = jnp.sum(sums_in[...], axis=0, keepdims=True)
        gains[l, 1:2, :] = jnp.sum(sums_mid[...], axis=0, keepdims=True)
        for k in range(2):
            biases[l, k : k + 1, :] = jnp.sum(bias[k], axis=0, keepdims=True)


def adam_moments(grads, first, second, fix_one, fix_two):
    first = BETA_ONE * first + (1.0 - BETA_ONE) * grads
    second = BETA_TWO * second + (1.0 - BETA_TWO) * grads * grads
    moves = first / fix_one / (jnp.sqrt(second / fix_two) + ADAM_EPS)
    return (first, second, moves)


def params(parallel=False):
    return pltpu.CompilerParams(
        dimension_semantics=("arbitrary",), vmem_limit_bytes=VMEM_LIMIT
    )


def sds(*shape, dtype=F32):
    return jax.ShapeDtypeStruct(shape, dtype)


def per_device(
    inputs,
    cotangent,
    lengths,
    hidden_weights,
    mlp_weights,
    norm_gains,
    gate_bias,
    left_bases,
    hidden_blocks,
    mlp_blocks,
    hidden_first,
    hidden_second,
    mlp_first,
    mlp_second,
    gain_first,
    gain_second,
    bias_first,
    bias_second,
    step_count,
    row_owner,
):
    dp_count = lax.axis_size("dp")
    mp = lax.axis_size("mp")
    me = lax.axis_index("mp")
    tokens = inputs.shape[1]
    width = inputs.shape[2]
    part_h = hidden_weights.shape[3]
    part_f = mlp_weights.shape[3]
    hid = part_h * mp
    ff = part_f * mp
    layers = hidden_weights.shape[0]
    steps = tokens // SEG
    ts = min(TILE_STEPS, steps)
    tr = ts * SEG
    grid = steps // ts
    share = width // dp_count

    def from_peer(value, j):
        return lax.ppermute(value, "mp", [((m + j) % mp, m) for m in range(mp)])

    def to_next(value):
        return lax.ppermute(value, "mp", [(m, (m + 1) % mp) for m in range(mp)])

    def to_prev(value):
        return lax.ppermute(value, "mp", [((m + 1) % mp, m) for m in range(mp)])

    def cast(picks):
        in_specs, out_specs, shapes = [], [], []
        for weights, l in picks:
            _, count, _, wide = weights.shape
            per = 4 // count
            in_specs.append(
                pl.BlockSpec((1, 1, width, wide // per), lambda g, l=l, per=per: (l, g // per, 0, g % per))
            )
            out_specs.append(pl.BlockSpec((1, width, wide // per), lambda g, per=per: (g // per, 0, g % per)))
            shapes.append(sds(count, width, wide, dtype=BF))
        return pl.pallas_call(
            k_cast,
            grid=(4,),
            in_specs=in_specs,
            out_specs=out_specs,
            out_shape=shapes,
            compiler_params=params(),
            cost_estimate=pl.CostEstimate(flops=0, bytes_accessed=6 * len(picks) * 2**20, transcendentals=0),
            name="cast",
        )(*[weights for weights, _ in picks])

    def with_peers(own):
        return [own] + [from_peer(own, j) for j in range(1, mp)]

    own = cast([(hidden_weights, 0)])
    own += cast([(mlp_weights, 0)] + [(w, l) for l in range(1, layers) for w in (hidden_weights, mlp_weights)])
    hid_parts = [with_peers(own[2 * l]) for l in range(layers)]
    mlp_parts = [with_peers(own[2 * l + 1]) for l in range(layers)]
    bias_all = jnp.concatenate([gate_bias] + [from_peer(gate_bias, j) for j in range(1, mp)], axis=2)
    info = jnp.stack([lengths[0], me, jnp.int32(mp)]).astype(jnp.int32)

    def make_specs(order):
        def tile(cols):
            return pl.BlockSpec((tr, cols), lambda g: (order(g), 0))

        return tile

    def whole(*shape):
        return pl.BlockSpec(shape, lambda g: (0,) * len(shape), pipeline_mode=pl.Buffered(1))

    smem = pl.BlockSpec(memory_space=pltpu.SMEM)
    vmem = pl.BlockSpec(memory_space=pltpu.VMEM)
    hbm = pl.BlockSpec(memory_space=pl.ANY)
    fwd = make_specs(lambda g: g)
    rev = make_specs(lambda g: grid - 1 - g)
    seg_fwd = pl.BlockSpec((SEG, ts, width), lambda g: (0, g, 0))
    seg_rev = pl.BlockSpec((SEG, ts, width), lambda g: (0, grid - 1 - g, 0))
    before_rev = pl.BlockSpec(
        (16, hid), lambda g: (jnp.maximum((grid - 1 - g) * (tr // 16) - 1, 0), 0)
    )
    start_spec = pl.BlockSpec((SEG, hid), lambda g: (0, 0))
    gates_spec = pl.BlockSpec((3, width, part_h), lambda g: (0, 0, 0), pipeline_mode=pl.Buffered(1))
    wout_spec = pl.BlockSpec((1, width, part_h), lambda g: (3, 0, 0), pipeline_mode=pl.Buffered(1))
    mlp_spec = whole(2, width, part_f)
    gain_spec = whole(2, width)
    bias_spec = whole(2, hid)
    ends_spec = pl.BlockSpec((2, SEG, hid), lambda g: (0, 0, 0))
    fin_spec = pl.BlockSpec((2, hid), lambda g: (0, 0))
    sums_spec = pl.BlockSpec((SEG, width), lambda g: (0, 0))
    bsum_spec = pl.BlockSpec((2, SEG, hid), lambda g: (0, 0, 0))
    kbuf = pltpu.VMEM((2, 3, tr, min(HC, max(part_h, part_f))), F32)
    state = pltpu.VMEM((2, SEG, hid), F32)
    start = pltpu.VMEM((SEG, hid), F32)
    row_f32 = pltpu.VMEM((tr, width), F32)
    lanes = pltpu.VMEM((width // 128, tr, 128), F32)

    t_w = sds(tokens, width)
    t_wb = sds(tokens, width, dtype=BF)
    t_hb = sds(tokens, hid, dtype=BF)
    t_fb = sds(tokens, ff, dtype=BF)
    ends_s = sds(2, SEG, hid)
    start_s = sds(SEG, hid)
    fin_s = sds(2, hid)
    sums_s = sds(SEG, width)
    bsum_s = sds(2, SEG, hid)

    def cost(matmul_cols, elems):
        return pl.CostEstimate(
            flops=2 * tokens * width * matmul_cols,
            bytes_accessed=elems,
            transcendentals=0,
        )

    def chain(fin, send, shift, live):
        carry = send(fin)
        for _ in range(mp - 2):
            known = jnp.roll(carry[0:1] * live, shift, axis=1)
            carry = send(jnp.concatenate([fin[0:1] + fin[1:2] * known, fin[1:2]]))
        return carry

    def chain_forward(fin):
        return chain(fin, to_next, -part_h, (me > 0).astype(F32))

    def chain_backward(fin):
        return chain(fin, to_prev, part_h, (me < mp - 1).astype(F32))

    seg_in = inputs.reshape(SEG, steps, width)
    seg_cot = cotangent.reshape(SEG, steps, width)
    saved = []
    f1_out_specs = lambda t: [t(width)] + [t(hid)] * 7 + [ends_spec, fin_spec]
    f1_out_shapes = [t_wb] + [t_hb] * 7 + [ends_s, fin_s]
    outs = pl.pallas_call(
        functools.partial(k_first, mp),
        grid=(grid,),
        in_specs=[seg_fwd, gain_spec, bias_spec] + [gates_spec] * mp,
        out_specs=[fwd(width)] + f1_out_specs(fwd),
        out_shape=[t_w] + f1_out_shapes,
        scratch_shapes=[kbuf, state, lanes],
        compiler_params=params(),
        cost_estimate=cost(3 * hid, 24 * 2**20),
        name="gates_first",
    )(seg_in, norm_gains[0], bias_all[0], *hid_parts[0])
    x, gate = outs[0], outs[1:]
    xs = [x]
    for l in range(layers - 1):
        nin, take, loc, prod, cand, wf, wi, q, ends, fin = gate
        inc = chain_forward(fin)
        outs = pl.pallas_call(
            functools.partial(k_middle, mp),
            grid=(grid,),
            in_specs=[smem, fin_spec, ends_spec, fwd(width), fwd(hid), fwd(hid)]
            + [gain_spec, gain_spec, bias_spec]
            + [wout_spec] * mp
            + [mlp_spec] * mp
            + [gates_spec] * mp,
            out_specs=[fwd(hid), start_spec] + [fwd(width)] * 2 + [fwd(ff)] * 2 + [fwd(width)] + f1_out_specs(fwd),
            out_shape=[t_hb, start_s, t_w, t_wb, t_fb, t_fb, t_w] + f1_out_shapes,
            scratch_shapes=[kbuf, state],
            compiler_params=params(),
            cost_estimate=cost(4 * hid + 2 * ff, 60 * 2**20),
            name="block_forward",
        )(
            info, inc, ends, xs[l], loc, prod,
            norm_gains[l], norm_gains[l + 1], bias_all[l + 1],
            *hid_parts[l], *mlp_parts[l], *hid_parts[l + 1],
        )
        hlow, began, mid, nmid, act, slope, xn = outs[:7]
        saved.append((nin, take, hlow, began, cand, wf, wi, q, mid, nmid, act, slope))
        xs.append(xn)
        gate = outs[7:]
    top = layers - 1
    nin, take, loc, prod, cand, wf, wi, q, ends, fin = gate
    inc = chain_forward(fin)
    outs = pl.pallas_call(
        functools.partial(k_turn, mp),
        grid=(grid,),
        in_specs=[smem, fin_spec, ends_spec, rev(width), rev(hid), rev(hid), rev(hid)]
        + [gain_spec, seg_rev]
        + [wout_spec] * mp
        + [mlp_spec] * mp,
        out_specs=[rev(hid), start_spec, rev(width), rev(ff), seg_rev, rev(width), rev(ff), rev(width), rev(width)]
        + [rev(hid), rev(hid), ends_spec, fin_spec, sums_spec],
        out_shape=[t_hb, start_s, t_wb, t_fb, sds(SEG, steps, width), t_wb, t_fb, t_wb, t_w]
        + [t_hb, t_hb, ends_s, fin_s, sums_s],
        scratch_shapes=[kbuf, state, row_f32, pltpu.VMEM((tr, ff), BF), row_f32, lanes, lanes],
        compiler_params=params(),
        cost_estimate=cost(2 * hid + 4 * ff, 60 * 2**20),
        name="block_turn",
    )(
        info, inc, ends, xs[top], loc, prod, take, norm_gains[top], seg_cot,
        *hid_parts[top], *mlp_parts[top],
    )
    hlow, began, nmid, act, output, dz, dpre, dout, dx, lam, rprod, ends, fin, sums_mid = outs
    output = output.reshape(1, tokens, width)
    saved.append((nin, take, hlow, began, cand, wf, wi, q, None, nmid, act, None))

    def weight_grads(pairs, lefts, rights, part, wide, after):
        count = len(pairs)
        block = min(256, wide)
        per = wide // block
        in_specs = [whole(tokens, width) for _ in lefts]
        in_specs += [pl.BlockSpec((tokens, block), lambda g: (0, part * per + g)) for _ in rights]
        shifted = tuple((left, len(lefts) + right) for left, right in pairs)
        return pl.pallas_call(
            functools.partial(k_grads, shifted, len(after)),
            grid=(per,),
            in_specs=[hbm] * len(after) + in_specs,
            out_specs=pl.BlockSpec((count, width, block), lambda g: (0, 0, g)),
            out_shape=sds(count, width, wide, dtype=BF),
            compiler_params=params(),
            cost_estimate=cost(count * wide, tokens * wide * count * 2),
            name="weight_grads",
        )(*after, *lefts, *rights)

    def send_parts(pairs, lefts, rights, wide, after=()):
        others = []
        for j in range(1, mp):
            sent = weight_grads(pairs, lefts, rights, j, wide, after)
            others.append(lax.ppermute(sent, "mp", [(m, (m + j) % mp) for m in range(mp)]))
        return others

    dp_me = lax.axis_index("dp")
    who = jnp.concatenate([row_owner, dp_me[None].astype(jnp.int32)])
    count_value = step_count[0].astype(F32)
    fix_one = 1.0 - jnp.power(jnp.float32(BETA_ONE), count_value)
    fix_two = 1.0 - jnp.power(jnp.float32(BETA_TWO), count_value)
    fix = jnp.stack([1.0 / fix_one, 1.0 / fix_two])

    def exchange(value, stage):
        low, count = stage
        return [
            lax.ppermute(value, "dp", [(i, i ^ (r << low)) for i in range(dp_count)])
            for r in range(1, 1 << count)
        ]

    def source_spec(plan, at, shape, tail):
        return pl.BlockSpec(shape, lambda g: tail(plan.local(at, g) // plan.pers[at], plan.local(at, g) % plan.pers[at]))

    def rotate(plan, l, pairs, lefts, rights, recv, blocks, after):
        basis_spec = pl.BlockSpec((1, 1, width, width), lambda g: (l, plan.basis_at(g), 0, 0))
        specs, flat = [], []
        for at, one in enumerate(blocks):
            order = one.shape[-1]
            nb = plan.blocks[at] // order
            specs.append(source_spec(plan, at, (1, 1, nb, order, order), lambda k, c: (l, k, c, 0, 0)))
        for at, ones in enumerate(recv):
            for one in ones:
                specs.append(source_spec(plan, at, (1, width, plan.blocks[at]), lambda k, c: (k, 0, c)))
                flat.append(one)
        specs += [whole(tokens, width)] * len(lefts)
        for m in range(len(rights)):
            at = plan.source_of[plan.matrix_of.index(m)]
            first = plan.matrix_of.index(m)
            last = plan.pers[at] - 1
            specs.append(
                pl.BlockSpec(
                    (tokens, plan.blocks[at]), lambda g, first=first, last=last: (0, jnp.clip(g - first, 0, last))
                )
            )
        out_shapes = [
            sds(width // n, cols, dtype=BF) for n, cols in zip(plan.firsts, plan.cols) for _ in range(n)
        ]
        outs = pl.pallas_call(
            functools.partial(k_rotate, plan, mp - 1, pairs, len(after)),
            grid=(plan.begins[-1],),
            in_specs=[smem, basis_spec] + [hbm] * len(after) + specs,
            out_specs=[pl.BlockSpec(o.shape, lambda g: (0, 0)) for o in out_shapes],
            out_shape=out_shapes,
            scratch_shapes=[pltpu.VMEM((width, cols), BF) for cols in plan.cols],
            compiler_params=params(),
            cost_estimate=cost(6 * sum(plan.cols), 24 * 2**20),
            name="rotate",
        )(who, left_bases, *after, *blocks, *flat, *lefts, *rights)
        pieces, at = [], 0
        for n in plan.firsts:
            pieces.append(outs[at : at + n])
            at += n
        return pieces

    def scatter_stage(plan, pieces, at):
        held = []
        for stages, mine in zip(plan.stages, pieces):
            low, count = stages[at]
            got = [
                lax.ppermute(mine[r], "dp", [(i, i ^ (r << low)) for i in range(dp_count)])
                for r in range(1, 1 << count)
            ]
            held.append([mine[0]] + got)
        return held

    def combine(plan, held, at, after=(), small=()):
        flat = [v for one in held for v in one]
        n_in = [len(one) for one in held]
        n_out = [1 << stages[at + 1][1] for stages in plan.stages]
        shapes = [
            sds(one[0].shape[0] // n, one[0].shape[1], dtype=BF) for one, n in zip(held, n_out) for _ in range(n)
        ]
        halves = 2 if all(cols % 256 == 0 for cols in plan.cols) else 1

        def part_of(shape):
            return pl.BlockSpec((shape[0], shape[1] // halves), lambda g: (0, g))

        small_specs = [pl.BlockSpec(v.shape, lambda g: (0, 0)) for v in small]
        outs = pl.pallas_call(
            functools.partial(k_combine, n_in, n_out, len(after), len(small)),
            grid=(halves,),
            in_specs=[hbm] * len(after) + [part_of(v.shape) for v in flat] + small_specs,
            out_specs=[part_of(v.shape) for v in shapes] + small_specs[:1],
            out_shape=shapes + [sds(*v.shape) for v in small[:1]],
            compiler_params=params(),
            cost_estimate=pl.CostEstimate(flops=0, bytes_accessed=6 * 2**20, transcendentals=0),
            name="combine",
        )(*after, *flat, *small)
        if small:
            return [outs[sum(n_out[:i]) : sum(n_out[: i + 1])] for i in range(len(n_out))], outs[-1]
        pieces, i = [], 0
        for n in n_out:
            pieces.append(outs[i : i + n])
            i += n
        return pieces

    def adam(plan, spread_plan, l, held, olds, splits, before):
        flat = [v for one in held for v in one]
        out_specs, shapes, in_specs, bufs = [], [], [], []
        for (_, count, wide), split in zip(plan.sources, splits):
            for lo, hi in ((0, count),) * 2 + split:
                out_specs.append(pl.BlockSpec((share, 1, hi - lo, wide), lambda g: (0, l, 0, 0)))
                shapes.append(sds(share, layers, hi - lo, wide))
            in_specs += [pl.BlockSpec((share, 1, count, wide), lambda g: (0, l, 0, 0))] * 2
            bufs.append(pltpu.VMEM((share, 1, count, wide), F32))
        n_state = len(shapes)
        before = before or ()
        outs = pl.pallas_call(
            functools.partial(k_adam, plan, spread_plan, splits, len(before)),
            grid=(1,),
            in_specs=[smem] + [vmem] * len(flat) + in_specs + [hbm] * len(before),
            out_specs=out_specs + [vmem] * len(spread_plan.cols),
            out_shape=shapes + [sds(share, cols, dtype=BF) for cols in spread_plan.cols],
            scratch_shapes=bufs,
            input_output_aliases={1 + len(flat) + len(olds) + i: i for i in range(len(before))},
            compiler_params=pltpu.CompilerParams(vmem_limit_bytes=VMEM_LIMIT),
            cost_estimate=pl.CostEstimate(flops=0, bytes_accessed=8 * 2**20, transcendentals=0),
            name="adam",
        )(fix, *flat, *olds, *before)
        return tuple(outs[:n_state]), outs[n_state:]

    def gather_moves(plan, moves, after=()):
        held = []
        for stages, value in zip(plan.stages, moves):
            for stage in reversed(stages[2:]):
                value = jnp.concatenate([value] + exchange(value, stage), axis=0)
            held.append([value] + exchange(value, stages[1]))
        halves = 2 if all(cols % 256 == 0 for cols in plan.cols) else 1
        ins = [v for one in held for v in one]
        shapes = [sds(one[0].shape[0] * len(one), one[0].shape[1], dtype=BF) for one in held]

        def part_of(shape):
            return pl.BlockSpec((shape[0], shape[1] // halves), lambda g: (0, g))

        joined = pl.pallas_call(
            functools.partial(k_join, [len(one) for one in held], len(after)),
            grid=(halves,),
            in_specs=[hbm] * len(after) + [part_of(v.shape) for v in ins],
            out_specs=[part_of(v.shape) for v in shapes],
            out_shape=shapes,
            compiler_params=params(),
            cost_estimate=pl.CostEstimate(flops=0, bytes_accessed=4 * 2**20, transcendentals=0),
            name="join",
        )(*after, *ins)
        return [v for stages, value in zip(plan.stages, joined) for v in [value] + exchange(value, stages[0])]

    def apply_moves(plan, l, flat, blocks, weights, before):
        basis_spec = pl.BlockSpec((1, 1, width, width), lambda g: (l, plan.basis_at(g), 0, 0))
        block_specs, specs = [], []
        for at, one in enumerate(blocks):
            order = one.shape[-1]
            nb = plan.blocks[at] // order
            block_specs.append(source_spec(plan, at, (1, 1, nb, order, order), lambda k, c: (l, k, c, 0, 0)))
            specs.append(source_spec(plan, at, (1, 1, width, plan.blocks[at]), lambda k, c: (l, k, 0, c)))
        before = before or ()
        ins = 2 + 2 * len(blocks) + len(flat)
        return tuple(
            pl.pallas_call(
                functools.partial(k_apply, plan, len(before)),
                grid=(plan.begins[-1],),
                in_specs=[smem, basis_spec]
                + block_specs
                + specs
                + [whole(*v.shape) for v in flat]
                + [hbm] * len(before),
                out_specs=specs,
                out_shape=[sds(*w.shape) for w in weights],
                scratch_shapes=[pltpu.VMEM((width, cols), BF) for cols in plan.cols]
                + [pltpu.VMEM((width, max(plan.blocks)), BF)],
                input_output_aliases={ins + i: i for i in range(len(before))},
                compiler_params=params(),
                cost_estimate=cost(2 * sum(plan.cols), 24 * 2**20),
                name="apply_moves",
            )(who, left_bases, *blocks, *weights, *flat, *before)
        )

    plan = Plan(dp_count, width, ((4, 2, part_f), (0, 4, part_h)))
    plain = Plan(dp_count, width, plan.sources, staged=False)
    olds = (mlp_first, mlp_second, hidden_first, hidden_second)
    splits = (((0, 2),), ((0, 2), (2, 4)))

    all_blocks = (mlp_blocks, hidden_blocks)
    stages = len(plan.stages[0])
    mlp_pairs = ((0, 0), (1, 1))
    hid_pairs = ((0, 0), (0, 1), (0, 2), (1, 3))
    all_pairs = tuple(mlp_pairs) + tuple((left + 2, right + 2) for left, right in hid_pairs)

    def finish(l, held, before):
        state, new = before[:2] if before else (None, None)
        back = plan
        state, moves = adam(plan, back, l, held, olds, splits, state)
        flat = gather_moves(back, moves, new[:1] if new else ())
        return state, apply_moves(back, l, flat, all_blocks, (mlp_weights, hidden_weights), new), moves[0]

    done = None
    held = None
    small = []
    gates_after = ()
    for l in reversed(range(layers)):
        nin, take, hlow, began, cand, wf, wi, q, mid, nmid, act, slope = saved[l]
        keys = (lam, rprod, hlow, hlow, cand, wf, wi, q)
        key_specs = [rev(hid)] * 3 + [before_rev] + [rev(hid)] * 4
        inc = chain_backward(fin)
        mlp_recv = send_parts(mlp_pairs, (nmid, dz), (dpre, act), part_f, gates_after)
        if l > 0:
            below = saved[l - 1]
            outs = pl.pallas_call(
                functools.partial(k_return, mp),
                grid=(grid,),
                in_specs=[smem, fin_spec, ends_spec, start_spec]
                + key_specs
                + [rev(width)] * 3
                + [rev(ff), rev(hid), gain_spec, gain_spec]
                + [gates_spec] * mp
                + [mlp_spec] * mp
                + [wout_spec] * mp,
                out_specs=[rev(hid)] * 3
                + [rev(width), rev(ff), rev(width), rev(width), rev(hid), rev(hid)]
                + [ends_spec, fin_spec, sums_spec, sums_spec, bsum_spec],
                out_shape=[t_hb] * 3
                + [t_wb, t_fb, t_wb, t_w, t_hb, t_hb, ends_s, fin_s, sums_s, sums_s, bsum_s],
                scratch_shapes=[kbuf, state, start, row_f32],
                compiler_params=params(),
                cost_estimate=cost(4 * hid + 2 * ff, 60 * 2**20),
                name="block_return",
            )(
                info, inc, ends, began, *keys, xs[l], dx, below[8], below[11], below[1],
                norm_gains[l], norm_gains[l - 1],
                *hid_parts[l], *mlp_parts[l - 1], *hid_parts[l - 1],
            )
            dkf, dki, dkc, dz_next, dpre_next, dout_next, dx, lam, rprod, ends, fin, sums_in, sums_next, bsum = outs
        else:
            outs = pl.pallas_call(
                functools.partial(k_last, mp, len(gates_after)),
                grid=(grid,),
                in_specs=[hbm] * len(gates_after)
                + [smem, fin_spec, ends_spec, start_spec]
                + key_specs
                + [rev(width)] * 2
                + [gain_spec]
                + [gates_spec] * mp,
                out_specs=[rev(hid)] * 3 + [seg_rev, sums_spec, bsum_spec],
                out_shape=[t_hb] * 3 + [sds(SEG, steps, width), sums_s, bsum_s],
                scratch_shapes=[start, row_f32, row_f32, lanes],
                compiler_params=params(),
                cost_estimate=cost(3 * hid, 30 * 2**20),
                name="block_last",
            )(*gates_after, info, inc, ends, began, *keys, xs[l], dx, norm_gains[l], *hid_parts[l])
            dkf, dki, dkc, input_grad, sums_in, bsum = outs
            dz_next = dpre_next = dout_next = sums_next = None
        after = ()
        if held is not None:
            pieces = combine(plan, held, 0)
            after = (pieces[0][0],)
            held = scatter_stage(plan, pieces, 1)
        hid_recv = send_parts(hid_pairs, (nin, dout), (dkf, dki, dkc, hlow), part_h, after)
        after = ()
        if held is not None:
            pieces = combine(plan, held, 1)
            after = (pieces[0][0],)
            held = scatter_stage(plan, pieces, 2)
        pieces = rotate(
            plan, l, all_pairs, (nmid, dz, nin, dout), (dpre, act, dkf, dki, dkc, hlow),
            (mlp_recv, hid_recv), all_blocks, after,
        )
        previous, held = held, scatter_stage(plan, pieces, 0)
        gates_after = (pieces[0][0],)
        if previous is not None:
            previous = scatter_stage(plan, combine(plan, previous, 2, gates_after), 3)
            done = finish(l + 1, previous, done)
        small.append((sums_in, sums_mid, bsum))
        dz, dpre, dout, sums_mid = dz_next, dpre_next, dout_next, sums_next
    small_in = [v for one in reversed(small) for v in one]
    gains, biases = pl.pallas_call(
        k_small,
        in_specs=[vmem] * len(small_in),
        out_specs=[vmem] * 2,
        out_shape=[sds(layers, 2, width), sds(layers, 2, hid)],
        name="small_sums",
    )(*small_in)

    def flat_part(j):
        return jnp.concatenate(
            [gains.reshape(-1, 128), biases[:, :, j * part_h : (j + 1) * part_h].reshape(-1, 128)]
        )

    total = flat_part(0)
    for j in range(1, mp):
        total = total + lax.ppermute(flat_part(j), "mp", [(m, (m + j) % mp) for m in range(mp)])

    def other_half(value, bit):
        return lax.ppermute(value, "dp", [(i, i ^ (1 << bit)) for i in range(dp_count)])

    bits = dp_count.bit_length() - 1
    for at in range(stages - 1):
        pieces, total = combine(plan, held, at, (), (total, other_half(total, at)))
        held = scatter_stage(plan, pieces, at + 1)
    for bit in range(stages - 1, bits):
        total = total + other_half(total, bit)
    total = total.reshape(-1)
    gain_grad = total[: gains.size].reshape(gains.shape)
    bias_grad = total[gains.size :].reshape(layers, 2, part_h)
    done = finish(0, held, done)
    input_grad = input_grad.reshape(1, tokens, width)
    state, (mlp_new, hidden_new), _ = done
    mlp_grad, mlp_first_new, mlp_second_new = state[:3]
    hidden_grad, hidden_first_new, gate_second_new, hidden_second_new = state[3:]
    gain_first_new, gain_second_new, gain_moves = adam_moments(
        gain_grad, gain_first, gain_second, fix_one, fix_two
    )
    bias_first_new, bias_second_new, bias_moves = adam_moments(
        bias_grad, bias_first, bias_second, fix_one, fix_two
    )
    gain_new = norm_gains - GAIN_RATE * gain_moves
    bias_new = gate_bias - BIAS_RATE * bias_moves
    return (
        output,
        input_grad,
        hidden_grad,
        hidden_first_new,
        hidden_second_new,
        gate_second_new,
        hidden_new,
        mlp_grad,
        mlp_first_new,
        mlp_second_new,
        mlp_new,
        gain_grad,
        gain_first_new,
        gain_second_new,
        gain_new,
        bias_grad,
        bias_first_new,
        bias_second_new,
        bias_new,
    )


def solution(mesh):
    in_specs = (
        P("dp", "mp", None),
        P("dp", "mp", None),
        P("dp"),
        P(None, None, None, "mp"),
        P(None, None, None, "mp"),
        P(),
        P(None, None, "mp"),
        P(),
        P(None, None, "mp", None, None),
        P(None, None, "mp", None, None),
        P("dp", None, None, "mp"),
        P("dp", None, None, "mp"),
        P("dp", None, None, "mp"),
        P("dp", None, None, "mp"),
        P(),
        P(),
        P(None, None, "mp"),
        P(None, None, "mp"),
        P(),
        P(),
    )
    out_specs = (
        P("dp", "mp", None),
        P("dp", "mp", None),
        P("dp", None, None, "mp"),
        P("dp", None, None, "mp"),
        P("dp", None, None, "mp"),
        P("dp", None, None, "mp"),
        P(None, None, None, "mp"),
        P("dp", None, None, "mp"),
        P("dp", None, None, "mp"),
        P("dp", None, None, "mp"),
        P(None, None, None, "mp"),
        P(),
        P(),
        P(),
        P(),
        P(None, None, "mp"),
        P(None, None, "mp"),
        P(None, None, "mp"),
        P(None, None, "mp"),
    )
    return jax.shard_map(
        per_device, mesh=mesh, in_specs=in_specs, out_specs=out_specs, check_vma=False
    )
```

time: 551 us -> 448 us (0.81)
  Pallas kernels: 315 us -> 253 us
  starting transfers between devices: 103 us -> 68.8 us
  waiting for transfers between devices: 96.7 us -> 85 us
    ppermute x24, starting transfers between devices: 51.4 us -> 26.3 us  [exchange(): lax.ppermute(value, 'dp', [(i, i ^ r << low) for i in range(dp_count)])]
    pallas_call x1, Pallas kernels: 52.7 us -> 30.2 us  [per_device(): pl.pallas_call(functools.partial(k_turn, mp), grid=(grid,), in_specs=[sme...]
    pallas_call x1, Pallas kernels: 54.1 us -> 33.3 us  [per_device(): pl.pallas_call(functools.partial(k_middle, mp), grid=(grid,), in_specs=[s...]
    pallas_call x1, Pallas kernels: 41.3 us -> 23.1 us  [per_device(): pl.pallas_call(functools.partial(k_return, mp), grid=(grid,), in_specs=[s...]
    ppermute x24, waiting for transfers between devices: 54.2 us -> 36.7 us  [exchange(): lax.ppermute(value, 'dp', [(i, i ^ r << low) for i in range(dp_count)])]
    pallas_call x1, Pallas kernels: 24.8 us -> 16.1 us  [per_device(): pl.pallas_call(functools.partial(k_first, mp), grid=(grid,), in_specs=[se...]
    ppermute x14 -> x9, starting transfers between devices: 14 us -> 6.46 us  [the longest x4 5.41 us: other_half(): lax.ppermute(value, 'dp', [(i, i ^ 1 << bit) for i in range(dp_count)])]
    pallas_call x15 -> x20, Pallas kernels: 111 us -> 118 us  [the longest x2 38.8 us: rotate(): pl.pallas_call(functools.partial(k_rotate, plan, mp - 1, pairs, len(after...]
  transfers between devices with their start and end apart: 71 -> 66, of which waited for: 21 -> 23; matrix products, arithmetic and copies ran while one was open for 2% -> 3% of each run, Pallas kernels for 45% -> 41%
where the time goes in v3:
time: 448 us; the launch traced here: 440 us
  Pallas kernels  253 us (56%)
  waiting for transfers between devices  85 us (19%)
  starting transfers between devices  68.8 us (15%)
  local copies, waits for them, and re-layouts  22.3 us (5%)
  other arithmetic  7.79 us (2%)
    pallas_call x2, Pallas kernels, rotate(): pl.pallas_call(functools.partial(k_rotate, plan, mp - 1, pairs, len(after...  38.8 us
    ppermute x24, waiting for transfers between devices, exchange(): lax.ppermute(value, 'dp', [(i, i ^ r << low) for i in range(dp_count)])  36.7 us
    ppermute x24, starting transfers between devices, scatter_stage(): lax.ppermute(mine[r], 'dp', [(i, i ^ r << low) for i in range(dp_count)])  33.9 us
    pallas_call x1, Pallas kernels, per_device(): pl.pallas_call(functools.partial(k_middle, mp), grid=(grid,), in_specs=[s...  33.3 us
    pallas_call x2, Pallas kernels, apply_moves(): pl.pallas_call(functools.partial(k_apply, plan, len(before)), grid=(plan....  32.1 us
    pallas_call x1, Pallas kernels, per_device(): pl.pallas_call(functools.partial(k_turn, mp), grid=(grid,), in_specs=[sme...  30.2 us
    ppermute x24, waiting for transfers between devices, scatter_stage(): lax.ppermute(mine[r], 'dp', [(i, i ^ r << low) for i in range(dp_count)])  28.2 us
    ppermute x24, starting transfers between devices, exchange(): lax.ppermute(value, 'dp', [(i, i ^ r << low) for i in range(dp_count)])  26.3 us
  transfers between devices with their start and end apart: 66, of which 23 were waited for; matrix products, arithmetic and copies ran while one was open for 3% of the time, Pallas kernels for 41%

profile of v3, /device:TPU:0, one launch (start us, length us, event | category | flops | bytes accessed | tf_op | source)
XLA Modules:
  0.0 440.1 jit_solution(8637112033487564772)
XLA Ops:
  0.7 4.2 cast.2.refs_0_.refs_19_.refs_16_
  5.3 7.4 %cast.3 = (bf16[2,512,1024]{2,1,0:T(8,128)(2,1)}, bf16[4,512,512]{2,1,0:T(8,128)(2,1)}, bf16[2,512,1024]{2,1,0:T(8,128)(2,1)}) custom-call(f32[2,2,512,1024]{3,2,1,0:T(8,128)} %refs_2_.7, f32[2,4,512,512]{3,2,1,0:T(8,128)} %refs_3_.3, f32[2,2,512,1024]{3,2,1,0:T(8,128)} %refs_2_.7), custom_call_target="tpu_custom_call" | custom-call | bytes 18874368 | tf_op jit(solution)/shard_map/cast/pallas_call | solution.py:764
  18.9 16.1 %gates_first.1 = (f32[1024,512]{1,0:T(8,128)}, bf16[1024,512]{1,0:T(8,128)(2,1)}, bf16[1024,1024]{1,0:T(8,128)(2,1)}, bf16[1024,1024]{1,0:T(8,128)(2,1)}, bf16[1...) custom-call(bf16[8,128,512]{2,1,0:T(8,128)(2,1)} %bitcast.19, ...), custom_call_target="tpu_custom_call" | custom-call | flops 3221225472 | bytes 25165824 | tf_op jit(solution)/shard_map/gates_first/pallas_call | solution.py:855
  37.0 33.3 %block_forward.1 = (bf16[1024,1024]{1,0:T(8,128)(2,1)}, f32[8,1024]{1,0:T(8,128)}, f32[1024,512]{1,0:T(8,128)}, bf16[1024,512]{1,0:T(8,128)(2,1)}, bf16[1024,204...) custom-call(s32[3]{0:T(128)} %pad_add_fusion.info.refs_1_, ...), custom_call_target="tpu_custom_call" | custom-call | flops 8589934592 | bytes 62914560 | tf_op jit(solution)/shard_map/block_forward/pallas_call | solution.py:871
  72.4 30.2 %block_turn.1 = (bf16[1024,1024]{1,0:T(8,128)(2,1)}, f32[8,1024]{1,0:T(8,128)}, bf16[1024,512]{1,0:T(8,128)(2,1)}, bf16[1024,2048]{1,0:T(8,128)(2,1)}, f32[8,128...) custom-call(s32[3]{0:T(128)} %pad_add_fusion.info.refs_1_, ...), custom_call_target="tpu_custom_call" | custom-call | flops 10737418240 | bytes 62914560 | tf_op jit(solution)/shard_map/block_turn/pallas_call | solution.py:897
  102.9 6.5 %weight_grads.4 = bf16[2,512,1024]{2,1,0:T(8,128)(2,1)} custom-call(bf16[1024,512]{1,0:T(8,128)(2,1)} %get-tuple-element.182.refs_0_.refs_4_, bf16[1024,512]{1,0:T(8,128)(2,1)} %get-tuple-element.183.refs_1_.refs_5_, bf16[1024,2048]{1,0:T(8,128)(2,1)} %get-tuple-element.184.refs_2_.refs_8_, bf16[1024,2048]{1,0:T(8,128)(2,1)} %get-tuple-element.185.refs_3_.refs_9_), custom_call_target="tpu_custom_call" | custom-call | flops 2147483648 | bytes 4194304 | tf_op jit(solution)/shard_map/weight_grads/pallas_call | solution.py:927
  110.3 23.1 %block_return.1 = (bf16[1024,1024]{1,0:T(8,128)(2,1)}, bf16[1024,1024]{1,0:T(8,128)(2,1)}, bf16[1024,1024]{1,0:T(8,128)(2,1)}, bf16[1024,512]{1,0:T(8,128)(2,1)}...) custom-call(s32[3]{0:T(128)} %pad_add_fusion.info.refs_1_, ...), custom_call_target="tpu_custom_call" | custom-call | flops 8589934592 | bytes 62914560 | tf_op jit(solution)/shard_map/block_return/pallas_call | solution.py:1155
  133.4 6.0 %weight_grads.5 = bf16[4,512,512]{2,1,0:T(8,128)(2,1)} custom-call(bf16[1024,512]{1,0:T(8,128)(2,1)} %get-tuple-element.186.refs_0_.refs_6_, bf16[1024,512]{1,0:T(8,128)(2,1)} %get-tuple-element.187.refs_1_.refs_7_, bf16[1024,1024]{1,0:T(8,128)(2,1)} %get-tuple-element.202.refs_2_.refs_10_, bf16[1024,1024]{1,0:T(8,128)(2,1)} %get-tuple-element.203.refs_3_.refs_11_, ...), custom_call_target="tpu_custom_call" | custom-call | flops 2147483648 | bytes 4194304 | tf_op jit(solution)/shard_map/weight_grads/pallas_call | solution.py:927
  140.3 3.7 collective-permute-done.9.refs_3_
  144.0 19.5 %rotate.2 = (bf16[256,1536]{1,0:T(8,128)(2,1)}, bf16[256,1536]{1,0:T(8,128)(2,1)}, bf16[256,1536]{1,0:T(8,128)(2,1)}, bf16[256,1536]{1,0:T(8,128)(2,1)}, bf16[25...) custom-call(s32[17]{0:T(128)} %pad_add_fusion.1.who, f32[2,6,512,512]{3,2,1,0:T(8,128)} %basis.7, ...), custom_call_target="tpu_custom_call" | custom-call | flops 25769803776 | bytes 25165824 | tf_op jit(solution)/shard_map/rotate/pallas_call | solution.py:986
  169.3 6.5 %weight_grads.6 = bf16[2,512,1024]{2,1,0:T(8,128)(2,1)} custom-call(bf16[256,1536]{1,0:T(8,128)(2,1)} %get-tuple-element.205.refs_0_, bf16[1024,512]{1,0:T(8,128)(2,1)} %get-tuple-element.230.refs_1_.refs_5_, bf16[1024,512]{1,0:T(8,128)(2,1)} %get-tuple-element.231.refs_2_.refs_6_, bf16[1024,2048]{1,0:T(8,128)(2,1)} %get-tuple-element.232.refs_3_.refs_9_, ...), custom_call_target="tpu_custom_call" | custom-call | flops 2147483648 | bytes 4194304 | tf_op jit(solution)/shard_map/weight_grads/pallas_call | solution.py:927
  176.9 12.4 %block_last.1 = (bf16[1024,1024]{1,0:T(8,128)(2,1)}, bf16[1024,1024]{1,0:T(8,128)(2,1)}, bf16[1024,1024]{1,0:T(8,128)(2,1)}, f32[8,128,512]{2,1,0:T(8,128)}, f32[8,512]{1,0:T(8,128)}, /*index=5*/f32[2,8,1024]{2,1,0:T(8,128)}) custom-call(bf16[256,1536]{1,0:T(8,128)(2,1)} %get-tuple-element.205.refs_0_, s32[3]{0:T(128)} %pad_add_fusion.info.refs_1_, ...), custom_call_target="tpu_custom_call" | custom-call | flops 3221225472 | bytes 31457280 | tf_op jit(solution)/shard_map/block_last/pallas_call | solution.py:1181
  190.6 3.3 combine.6
  194.0 6.4 %weight_grads.7 = bf16[4,512,512]{2,1,0:T(8,128)(2,1)} custom-call(bf16[128,1536]{1,0:T(8,128)(2,1)} %get-tuple-element.223.refs_0_, bf16[1024,512]{1,0:T(8,128)(2,1)} %get-tuple-element.234.refs_1_.refs_7_, bf16[1024,512]{1,0:T(8,128)(2,1)} %get-tuple-element.235.refs_2_.refs_8_, bf16[1024,1024]{1,0:T(8,128)(2,1)} %get-tuple-element.236.refs_3_.refs_11_, ...), custom_call_target="tpu_custom_call" | custom-call | flops 2147483648 | bytes 4194304 | tf_op jit(solution)/shard_map/weight_grads/pallas_call | solution.py:927
  208.5 10.5 %collective-permute-done.16.refs_5_ = bf16[128,1024]{1,0:T(8,128)(2,1)S(1)} collective-permute-done((bf16[128,1024]{1,0:T(8,128)(2,1)S(1)}, bf16[128,1024]{1,0:T(8,128)(2,1)S(1)}, u32[]{:S(2)}, u32[]{:S(2)}) %collective-permute-start.16) | collective-permute-done | bytes 262176 | tf_op jit(solution)/shard_map/ppermute | solution.py:1008
  226.0 19.3 %rotate.3 = (bf16[256,1536]{1,0:T(8,128)(2,1)}, bf16[256,1536]{1,0:T(8,128)(2,1)}, bf16[256,1536]{1,0:T(8,128)(2,1)}, bf16[256,1536]{1,0:T(8,128)(2,1)}, bf16[25...) custom-call(s32[17]{0:T(128)} %pad_add_fusion.1.who, f32[2,6,512,512]{3,2,1,0:T(8,128)} %basis.7, ...), custom_call_target="tpu_custom_call" | custom-call | flops 25769803776 | bytes 25165824 | tf_op jit(solution)/shard_map/rotate/pallas_call | solution.py:986
  260.8 3.4 adam.2
  267.6 7.6 %collective-permute-done.47 = bf16[32,1024]{1,0:T(8,128)(2,1)S(1)} collective-permute-done((bf16[32,1024]{1,0:T(8,128)(2,1)}, bf16[32,1024]{1,0:T(8,128)(2,1)S(1)}, u32[]{:S(2)}, u32[]{:S(2)}) %collective-permute-start.47) | collective-permute-done | bytes 65568 | tf_op jit(solution)/shard_map/ppermute | solution.py:955
  277.5 6.2 %collective-permute-done.44 = bf16[32,1536]{1,0:T(8,128)(2,1)S(1)} collective-permute-done((bf16[32,1536]{1,0:T(8,128)(2,1)}, bf16[32,1536]{1,0:T(8,128)(2,1)S(1)}, u32[]{:S(2)}, u32[]{:S(2)}) %collective-permute-start.44) | collective-permute-done | bytes 98336 | tf_op jit(solution)/shard_map/ppermute | solution.py:955
  284.7 5.7 %collective-permute-done.41 = bf16[32,1536]{1,0:T(8,128)(2,1)S(1)} collective-permute-done((bf16[32,1536]{1,0:T(8,128)(2,1)}, bf16[32,1536]{1,0:T(8,128)(2,1)S(1)}, u32[]{:S(2)}, u32[]{:S(2)}) %collective-permute-start.41) | collective-permute-done | bytes 98336 | tf_op jit(solution)/shard_map/ppermute | solution.py:955
  294.8 3.4 combine.8
  302.7 5.3 %collective-permute-done.27.refs_7_ = f32[32,128]{1,0:T(8,128)S(1)} collective-permute-done((f32[32,128]{1,0:T(8,128)}, f32[32,128]{1,0:T(8,128)S(1)}, u32[]{:S(2)}, u32[]{:S(2)}) %collective-permute-start.27) | collective-permute-done | bytes 16416 | tf_op jit(solution)/shard_map/ppermute | solution.py:1240
  310.7 4.9 %collective-permute-done.26.refs_5_ = bf16[128,1024]{1,0:T(8,128)(2,1)S(1)} collective-permute-done((bf16[128,1024]{1,0:T(8,128)(2,1)}, bf16[128,1024]{1,0:T(8,128)(2,1)S(1)}, u32[]{:S(2)}, u32[]{:S(2)}) %collective-permute-start.26) | collective-permute-done | bytes 262176 | tf_op jit(solution)/shard_map/ppermute | solution.py:1008
  325.9 7.1 %collective-permute-done.28.refs_1_ = bf16[64,1536]{1,0:T(8,128)(2,1)S(1)} collective-permute-done((bf16[64,1536]{1,0:T(8,128)(2,1)}, bf16[64,1536]{1,0:T(8,128)(2,1)S(1)}, u32[]{:S(2)}, u32[]{:S(2)}) %collective-permute-start.28) | collective-permute-done | bytes 196640 | tf_op jit(solution)/shard_map/ppermute | solution.py:1008
  340.9 4.1 collective-permute-start.34
  349.2 5.9 %collective-permute-start.50 = (bf16[256,1536]{1,0:T(8,128)(2,1)}, bf16[256,1536]{1,0:T(8,128)(2,1)S(1)}, u32[]{:S(2)}, u32[]{:S(2)}) collective-permute-start(bf16[256,1536]{1,0:T(8,128)(2,1)} %get-tuple-element.298.refs_4_), channel_id=1, source_target_pairs={{0,2},{2,0},{4,6},{6,4},{8,10},{10,8},{12,14},{14,12},{16,18},{18,... | collective-permute-start | bytes 2359304 | tf_op jit(solution)/shard_map/ppermute | solution.py:955
  355.9 3.4 adam.3
  365.3 6.9 %collective-permute-done.59 = bf16[32,1024]{1,0:T(8,128)(2,1)S(1)} collective-permute-done((bf16[32,1024]{1,0:T(8,128)(2,1)}, bf16[32,1024]{1,0:T(8,128)(2,1)S(1)}, u32[]{:S(2)}, u32[]{:S(2)}) %collective-permute-start.59) | collective-permute-done | bytes 65568 | tf_op jit(solution)/shard_map/ppermute | solution.py:955
  374.2 3.7 collective-permute-done.53
  388.8 16.0 %apply_moves.2 = (f32[2,2,512,1024]{3,2,1,0:T(8,128)}, f32[2,4,512,512]{3,2,1,0:T(8,128)}) custom-call(s32[17]{0:T(128)} %pad_add_fusion.1.who, f32[2,6,512,512]{3,2,1,0:T(8,128)} %basis.7, f32[2,2,8,128,128]{4,3,2,1,0:T(8,128)} %refs_0_.9, f32[2,4,4,128,128]{4,3,2,1,0:T(8,128)} %refs_1_.9, f32[2,2,512,1024]{3,2,1,0:T(8,128)} %refs_2_.7, ...), custom_call_target="tpu_custom_call" | custom-call | flops 8589934592 | bytes 25165824 | tf_op jit(solution)/shard_map/apply_moves/pallas_call | solution.py:1106
  415.2 5.4 %collective-permute-done.65 = f32[32,128]{1,0:T(8,128)S(1)} collective-permute-done((f32[32,128]{1,0:T(8,128)S(1)}, f32[32,128]{1,0:T(8,128)S(1)}, u32[]{:S(2)}, u32[]{:S(2)}) %collective-permute-start.65) | collective-permute-done | bytes 16416 | tf_op jit(solution)/shard_map/ppermute | solution.py:1240
  423.7 16.1 %apply_moves.3 = (f32[2,2,512,1024]{3,2,1,0:T(8,128)}, f32[2,4,512,512]{3,2,1,0:T(8,128)}) custom-call(s32[17]{0:T(128)} %pad_add_fusion.1.who, f32[2,6,512,512]{3,2,1,0:T(8,128)} %basis.7, f32[2,2,8,128,128]{4,3,2,1,0:T(8,128)} %refs_0_.9, f32[2,4,4,128,128]{4,3,2,1,0:T(8,128)} %refs_1_.9, ...), custom_call_target="tpu_custom_call", output_to_operand_aliasing={{0}: (12, {}), {1}: (13, {})} | custom-call | flops 8589934592 | bytes 25165824 | tf_op jit(solution)/shard_map/apply_moves/pallas_call | solution.py:1106
  (298 shorter events, 123.5 us)
Async XLA Ops:
  12.7 23.0 %collective-permute-start.4 = (bf16[4,512,512]{2,1,0:T(8,128)(2,1)}, bf16[4,512,512]{2,1,0:T(8,128)(2,1)}, u32[]{:S(2)}, u32[]{:S(2)}) collective-permute-start(bf16[4,512,512]{2,1,0:T(8,128)(2,1)} %get-tuple-element.173.refs_4_.refs_0_.refs_15_), channel_id=1, source_target_pairs={{1,0},{0,1},{3,2},{2,3},{5,4},{4,5},{7,6},{6,7},{9,8},{8,9},{11,10... | collective-permute-start | bytes 6291464 | tf_op jit(solution)/shard_map/ppermute | solution.py:746
  12.8 23.0 %collective-permute-start.3 = (bf16[2,512,1024]{2,1,0:T(8,128)(2,1)}, bf16[2,512,1024]{2,1,0:T(8,128)(2,1)}, u32[]{:S(2)}, u32[]{:S(2)}) collective-permute-start(bf16[2,512,1024]{2,1,0:T(8,128)(2,1)} %get-tuple-element.172.refs_2_.refs_17_), channel_id=1, source_target_pairs={{1,0},{0,1},{3,2},{2,3},{5,4},{4,5},{7,6},{6,7},{9,8},{8,9},{11,10... | collective-permute-start | bytes 6291464 | tf_op jit(solution)/shard_map/ppermute | solution.py:746
  13.3 57.3 %collective-permute-start.6 = (bf16[2,512,1024]{2,1,0:T(8,128)(2,1)}, bf16[2,512,1024]{2,1,0:T(8,128)(2,1)}, u32[]{:S(2)}, u32[]{:S(2)}) collective-permute-start(bf16[2,512,1024]{2,1,0:T(8,128)(2,1)} %get-tuple-element.180.refs_2_), channel_id=1, source_target_pairs={{1,0},{0,1},{3,2},{2,3},{5,4},{4,5},{7,6},{6,7},{9,8},{8,9},{11,10... | collective-permute-start | bytes 6291464 | tf_op jit(solution)/shard_map/ppermute | solution.py:746
  109.4 30.9 %collective-permute-start.7 = (bf16[2,512,1024]{2,1,0:T(8,128)(2,1)}, bf16[2,512,1024]{2,1,0:T(8,128)(2,1)S(1)}, u32[]{:S(2)}, u32[]{:S(2)}) collective-permute-start(bf16[2,512,1024]{2,1,0:T(8,128)(2,1)} %weight_grads.4), channel_id=1, source_target_pairs={{0,1},{1,0},{2,3},{3,2},{4,5},{5,4},{6,7},{7,6},{8,9},{9,8},{10,11... | collective-permute-start | bytes 6291464 | tf_op jit(solution)/shard_map/ppermute | solution.py:942
  163.5 25.9 %collective-permute-start.11 = (bf16[256,1536]{1,0:T(8,128)(2,1)}, bf16[256,1536]{1,0:T(8,128)(2,1)S(1)}, u32[]{:S(2)}, u32[]{:S(2)}) collective-permute-start(bf16[256,1536]{1,0:T(8,128)(2,1)} %get-tuple-element.218), channel_id=1, source_target_pairs={{0,2},{2,0},{4,6},{6,4},{8,10},{10,8},{12,14},{14,12},{16,18},{18,... | collective-permute-start | bytes 2359304 | tf_op jit(solution)/shard_map/ppermute | solution.py:1008
  166.2 23.2 %collective-permute-start.12 = (bf16[256,1536]{1,0:T(8,128)(2,1)}, bf16[256,1536]{1,0:T(8,128)(2,1)S(1)}, u32[]{:S(2)}, u32[]{:S(2)}) collective-permute-start(bf16[256,1536]{1,0:T(8,128)(2,1)} %get-tuple-element.220), channel_id=1, source_target_pairs={{0,4},{2,6},{4,0},{6,2},{8,12},{10,14},{12,8},{14,10},{16,20},{18,... | collective-permute-start | bytes 2359304 | tf_op jit(solution)/shard_map/ppermute | solution.py:1008
  167.7 21.6 %collective-permute-start.13 = (bf16[256,1024]{1,0:T(8,128)(2,1)}, bf16[256,1024]{1,0:T(8,128)(2,1)S(1)}, u32[]{:S(2)}, u32[]{:S(2)}) collective-permute-start(bf16[256,1024]{1,0:T(8,128)(2,1)} %get-tuple-element.222), channel_id=1, source_target_pairs={{0,8},{2,10},{4,12},{6,14},{8,0},{10,2},{12,4},{14,6},{16,24},{18,... | collective-permute-start | bytes 1572872 | tf_op jit(solution)/shard_map/ppermute | solution.py:1008
  175.8 48.7 %collective-permute-start.17 = (bf16[2,512,1024]{2,1,0:T(8,128)(2,1)}, bf16[2,512,1024]{2,1,0:T(8,128)(2,1)}, u32[]{:S(2)}, u32[]{:S(2)}) collective-permute-start(bf16[2,512,1024]{2,1,0:T(8,128)(2,1)} %weight_grads.6), channel_id=1, source_target_pairs={{0,1},{1,0},{2,3},{3,2},{4,5},{5,4},{6,7},{7,6},{8,9},{9,8},{10,11... | collective-permute-start | bytes 6291464 | tf_op jit(solution)/shard_map/ppermute | solution.py:942
  200.3 25.7 %collective-permute-start.18 = (bf16[4,512,512]{2,1,0:T(8,128)(2,1)}, bf16[4,512,512]{2,1,0:T(8,128)(2,1)}, u32[]{:S(2)}, u32[]{:S(2)}) collective-permute-start(bf16[4,512,512]{2,1,0:T(8,128)(2,1)} %weight_grads.7), channel_id=1, source_target_pairs={{0,1},{1,0},{2,3},{3,2},{4,5},{5,4},{6,7},{7,6},{8,9},{9,8},{10,11... | collective-permute-start | bytes 6291464 | tf_op jit(solution)/shard_map/ppermute | solution.py:942
  201.2 17.8 %collective-permute-start.14 = (bf16[128,1536]{1,0:T(8,128)(2,1)S(1)}, bf16[128,1536]{1,0:T(8,128)(2,1)S(1)}, u32[]{:S(2)}, u32[]{:S(2)}) collective-permute-start(bf16[128,1536]{1,0:T(8,128)(2,1)S(1)} %copy-done.60), channel_id=1, source_target_pairs={{0,4},{2,6},{4,0},{6,2},{8,12},{10,14},{12,8},{14,10},{16,20},{18,... | collective-permute-start | bytes 1179656 | tf_op jit(solution)/shard_map/ppermute | solution.py:1008
  201.7 17.3 %collective-permute-start.15 = (bf16[128,1536]{1,0:T(8,128)(2,1)S(1)}, bf16[128,1536]{1,0:T(8,128)(2,1)S(1)}, u32[]{:S(2)}, u32[]{:S(2)}) collective-permute-start(bf16[128,1536]{1,0:T(8,128)(2,1)S(1)} %copy-done.59), channel_id=1, source_target_pairs={{0,2},{2,0},{4,6},{6,4},{8,10},{10,8},{12,14},{14,12},{16,18},{18,... | collective-permute-start | bytes 1179656 | tf_op jit(solution)/shard_map/ppermute | solution.py:1008
  219.0 34.0 %collective-permute-start.22 = (f32[32,128]{1,0:T(8,128)S(1)}, f32[32,128]{1,0:T(8,128)S(1)}, u32[]{:S(2)}, u32[]{:S(2)}) collective-permute-start(f32[32,128]{1,0:T(8,128)S(1)} %pad_maximum_fusion.6), channel_id=1, source_target_pairs={{0,1},{1,0},{2,3},{3,2},{4,5},{5,4},{6,7},{7,6},{8,9},{9,8},{10,11... | collective-permute-start | bytes 49160 | tf_op jit(solution)/shard_map/ppermute | solution.py:1237
  222.4 22.9 %collective-permute-start.35 = (bf16[64,1536]{1,0:T(8,128)(2,1)}, bf16[64,1536]{1,0:T(8,128)(2,1)S(1)}, u32[]{:S(2)}, u32[]{:S(2)}) collective-permute-start(bf16[64,1536]{1,0:T(8,128)(2,1)} %get-tuple-element.273), channel_id=1, source_target_pairs={{0,8},{2,10},{4,12},{6,14},{8,0},{10,2},{12,4},{14,6},{16,24},{18,... | collective-permute-start | bytes 589832 | tf_op jit(solution)/shard_map/ppermute | solution.py:1008
  222.5 22.9 %collective-permute-start.36 = (bf16[64,1536]{1,0:T(8,128)(2,1)}, bf16[64,1536]{1,0:T(8,128)(2,1)S(1)}, u32[]{:S(2)}, u32[]{:S(2)}) collective-permute-start(bf16[64,1536]{1,0:T(8,128)(2,1)} %get-tuple-element.275), channel_id=1, source_target_pairs={{0,8},{2,10},{4,12},{6,14},{8,0},{10,2},{12,4},{14,6},{16,24},{18,... | collective-permute-start | bytes 589832 | tf_op jit(solution)/shard_map/ppermute | solution.py:1008
  224.5 20.8 %collective-permute-start.37 = (bf16[64,1024]{1,0:T(8,128)(2,1)}, bf16[64,1024]{1,0:T(8,128)(2,1)S(1)}, u32[]{:S(2)}, u32[]{:S(2)}) collective-permute-start(bf16[64,1024]{1,0:T(8,128)(2,1)} %get-tuple-element.277), channel_id=1, source_target_pairs={{0,2},{2,0},{4,6},{6,4},{8,10},{10,8},{12,14},{14,12},{16,18},{18,... | collective-permute-start | bytes 393224 | tf_op jit(solution)/shard_map/ppermute | solution.py:1008
  253.0 38.4 %collective-permute-start.23 = (f32[32,128]{1,0:T(8,128)S(1)}, f32[32,128]{1,0:T(8,128)S(1)}, u32[]{:S(2)}, u32[]{:S(2)}) collective-permute-start(f32[32,128]{1,0:T(8,128)S(1)} %fusion.refs_6_), channel_id=1, source_target_pairs={{0,2},{2,0},{4,6},{6,4},{8,10},{10,8},{12,14},{14,12},{16,18},{18,... | collective-permute-start | bytes 49160 | tf_op jit(solution)/shard_map/ppermute | solution.py:1240
  253.6 40.0 %collective-permute-start.19 = (bf16[256,1536]{1,0:T(8,128)(2,1)}, bf16[256,1536]{1,0:T(8,128)(2,1)S(1)}, u32[]{:S(2)}, u32[]{:S(2)}) collective-permute-start(bf16[256,1536]{1,0:T(8,128)(2,1)} %get-tuple-element.240), channel_id=1, source_target_pairs={{0,2},{2,0},{4,6},{6,4},{8,10},{10,8},{12,14},{14,12},{16,18},{18,... | collective-permute-start | bytes 2359304 | tf_op jit(solution)/shard_map/ppermute | solution.py:1008
  255.9 37.7 %collective-permute-start.20 = (bf16[256,1536]{1,0:T(8,128)(2,1)}, bf16[256,1536]{1,0:T(8,128)(2,1)S(1)}, u32[]{:S(2)}, u32[]{:S(2)}) collective-permute-start(bf16[256,1536]{1,0:T(8,128)(2,1)} %get-tuple-element.242), channel_id=1, source_target_pairs={{0,4},{2,6},{4,0},{6,2},{8,12},{10,14},{12,8},{14,10},{16,20},{18,... | collective-permute-start | bytes 2359304 | tf_op jit(solution)/shard_map/ppermute | solution.py:1008
  258.2 33.8 %collective-permute-start.21 = (bf16[256,1024]{1,0:T(8,128)(2,1)}, bf16[256,1024]{1,0:T(8,128)(2,1)S(1)}, u32[]{:S(2)}, u32[]{:S(2)}) collective-permute-start(bf16[256,1024]{1,0:T(8,128)(2,1)} %get-tuple-element.244), channel_id=1, source_target_pairs={{0,8},{2,10},{4,12},{6,14},{8,0},{10,2},{12,4},{14,6},{16,24},{18,... | collective-permute-start | bytes 1572872 | tf_op jit(solution)/shard_map/ppermute | solution.py:1008
  291.4 27.7 %collective-permute-start.48 = (bf16[64,1024]{1,0:T(8,128)(2,1)S(1)}, bf16[64,1024]{1,0:T(8,128)(2,1)S(1)}, u32[]{:S(2)}, u32[]{:S(2)}) collective-permute-start(bf16[64,1024]{1,0:T(8,128)(2,1)S(1)} %pad_maximum_fusion.4), channel_id=1, source_target_pairs={{0,2},{2,0},{4,6},{6,4},{8,10},{10,8},{12,14},{14,12},{16,18},{18,... | collective-permute-start | bytes 393224 | tf_op jit(solution)/shard_map/ppermute | solution.py:955
  298.2 17.4 %collective-permute-start.24 = (bf16[128,1536]{1,0:T(8,128)(2,1)}, bf16[128,1536]{1,0:T(8,128)(2,1)S(1)}, u32[]{:S(2)}, u32[]{:S(2)}) collective-permute-start(bf16[128,1536]{1,0:T(8,128)(2,1)} %get-tuple-element.254), channel_id=1, source_target_pairs={{0,4},{2,6},{4,0},{6,2},{8,12},{10,14},{12,8},{14,10},{16,20},{18,... | collective-permute-start | bytes 1179656 | tf_op jit(solution)/shard_map/ppermute | solution.py:1008
  308.0 37.0 %collective-permute-start.46 = (bf16[128,1536]{1,0:T(8,128)(2,1)S(1)}, bf16[128,1536]{1,0:T(8,128)(2,1)S(1)}, u32[]{:S(2)}, u32[]{:S(2)}) collective-permute-start(bf16[128,1536]{1,0:T(8,128)(2,1)S(1)} %constant_dynamic-update-slice_fusion.5.refs_2_), channel_id=1, source_target_pairs={{0,2},{2,0},{4,6},{6,4},{8,10},{10,8},{12,14},{14,12},{16,18},{18,... | collective-permute-start | bytes 1179656 | tf_op jit(solution)/shard_map/ppermute | solution.py:955
  315.6 29.4 %collective-permute-start.43 = (bf16[128,1536]{1,0:T(8,128)(2,1)S(1)}, bf16[128,1536]{1,0:T(8,128)(2,1)S(1)}, u32[]{:S(2)}, u32[]{:S(2)}) collective-permute-start(bf16[128,1536]{1,0:T(8,128)(2,1)S(1)} %constant_dynamic-update-slice_fusion.2.refs_0_), channel_id=1, source_target_pairs={{0,4},{2,6},{4,0},{6,2},{8,12},{10,14},{12,8},{14,10},{16,20},{18,... | collective-permute-start | bytes 1179656 | tf_op jit(solution)/shard_map/ppermute | solution.py:955
  319.2 21.7 %collective-permute-start.49 = (bf16[128,1024]{1,0:T(8,128)(2,1)S(1)}, bf16[128,1024]{1,0:T(8,128)(2,1)S(1)}, u32[]{:S(2)}, u32[]{:S(2)}) collective-permute-start(bf16[128,1024]{1,0:T(8,128)(2,1)S(1)} %constant_dynamic-update-slice_fusion.8.refs_4_), channel_id=1, source_target_pairs={{0,16},{2,18},{4,20},{6,22},{8,24},{10,26},{12,28},{14,30},{16,0},... | collective-permute-start | bytes 786440 | tf_op jit(solution)/shard_map/ppermute | solution.py:955
  337.9 17.3 %collective-permute-start.32 = (bf16[32,1536]{1,0:T(8,128)(2,1)}, bf16[32,1536]{1,0:T(8,128)(2,1)S(1)}, u32[]{:S(2)}, u32[]{:S(2)}) collective-permute-start(bf16[32,1536]{1,0:T(8,128)(2,1)} %get-tuple-element.268), channel_id=1, source_target_pairs={{0,16},{2,18},{4,20},{6,22},{8,24},{10,26},{12,28},{14,30},{16,0},... | collective-permute-start | bytes 294920 | tf_op jit(solution)/shard_map/ppermute | solution.py:1008
  338.1 17.1 %collective-permute-start.33 = (bf16[32,1536]{1,0:T(8,128)(2,1)}, bf16[32,1536]{1,0:T(8,128)(2,1)S(1)}, u32[]{:S(2)}, u32[]{:S(2)}) collective-permute-start(bf16[32,1536]{1,0:T(8,128)(2,1)} %get-tuple-element.270), channel_id=1, source_target_pairs={{0,16},{2,18},{4,20},{6,22},{8,24},{10,26},{12,28},{14,30},{16,0},... | collective-permute-start | bytes 294920 | tf_op jit(solution)/shard_map/ppermute | solution.py:1008
  349.2 37.7 %collective-permute-start.50 = (bf16[256,1536]{1,0:T(8,128)(2,1)}, bf16[256,1536]{1,0:T(8,128)(2,1)S(1)}, u32[]{:S(2)}, u32[]{:S(2)}) collective-permute-start(bf16[256,1536]{1,0:T(8,128)(2,1)} %get-tuple-element.298.refs_4_), channel_id=1, source_target_pairs={{0,2},{2,0},{4,6},{6,4},{8,10},{10,8},{12,14},{14,12},{16,18},{18,... | collective-permute-start | bytes 2359304 | tf_op jit(solution)/shard_map/ppermute | solution.py:955
  355.1 31.8 %collective-permute-start.51 = (bf16[256,1536]{1,0:T(8,128)(2,1)}, bf16[256,1536]{1,0:T(8,128)(2,1)S(1)}, u32[]{:S(2)}, u32[]{:S(2)}) collective-permute-start(bf16[256,1536]{1,0:T(8,128)(2,1)} %get-tuple-element.299.refs_6_), channel_id=1, source_target_pairs={{0,4},{2,6},{4,0},{6,2},{8,12},{10,14},{12,8},{14,10},{16,20},{18,... | collective-permute-start | bytes 2359304 | tf_op jit(solution)/shard_map/ppermute | solution.py:955
  355.2 31.6 %collective-permute-start.52 = (bf16[256,1024]{1,0:T(8,128)(2,1)}, bf16[256,1024]{1,0:T(8,128)(2,1)S(1)}, u32[]{:S(2)}, u32[]{:S(2)}) collective-permute-start(bf16[256,1024]{1,0:T(8,128)(2,1)} %get-tuple-element.300.refs_8_), channel_id=1, source_target_pairs={{0,8},{2,10},{4,12},{6,14},{8,0},{10,2},{12,4},{14,6},{16,24},{18,... | collective-permute-start | bytes 1572872 | tf_op jit(solution)/shard_map/ppermute | solution.py:955
  383.6 21.2 %collective-permute-start.61 = (bf16[128,1024]{1,0:T(8,128)(2,1)S(1)}, bf16[128,1024]{1,0:T(8,128)(2,1)S(1)}, u32[]{:S(2)}, u32[]{:S(2)}) collective-permute-start(bf16[128,1024]{1,0:T(8,128)(2,1)S(1)} %constant_dynamic-update-slice_fusion.17.refs_5_), channel_id=1, source_target_pairs={{0,16},{2,18},{4,20},{6,22},{8,24},{10,26},{12,28},{14,30},{16,0},... | collective-permute-start | bytes 786440 | tf_op jit(solution)/shard_map/ppermute | solution.py:955
  386.8 18.1 %collective-permute-start.58 = (bf16[128,1536]{1,0:T(8,128)(2,1)S(1)}, bf16[128,1536]{1,0:T(8,128)(2,1)S(1)}, u32[]{:S(2)}, u32[]{:S(2)}) collective-permute-start(bf16[128,1536]{1,0:T(8,128)(2,1)S(1)} %constant_dynamic-update-slice_fusion.14.refs_3_), channel_id=1, source_target_pairs={{0,2},{2,0},{4,6},{6,4},{8,10},{10,8},{12,14},{14,12},{16,18},{18,... | collective-permute-start | bytes 1179656 | tf_op jit(solution)/shard_map/ppermute | solution.py:955
  386.8 18.0 %collective-permute-start.55 = (bf16[128,1536]{1,0:T(8,128)(2,1)S(1)}, bf16[128,1536]{1,0:T(8,128)(2,1)S(1)}, u32[]{:S(2)}, u32[]{:S(2)}) collective-permute-start(bf16[128,1536]{1,0:T(8,128)(2,1)S(1)} %constant_dynamic-update-slice_fusion.11.refs_1_), channel_id=1, source_target_pairs={{0,4},{2,6},{4,0},{6,2},{8,12},{10,14},{12,8},{14,10},{16,20},{18,... | collective-permute-start | bytes 1179656 | tf_op jit(solution)/shard_map/ppermute | solution.py:955
  (100 other events, 771.3 us)

commit v4 on v3

--- a/solution.py
+++ b/solution.py
@@ -17,9 +17,9 @@
 BF = jnp.bfloat16
 F32 = jnp.float32
 SEG = 8
-TILE_STEPS = 32
-HC = 512
-VMEM_LIMIT = 58 * 1024 * 1024
+TILE_STEPS = 64
+HC = 256
+VMEM_LIMIT = 60 * 1024 * 1024
 LOG2E = 1.4426950408889634
 
 

time: 448 us -> 439 us (0.980)
  waiting for transfers between devices: 85 us -> 76.4 us
    ppermute x24, waiting for transfers between devices: 36.7 us -> 29.1 us  [exchange(): lax.ppermute(value, 'dp', [(i, i ^ r << low) for i in range(dp_count)])]
    unnamed x143 -> x137, local copies, waits for them, and re-layouts: 19.6 us -> 20.9 us
  transfers between devices with their start and end apart: 66 -> 66, of which waited for: 23 -> 24; matrix products, arithmetic and copies ran while one was open for 3% -> 4% of each run, Pallas kernels for 41% -> 42%
where the time goes in v4:
time: 439 us; the launch traced here: 432 us
  Pallas kernels  252 us (57%)
  waiting for transfers between devices  76.4 us (17%)
  starting transfers between devices  68.5 us (16%)
  local copies, waits for them, and re-layouts  24.6 us (6%)
  other arithmetic  7.84 us (2%)
    pallas_call x2, Pallas kernels, rotate(): pl.pallas_call(functools.partial(k_rotate, plan, mp - 1, pairs, len(after...  38.8 us
    pallas_call x1, Pallas kernels, per_device(): pl.pallas_call(functools.partial(k_middle, mp), grid=(grid,), in_specs=[s...  33.3 us
    ppermute x24, starting transfers between devices, scatter_stage(): lax.ppermute(mine[r], 'dp', [(i, i ^ r << low) for i in range(dp_count)])  32.8 us
    pallas_call x2, Pallas kernels, apply_moves(): pl.pallas_call(functools.partial(k_apply, plan, len(before)), grid=(plan....  31.9 us
    ppermute x24, waiting for transfers between devices, exchange(): lax.ppermute(value, 'dp', [(i, i ^ r << low) for i in range(dp_count)])  29.1 us
    pallas_call x1, Pallas kernels, per_device(): pl.pallas_call(functools.partial(k_turn, mp), grid=(grid,), in_specs=[sme...  27.7 us
    ppermute x24, waiting for transfers between devices, scatter_stage(): lax.ppermute(mine[r], 'dp', [(i, i ^ r << low) for i in range(dp_count)])  27.3 us
    ppermute x24, starting transfers between devices, exchange(): lax.ppermute(value, 'dp', [(i, i ^ r << low) for i in range(dp_count)])  27.1 us
  transfers between devices with their start and end apart: 66, of which 24 were waited for; matrix products, arithmetic and copies ran while one was open for 4% of the time, Pallas kernels for 42%

profile of v4, /device:TPU:0, one launch (start us, length us, event | category | flops | bytes accessed | tf_op | source)
XLA Modules:
  0.0 432.3 jit_solution(2701356526092624910)
XLA Ops:
  0.7 4.2 cast.2.refs_0_.refs_19_.refs_16_
  5.3 7.4 %cast.3 = (bf16[2,512,1024]{2,1,0:T(8,128)(2,1)}, bf16[4,512,512]{2,1,0:T(8,128)(2,1)}, bf16[2,512,1024]{2,1,0:T(8,128)(2,1)}) custom-call(f32[2,2,512,1024]{3,2,1,0:T(8,128)} %refs_2_.7, f32[2,4,512,512]{3,2,1,0:T(8,128)} %refs_3_.3, f32[2,2,512,1024]{3,2,1,0:T(8,128)} %refs_2_.7), custom_call_target="tpu_custom_call" | custom-call | bytes 18874368 | tf_op jit(solution)/shard_map/cast/pallas_call | solution.py:764
  18.9 16.8 %gates_first.1 = (f32[1024,512]{1,0:T(8,128)}, bf16[1024,512]{1,0:T(8,128)(2,1)}, bf16[1024,1024]{1,0:T(8,128)(2,1)}, bf16[1024,1024]{1,0:T(8,128)(2,1)}, bf16[1...) custom-call(bf16[8,128,512]{2,1,0:T(8,128)(2,1)} %bitcast.19, ...), custom_call_target="tpu_custom_call" | custom-call | flops 3221225472 | bytes 25165824 | tf_op jit(solution)/shard_map/gates_first/pallas_call | solution.py:855
  37.7 33.3 %block_forward.1 = (bf16[1024,1024]{1,0:T(8,128)(2,1)}, f32[8,1024]{1,0:T(8,128)}, f32[1024,512]{1,0:T(8,128)}, bf16[1024,512]{1,0:T(8,128)(2,1)}, bf16[1024,204...) custom-call(s32[3]{0:T(128)} %pad_add_fusion.info.refs_1_, ...), custom_call_target="tpu_custom_call" | custom-call | flops 8589934592 | bytes 62914560 | tf_op jit(solution)/shard_map/block_forward/pallas_call | solution.py:871
  73.0 27.7 %block_turn.1 = (bf16[1024,1024]{1,0:T(8,128)(2,1)}, f32[8,1024]{1,0:T(8,128)}, bf16[1024,512]{1,0:T(8,128)(2,1)}, bf16[1024,2048]{1,0:T(8,128)(2,1)}, f32[8,128...) custom-call(s32[3]{0:T(128)} %pad_add_fusion.info.refs_1_, ...), custom_call_target="tpu_custom_call" | custom-call | flops 10737418240 | bytes 62914560 | tf_op jit(solution)/shard_map/block_turn/pallas_call | solution.py:897
  101.0 6.5 %weight_grads.4 = bf16[2,512,1024]{2,1,0:T(8,128)(2,1)} custom-call(bf16[1024,512]{1,0:T(8,128)(2,1)} %get-tuple-element.182.refs_0_.refs_4_, bf16[1024,512]{1,0:T(8,128)(2,1)} %get-tuple-element.183.refs_1_.refs_5_, bf16[1024,2048]{1,0:T(8,128)(2,1)} %get-tuple-element.184.refs_2_.refs_8_, bf16[1024,2048]{1,0:T(8,128)(2,1)} %get-tuple-element.185.refs_3_.refs_9_), custom_call_target="tpu_custom_call" | custom-call | flops 2147483648 | bytes 4194304 | tf_op jit(solution)/shard_map/weight_grads/pallas_call | solution.py:927
  108.4 23.6 %block_return.1 = (bf16[1024,1024]{1,0:T(8,128)(2,1)}, bf16[1024,1024]{1,0:T(8,128)(2,1)}, bf16[1024,1024]{1,0:T(8,128)(2,1)}, bf16[1024,512]{1,0:T(8,128)(2,1)}...) custom-call(s32[3]{0:T(128)} %pad_add_fusion.info.refs_1_, ...), custom_call_target="tpu_custom_call" | custom-call | flops 8589934592 | bytes 62914560 | tf_op jit(solution)/shard_map/block_return/pallas_call | solution.py:1155
  132.0 6.0 %weight_grads.5 = bf16[4,512,512]{2,1,0:T(8,128)(2,1)} custom-call(bf16[1024,512]{1,0:T(8,128)(2,1)} %get-tuple-element.186.refs_0_.refs_6_, bf16[1024,512]{1,0:T(8,128)(2,1)} %get-tuple-element.187.refs_1_.refs_7_, bf16[1024,1024]{1,0:T(8,128)(2,1)} %get-tuple-element.202.refs_2_.refs_10_, bf16[1024,1024]{1,0:T(8,128)(2,1)} %get-tuple-element.203.refs_3_.refs_11_, ...), custom_call_target="tpu_custom_call" | custom-call | flops 2147483648 | bytes 4194304 | tf_op jit(solution)/shard_map/weight_grads/pallas_call | solution.py:927
  138.9 3.7 collective-permute-done.9.refs_3_
  142.6 19.5 %rotate.2 = (bf16[256,1536]{1,0:T(8,128)(2,1)}, bf16[256,1536]{1,0:T(8,128)(2,1)}, bf16[256,1536]{1,0:T(8,128)(2,1)}, bf16[256,1536]{1,0:T(8,128)(2,1)}, bf16[25...) custom-call(s32[17]{0:T(128)} %pad_add_fusion.1.who, f32[2,6,512,512]{3,2,1,0:T(8,128)} %basis.7, ...), custom_call_target="tpu_custom_call" | custom-call | flops 25769803776 | bytes 25165824 | tf_op jit(solution)/shard_map/rotate/pallas_call | solution.py:986
  167.9 6.5 %weight_grads.6 = bf16[2,512,1024]{2,1,0:T(8,128)(2,1)} custom-call(bf16[256,1536]{1,0:T(8,128)(2,1)} %get-tuple-element.205.refs_0_, bf16[1024,512]{1,0:T(8,128)(2,1)} %get-tuple-element.230.refs_1_.refs_5_, bf16[1024,512]{1,0:T(8,128)(2,1)} %get-tuple-element.231.refs_2_.refs_6_, bf16[1024,2048]{1,0:T(8,128)(2,1)} %get-tuple-element.232.refs_3_.refs_9_, ...), custom_call_target="tpu_custom_call" | custom-call | flops 2147483648 | bytes 4194304 | tf_op jit(solution)/shard_map/weight_grads/pallas_call | solution.py:927
  175.5 13.2 %block_last.1 = (bf16[1024,1024]{1,0:T(8,128)(2,1)}, bf16[1024,1024]{1,0:T(8,128)(2,1)}, bf16[1024,1024]{1,0:T(8,128)(2,1)}, f32[8,128,512]{2,1,0:T(8,128)}, f32[8,512]{1,0:T(8,128)}, /*index=5*/f32[2,8,1024]{2,1,0:T(8,128)}) custom-call(bf16[256,1536]{1,0:T(8,128)(2,1)} %get-tuple-element.205.refs_0_, s32[3]{0:T(128)} %pad_add_fusion.info.refs_1_, ...), custom_call_target="tpu_custom_call" | custom-call | flops 3221225472 | bytes 31457280 | tf_op jit(solution)/shard_map/block_last/pallas_call | solution.py:1181
  190.1 3.3 combine.6
  193.3 6.1 %weight_grads.7 = bf16[4,512,512]{2,1,0:T(8,128)(2,1)} custom-call(bf16[128,1536]{1,0:T(8,128)(2,1)} %get-tuple-element.223.refs_0_, bf16[1024,512]{1,0:T(8,128)(2,1)} %get-tuple-element.234.refs_1_.refs_7_, bf16[1024,512]{1,0:T(8,128)(2,1)} %get-tuple-element.235.refs_2_.refs_8_, bf16[1024,1024]{1,0:T(8,128)(2,1)} %get-tuple-element.236.refs_3_.refs_11_, ...), custom_call_target="tpu_custom_call" | custom-call | flops 2147483648 | bytes 4194304 | tf_op jit(solution)/shard_map/weight_grads/pallas_call | solution.py:927
  207.6 10.6 %collective-permute-done.16.refs_5_ = bf16[128,1024]{1,0:T(8,128)(2,1)S(1)} collective-permute-done((bf16[128,1024]{1,0:T(8,128)(2,1)}, bf16[128,1024]{1,0:T(8,128)(2,1)S(1)}, u32[]{:S(2)}, u32[]{:S(2)}) %collective-permute-start.16) | collective-permute-done | bytes 262176 | tf_op jit(solution)/shard_map/ppermute | solution.py:1008
  226.7 19.3 %rotate.3 = (bf16[256,1536]{1,0:T(8,128)(2,1)}, bf16[256,1536]{1,0:T(8,128)(2,1)}, bf16[256,1536]{1,0:T(8,128)(2,1)}, bf16[256,1536]{1,0:T(8,128)(2,1)}, bf16[25...) custom-call(s32[17]{0:T(128)} %pad_add_fusion.1.who, f32[2,6,512,512]{3,2,1,0:T(8,128)} %basis.7, ...), custom_call_target="tpu_custom_call" | custom-call | flops 25769803776 | bytes 25165824 | tf_op jit(solution)/shard_map/rotate/pallas_call | solution.py:986
  261.2 3.4 adam.2
  267.9 7.6 %collective-permute-done.47 = bf16[32,1024]{1,0:T(8,128)(2,1)S(1)} collective-permute-done((bf16[32,1024]{1,0:T(8,128)(2,1)}, bf16[32,1024]{1,0:T(8,128)(2,1)S(1)}, u32[]{:S(2)}, u32[]{:S(2)}) %collective-permute-start.47) | collective-permute-done | bytes 65568 | tf_op jit(solution)/shard_map/ppermute | solution.py:955
  277.8 6.2 %collective-permute-done.44 = bf16[32,1536]{1,0:T(8,128)(2,1)S(1)} collective-permute-done((bf16[32,1536]{1,0:T(8,128)(2,1)}, bf16[32,1536]{1,0:T(8,128)(2,1)S(1)}, u32[]{:S(2)}, u32[]{:S(2)}) %collective-permute-start.44) | collective-permute-done | bytes 98336 | tf_op jit(solution)/shard_map/ppermute | solution.py:955
  285.0 5.6 %collective-permute-done.41 = bf16[32,1536]{1,0:T(8,128)(2,1)S(1)} collective-permute-done((bf16[32,1536]{1,0:T(8,128)(2,1)}, bf16[32,1536]{1,0:T(8,128)(2,1)S(1)}, u32[]{:S(2)}, u32[]{:S(2)}) %collective-permute-start.41) | collective-permute-done | bytes 98336 | tf_op jit(solution)/shard_map/ppermute | solution.py:955
  295.1 3.5 combine.8
  303.2 5.2 %collective-permute-done.27.refs_7_ = f32[32,128]{1,0:T(8,128)S(1)} collective-permute-done((f32[32,128]{1,0:T(8,128)}, f32[32,128]{1,0:T(8,128)S(1)}, u32[]{:S(2)}, u32[]{:S(2)}) %collective-permute-start.27) | collective-permute-done | bytes 16416 | tf_op jit(solution)/shard_map/ppermute | solution.py:1240
  311.1 3.9 collective-permute-done.26.refs_5_
  326.2 7.0 %collective-permute-done.28.refs_1_ = bf16[64,1536]{1,0:T(8,128)(2,1)S(1)} collective-permute-done((bf16[64,1536]{1,0:T(8,128)(2,1)}, bf16[64,1536]{1,0:T(8,128)(2,1)S(1)}, u32[]{:S(2)}, u32[]{:S(2)}) %collective-permute-start.28) | collective-permute-done | bytes 196640 | tf_op jit(solution)/shard_map/ppermute | solution.py:1008
  341.1 3.1 collective-permute-start.34
  348.4 3.7 collective-permute-start.50
  352.9 3.4 adam.3
  362.2 2.8 collective-permute-done.59
  366.0 4.5 %collective-permute-start.60 = (bf16[64,1024]{1,0:T(8,128)(2,1)S(1)}, bf16[64,1024]{1,0:T(8,128)(2,1)S(1)}, u32[]{:S(2)}, u32[]{:S(2)}) collective-permute-start(bf16[64,1024]{1,0:T(8,128)(2,1)S(1)} %pad_maximum_fusion.5), channel_id=1, source_target_pairs={{0,2},{2,0},{4,6},{6,4},{8,10},{10,8},{12,14},{14,12},{16,18},{18,... | collective-permute-start | bytes 393224 | tf_op jit(solution)/shard_map/ppermute | solution.py:955
  383.1 16.0 %apply_moves.2 = (f32[2,2,512,1024]{3,2,1,0:T(8,128)}, f32[2,4,512,512]{3,2,1,0:T(8,128)}) custom-call(s32[17]{0:T(128)} %pad_add_fusion.1.who, f32[2,6,512,512]{3,2,1,0:T(8,128)} %basis.7, f32[2,2,8,128,128]{4,3,2,1,0:T(8,128)} %refs_0_.9, f32[2,4,4,128,128]{4,3,2,1,0:T(8,128)} %refs_1_.9, f32[2,2,512,1024]{3,2,1,0:T(8,128)} %refs_2_.7, ...), custom_call_target="tpu_custom_call" | custom-call | flops 8589934592 | bytes 25165824 | tf_op jit(solution)/shard_map/apply_moves/pallas_call | solution.py:1106
  407.4 5.5 %collective-permute-done.65 = f32[32,128]{1,0:T(8,128)S(1)} collective-permute-done((f32[32,128]{1,0:T(8,128)S(1)}, f32[32,128]{1,0:T(8,128)S(1)}, u32[]{:S(2)}, u32[]{:S(2)}) %collective-permute-start.65) | collective-permute-done | bytes 16416 | tf_op jit(solution)/shard_map/ppermute | solution.py:1240
  416.2 16.0 %apply_moves.3 = (f32[2,2,512,1024]{3,2,1,0:T(8,128)}, f32[2,4,512,512]{3,2,1,0:T(8,128)}) custom-call(s32[17]{0:T(128)} %pad_add_fusion.1.who, f32[2,6,512,512]{3,2,1,0:T(8,128)} %basis.7, f32[2,2,8,128,128]{4,3,2,1,0:T(8,128)} %refs_0_.9, f32[2,4,4,128,128]{4,3,2,1,0:T(8,128)} %refs_1_.9, ...), custom_call_target="tpu_custom_call", output_to_operand_aliasing={{0}: (12, {}), {1}: (13, {})} | custom-call | flops 8589934592 | bytes 25165824 | tf_op jit(solution)/shard_map/apply_moves/pallas_call | solution.py:1106
  (292 shorter events, 124.1 us)
Async XLA Ops:
  12.7 23.7 %collective-permute-start.4 = (bf16[4,512,512]{2,1,0:T(8,128)(2,1)}, bf16[4,512,512]{2,1,0:T(8,128)(2,1)}, u32[]{:S(2)}, u32[]{:S(2)}) collective-permute-start(bf16[4,512,512]{2,1,0:T(8,128)(2,1)} %get-tuple-element.173.refs_4_.refs_0_.refs_15_), channel_id=1, source_target_pairs={{1,0},{0,1},{3,2},{2,3},{5,4},{4,5},{7,6},{6,7},{9,8},{8,9},{11,10... | collective-permute-start | bytes 6291464 | tf_op jit(solution)/shard_map/ppermute | solution.py:746
  12.8 23.6 %collective-permute-start.3 = (bf16[2,512,1024]{2,1,0:T(8,128)(2,1)}, bf16[2,512,1024]{2,1,0:T(8,128)(2,1)}, u32[]{:S(2)}, u32[]{:S(2)}) collective-permute-start(bf16[2,512,1024]{2,1,0:T(8,128)(2,1)} %get-tuple-element.172.refs_2_.refs_17_), channel_id=1, source_target_pairs={{1,0},{0,1},{3,2},{2,3},{5,4},{4,5},{7,6},{6,7},{9,8},{8,9},{11,10... | collective-permute-start | bytes 6291464 | tf_op jit(solution)/shard_map/ppermute | solution.py:746
  13.3 57.9 %collective-permute-start.6 = (bf16[2,512,1024]{2,1,0:T(8,128)(2,1)}, bf16[2,512,1024]{2,1,0:T(8,128)(2,1)}, u32[]{:S(2)}, u32[]{:S(2)}) collective-permute-start(bf16[2,512,1024]{2,1,0:T(8,128)(2,1)} %get-tuple-element.180.refs_2_), channel_id=1, source_target_pairs={{1,0},{0,1},{3,2},{2,3},{5,4},{4,5},{7,6},{6,7},{9,8},{8,9},{11,10... | collective-permute-start | bytes 6291464 | tf_op jit(solution)/shard_map/ppermute | solution.py:746
  107.5 31.4 %collective-permute-start.7 = (bf16[2,512,1024]{2,1,0:T(8,128)(2,1)}, bf16[2,512,1024]{2,1,0:T(8,128)(2,1)S(1)}, u32[]{:S(2)}, u32[]{:S(2)}) collective-permute-start(bf16[2,512,1024]{2,1,0:T(8,128)(2,1)} %weight_grads.4), channel_id=1, source_target_pairs={{0,1},{1,0},{2,3},{3,2},{4,5},{5,4},{6,7},{7,6},{8,9},{9,8},{10,11... | collective-permute-start | bytes 6291464 | tf_op jit(solution)/shard_map/ppermute | solution.py:942
  162.1 26.7 %collective-permute-start.11 = (bf16[256,1536]{1,0:T(8,128)(2,1)}, bf16[256,1536]{1,0:T(8,128)(2,1)S(1)}, u32[]{:S(2)}, u32[]{:S(2)}) collective-permute-start(bf16[256,1536]{1,0:T(8,128)(2,1)} %get-tuple-element.218), channel_id=1, source_target_pairs={{0,2},{2,0},{4,6},{6,4},{8,10},{10,8},{12,14},{14,12},{16,18},{18,... | collective-permute-start | bytes 2359304 | tf_op jit(solution)/shard_map/ppermute | solution.py:1008
  164.8 24.0 %collective-permute-start.12 = (bf16[256,1536]{1,0:T(8,128)(2,1)}, bf16[256,1536]{1,0:T(8,128)(2,1)S(1)}, u32[]{:S(2)}, u32[]{:S(2)}) collective-permute-start(bf16[256,1536]{1,0:T(8,128)(2,1)} %get-tuple-element.220), channel_id=1, source_target_pairs={{0,4},{2,6},{4,0},{6,2},{8,12},{10,14},{12,8},{14,10},{16,20},{18,... | collective-permute-start | bytes 2359304 | tf_op jit(solution)/shard_map/ppermute | solution.py:1008
  166.3 22.4 %collective-permute-start.13 = (bf16[256,1024]{1,0:T(8,128)(2,1)}, bf16[256,1024]{1,0:T(8,128)(2,1)S(1)}, u32[]{:S(2)}, u32[]{:S(2)}) collective-permute-start(bf16[256,1024]{1,0:T(8,128)(2,1)} %get-tuple-element.222), channel_id=1, source_target_pairs={{0,8},{2,10},{4,12},{6,14},{8,0},{10,2},{12,4},{14,6},{16,24},{18,... | collective-permute-start | bytes 1572872 | tf_op jit(solution)/shard_map/ppermute | solution.py:1008
  174.4 49.4 %collective-permute-start.17 = (bf16[2,512,1024]{2,1,0:T(8,128)(2,1)}, bf16[2,512,1024]{2,1,0:T(8,128)(2,1)}, u32[]{:S(2)}, u32[]{:S(2)}) collective-permute-start(bf16[2,512,1024]{2,1,0:T(8,128)(2,1)} %weight_grads.6), channel_id=1, source_target_pairs={{0,1},{1,0},{2,3},{3,2},{4,5},{5,4},{6,7},{7,6},{8,9},{9,8},{10,11... | collective-permute-start | bytes 6291464 | tf_op jit(solution)/shard_map/ppermute | solution.py:942
  199.4 25.9 %collective-permute-start.18 = (bf16[4,512,512]{2,1,0:T(8,128)(2,1)}, bf16[4,512,512]{2,1,0:T(8,128)(2,1)S(1)}, u32[]{:S(2)}, u32[]{:S(2)}) collective-permute-start(bf16[4,512,512]{2,1,0:T(8,128)(2,1)} %weight_grads.7), channel_id=1, source_target_pairs={{0,1},{1,0},{2,3},{3,2},{4,5},{5,4},{6,7},{7,6},{8,9},{9,8},{10,11... | collective-permute-start | bytes 6291464 | tf_op jit(solution)/shard_map/ppermute | solution.py:942
  200.3 18.0 %collective-permute-start.14 = (bf16[128,1536]{1,0:T(8,128)(2,1)}, bf16[128,1536]{1,0:T(8,128)(2,1)S(1)}, u32[]{:S(2)}, u32[]{:S(2)}) collective-permute-start(bf16[128,1536]{1,0:T(8,128)(2,1)} %get-tuple-element.224), channel_id=1, source_target_pairs={{0,4},{2,6},{4,0},{6,2},{8,12},{10,14},{12,8},{14,10},{16,20},{18,... | collective-permute-start | bytes 1179656 | tf_op jit(solution)/shard_map/ppermute | solution.py:1008
  200.9 17.4 %collective-permute-start.15 = (bf16[128,1536]{1,0:T(8,128)(2,1)}, bf16[128,1536]{1,0:T(8,128)(2,1)S(1)}, u32[]{:S(2)}, u32[]{:S(2)}) collective-permute-start(bf16[128,1536]{1,0:T(8,128)(2,1)} %get-tuple-element.226), channel_id=1, source_target_pairs={{0,2},{2,0},{4,6},{6,4},{8,10},{10,8},{12,14},{14,12},{16,18},{18,... | collective-permute-start | bytes 1179656 | tf_op jit(solution)/shard_map/ppermute | solution.py:1008
  203.6 14.7 %collective-permute-start.16 = (bf16[128,1024]{1,0:T(8,128)(2,1)}, bf16[128,1024]{1,0:T(8,128)(2,1)S(1)}, u32[]{:S(2)}, u32[]{:S(2)}) collective-permute-start(bf16[128,1024]{1,0:T(8,128)(2,1)} %get-tuple-element.228), channel_id=1, source_target_pairs={{0,16},{2,18},{4,20},{6,22},{8,24},{10,26},{12,28},{14,30},{16,0},... | collective-permute-start | bytes 786440 | tf_op jit(solution)/shard_map/ppermute | solution.py:1008
  218.3 35.0 %collective-permute-start.22 = (f32[32,128]{1,0:T(8,128)S(1)}, f32[32,128]{1,0:T(8,128)S(1)}, u32[]{:S(2)}, u32[]{:S(2)}) collective-permute-start(f32[32,128]{1,0:T(8,128)S(1)} %pad_maximum_fusion.6), channel_id=1, source_target_pairs={{0,1},{1,0},{2,3},{3,2},{4,5},{5,4},{6,7},{7,6},{8,9},{9,8},{10,11... | collective-permute-start | bytes 49160 | tf_op jit(solution)/shard_map/ppermute | solution.py:1237
  221.7 24.3 %collective-permute-start.35 = (bf16[64,1536]{1,0:T(8,128)(2,1)}, bf16[64,1536]{1,0:T(8,128)(2,1)S(1)}, u32[]{:S(2)}, u32[]{:S(2)}) collective-permute-start(bf16[64,1536]{1,0:T(8,128)(2,1)} %get-tuple-element.273), channel_id=1, source_target_pairs={{0,8},{2,10},{4,12},{6,14},{8,0},{10,2},{12,4},{14,6},{16,24},{18,... | collective-permute-start | bytes 589832 | tf_op jit(solution)/shard_map/ppermute | solution.py:1008
  221.8 24.2 %collective-permute-start.36 = (bf16[64,1536]{1,0:T(8,128)(2,1)}, bf16[64,1536]{1,0:T(8,128)(2,1)S(1)}, u32[]{:S(2)}, u32[]{:S(2)}) collective-permute-start(bf16[64,1536]{1,0:T(8,128)(2,1)} %get-tuple-element.275), channel_id=1, source_target_pairs={{0,8},{2,10},{4,12},{6,14},{8,0},{10,2},{12,4},{14,6},{16,24},{18,... | collective-permute-start | bytes 589832 | tf_op jit(solution)/shard_map/ppermute | solution.py:1008
  223.8 22.2 %collective-permute-start.37 = (bf16[64,1024]{1,0:T(8,128)(2,1)}, bf16[64,1024]{1,0:T(8,128)(2,1)S(1)}, u32[]{:S(2)}, u32[]{:S(2)}) collective-permute-start(bf16[64,1024]{1,0:T(8,128)(2,1)} %get-tuple-element.277), channel_id=1, source_target_pairs={{0,2},{2,0},{4,6},{6,4},{8,10},{10,8},{12,14},{14,12},{16,18},{18,... | collective-permute-start | bytes 393224 | tf_op jit(solution)/shard_map/ppermute | solution.py:1008
  253.3 38.4 %collective-permute-start.23 = (f32[32,128]{1,0:T(8,128)S(1)}, f32[32,128]{1,0:T(8,128)S(1)}, u32[]{:S(2)}, u32[]{:S(2)}) collective-permute-start(f32[32,128]{1,0:T(8,128)S(1)} %fusion.refs_6_), channel_id=1, source_target_pairs={{0,2},{2,0},{4,6},{6,4},{8,10},{10,8},{12,14},{14,12},{16,18},{18,... | collective-permute-start | bytes 49160 | tf_op jit(solution)/shard_map/ppermute | solution.py:1240
  253.9 40.1 %collective-permute-start.19 = (bf16[256,1536]{1,0:T(8,128)(2,1)}, bf16[256,1536]{1,0:T(8,128)(2,1)S(1)}, u32[]{:S(2)}, u32[]{:S(2)}) collective-permute-start(bf16[256,1536]{1,0:T(8,128)(2,1)} %get-tuple-element.240), channel_id=1, source_target_pairs={{0,2},{2,0},{4,6},{6,4},{8,10},{10,8},{12,14},{14,12},{16,18},{18,... | collective-permute-start | bytes 2359304 | tf_op jit(solution)/shard_map/ppermute | solution.py:1008
  256.2 37.8 %collective-permute-start.20 = (bf16[256,1536]{1,0:T(8,128)(2,1)}, bf16[256,1536]{1,0:T(8,128)(2,1)S(1)}, u32[]{:S(2)}, u32[]{:S(2)}) collective-permute-start(bf16[256,1536]{1,0:T(8,128)(2,1)} %get-tuple-element.242), channel_id=1, source_target_pairs={{0,4},{2,6},{4,0},{6,2},{8,12},{10,14},{12,8},{14,10},{16,20},{18,... | collective-permute-start | bytes 2359304 | tf_op jit(solution)/shard_map/ppermute | solution.py:1008
  258.5 33.8 %collective-permute-start.21 = (bf16[256,1024]{1,0:T(8,128)(2,1)}, bf16[256,1024]{1,0:T(8,128)(2,1)S(1)}, u32[]{:S(2)}, u32[]{:S(2)}) collective-permute-start(bf16[256,1024]{1,0:T(8,128)(2,1)} %get-tuple-element.244), channel_id=1, source_target_pairs={{0,8},{2,10},{4,12},{6,14},{8,0},{10,2},{12,4},{14,6},{16,24},{18,... | collective-permute-start | bytes 1572872 | tf_op jit(solution)/shard_map/ppermute | solution.py:1008
  291.7 26.8 %collective-permute-start.48 = (bf16[64,1024]{1,0:T(8,128)(2,1)S(1)}, bf16[64,1024]{1,0:T(8,128)(2,1)}, u32[]{:S(2)}, u32[]{:S(2)}) collective-permute-start(bf16[64,1024]{1,0:T(8,128)(2,1)S(1)} %pad_maximum_fusion.4), channel_id=1, source_target_pairs={{0,2},{2,0},{4,6},{6,4},{8,10},{10,8},{12,14},{14,12},{16,18},{18,... | collective-permute-start | bytes 393224 | tf_op jit(solution)/shard_map/ppermute | solution.py:955
  298.6 16.3 %collective-permute-start.24 = (bf16[128,1536]{1,0:T(8,128)(2,1)}, bf16[128,1536]{1,0:T(8,128)(2,1)S(1)}, u32[]{:S(2)}, u32[]{:S(2)}) collective-permute-start(bf16[128,1536]{1,0:T(8,128)(2,1)} %get-tuple-element.254), channel_id=1, source_target_pairs={{0,4},{2,6},{4,0},{6,2},{8,12},{10,14},{12,8},{14,10},{16,20},{18,... | collective-permute-start | bytes 1179656 | tf_op jit(solution)/shard_map/ppermute | solution.py:1008
  300.4 14.5 %collective-permute-start.25 = (bf16[128,1536]{1,0:T(8,128)(2,1)}, bf16[128,1536]{1,0:T(8,128)(2,1)S(1)}, u32[]{:S(2)}, u32[]{:S(2)}) collective-permute-start(bf16[128,1536]{1,0:T(8,128)(2,1)} %get-tuple-element.256), channel_id=1, source_target_pairs={{0,2},{2,0},{4,6},{6,4},{8,10},{10,8},{12,14},{14,12},{16,18},{18,... | collective-permute-start | bytes 1179656 | tf_op jit(solution)/shard_map/ppermute | solution.py:1008
  308.4 35.8 %collective-permute-start.46 = (bf16[128,1536]{1,0:T(8,128)(2,1)S(1)}, bf16[128,1536]{1,0:T(8,128)(2,1)S(1)}, u32[]{:S(2)}, u32[]{:S(2)}) collective-permute-start(bf16[128,1536]{1,0:T(8,128)(2,1)S(1)} %constant_dynamic-update-slice_fusion.5.refs_2_), channel_id=1, source_target_pairs={{0,2},{2,0},{4,6},{6,4},{8,10},{10,8},{12,14},{14,12},{16,18},{18,... | collective-permute-start | bytes 1179656 | tf_op jit(solution)/shard_map/ppermute | solution.py:955
  314.9 29.3 %collective-permute-start.43 = (bf16[128,1536]{1,0:T(8,128)(2,1)S(1)}, bf16[128,1536]{1,0:T(8,128)(2,1)S(1)}, u32[]{:S(2)}, u32[]{:S(2)}) collective-permute-start(bf16[128,1536]{1,0:T(8,128)(2,1)S(1)} %constant_dynamic-update-slice_fusion.2.refs_0_), channel_id=1, source_target_pairs={{0,4},{2,6},{4,0},{6,2},{8,12},{10,14},{12,8},{14,10},{16,20},{18,... | collective-permute-start | bytes 1179656 | tf_op jit(solution)/shard_map/ppermute | solution.py:955
  319.4 21.6 %collective-permute-start.49 = (bf16[128,1024]{1,0:T(8,128)(2,1)S(1)}, bf16[128,1024]{1,0:T(8,128)(2,1)S(1)}, u32[]{:S(2)}, u32[]{:S(2)}) collective-permute-start(bf16[128,1024]{1,0:T(8,128)(2,1)S(1)} %constant_dynamic-update-slice_fusion.8.refs_4_), channel_id=1, source_target_pairs={{0,16},{2,18},{4,20},{6,22},{8,24},{10,26},{12,28},{14,30},{16,0},... | collective-permute-start | bytes 786440 | tf_op jit(solution)/shard_map/ppermute | solution.py:955
  348.4 32.8 %collective-permute-start.50 = (bf16[256,1536]{1,0:T(8,128)(2,1)}, bf16[256,1536]{1,0:T(8,128)(2,1)S(1)}, u32[]{:S(2)}, u32[]{:S(2)}) collective-permute-start(bf16[256,1536]{1,0:T(8,128)(2,1)} %get-tuple-element.298.refs_4_), channel_id=1, source_target_pairs={{0,2},{2,0},{4,6},{6,4},{8,10},{10,8},{12,14},{14,12},{16,18},{18,... | collective-permute-start | bytes 2359304 | tf_op jit(solution)/shard_map/ppermute | solution.py:955
  352.1 29.1 %collective-permute-start.51 = (bf16[256,1536]{1,0:T(8,128)(2,1)}, bf16[256,1536]{1,0:T(8,128)(2,1)S(1)}, u32[]{:S(2)}, u32[]{:S(2)}) collective-permute-start(bf16[256,1536]{1,0:T(8,128)(2,1)} %get-tuple-element.299.refs_6_), channel_id=1, source_target_pairs={{0,4},{2,6},{4,0},{6,2},{8,12},{10,14},{12,8},{14,10},{16,20},{18,... | collective-permute-start | bytes 2359304 | tf_op jit(solution)/shard_map/ppermute | solution.py:955
  352.2 28.9 %collective-permute-start.52 = (bf16[256,1024]{1,0:T(8,128)(2,1)}, bf16[256,1024]{1,0:T(8,128)(2,1)S(1)}, u32[]{:S(2)}, u32[]{:S(2)}) collective-permute-start(bf16[256,1024]{1,0:T(8,128)(2,1)} %get-tuple-element.300.refs_8_), channel_id=1, source_target_pairs={{0,8},{2,10},{4,12},{6,14},{8,0},{10,2},{12,4},{14,6},{16,24},{18,... | collective-permute-start | bytes 1572872 | tf_op jit(solution)/shard_map/ppermute | solution.py:955
  377.1 22.0 %collective-permute-start.61 = (bf16[128,1024]{1,0:T(8,128)(2,1)S(1)}, bf16[128,1024]{1,0:T(8,128)(2,1)}, u32[]{:S(2)}, u32[]{:S(2)}) collective-permute-start(bf16[128,1024]{1,0:T(8,128)(2,1)S(1)} %constant_dynamic-update-slice_fusion.17.refs_5_), channel_id=1, source_target_pairs={{0,16},{2,18},{4,20},{6,22},{8,24},{10,26},{12,28},{14,30},{16,0},... | collective-permute-start | bytes 786440 | tf_op jit(solution)/shard_map/ppermute | solution.py:955
  379.2 19.9 %collective-permute-start.58 = (bf16[128,1536]{1,0:T(8,128)(2,1)S(1)}, bf16[128,1536]{1,0:T(8,128)(2,1)S(1)}, u32[]{:S(2)}, u32[]{:S(2)}) collective-permute-start(bf16[128,1536]{1,0:T(8,128)(2,1)S(1)} %constant_dynamic-update-slice_fusion.14.refs_3_), channel_id=1, source_target_pairs={{0,2},{2,0},{4,6},{6,4},{8,10},{10,8},{12,14},{14,12},{16,18},{18,... | collective-permute-start | bytes 1179656 | tf_op jit(solution)/shard_map/ppermute | solution.py:955
  381.1 18.0 %collective-permute-start.55 = (bf16[128,1536]{1,0:T(8,128)(2,1)S(1)}, bf16[128,1536]{1,0:T(8,128)(2,1)S(1)}, u32[]{:S(2)}, u32[]{:S(2)}) collective-permute-start(bf16[128,1536]{1,0:T(8,128)(2,1)S(1)} %constant_dynamic-update-slice_fusion.11.refs_1_), channel_id=1, source_target_pairs={{0,4},{2,6},{4,0},{6,2},{8,12},{10,14},{12,8},{14,10},{16,20},{18,... | collective-permute-start | bytes 1179656 | tf_op jit(solution)/shard_map/ppermute | solution.py:955
  (97 other events, 717.2 us)

commit v5 on v4

--- a/solution.py
+++ b/solution.py
@@ -1202,19 +1202,16 @@
             after = (pieces[0][0],)
             held = scatter_stage(plan, pieces, 1)
         hid_recv = send_parts(hid_pairs, (nin, dout), (dkf, dki, dkc, hlow), part_h, after)
-        after = ()
-        if held is not None:
-            pieces = combine(plan, held, 1)
-            after = (pieces[0][0],)
-            held = scatter_stage(plan, pieces, 2)
+        early = after
         pieces = rotate(
             plan, l, all_pairs, (nmid, dz, nin, dout), (dpre, act, dkf, dki, dkc, hlow),
-            (mlp_recv, hid_recv), all_blocks, after,
+            (mlp_recv, hid_recv), all_blocks, early,
         )
         previous, held = held, scatter_stage(plan, pieces, 0)
         gates_after = (pieces[0][0],)
         if previous is not None:
-            previous = scatter_stage(plan, combine(plan, previous, 2, gates_after), 3)
+            previous = scatter_stage(plan, combine(plan, previous, 1, gates_after), 2)
+            previous = scatter_stage(plan, combine(plan, previous, 2), 3)
             done = finish(l + 1, previous, done)
         small.append((sums_in, sums_mid, bsum))
         dz, dpre, dout, sums_mid = dz_next, dpre_next, dout_next, sums_next

time: 439 us -> 431 us (0.982)
  starting transfers between devices: 68.5 us -> 60.4 us
    ppermute x24, starting transfers between devices: 27.1 us -> 19.6 us  [exchange(): lax.ppermute(value, 'dp', [(i, i ^ r << low) for i in range(dp_count)])]
    ppermute x24, waiting for transfers between devices: 27.3 us -> 19.9 us  [scatter_stage(): lax.ppermute(mine[r], 'dp', [(i, i ^ r << low) for i in range(dp_count)])]
    ppermute x24, waiting for transfers between devices: 29.1 us -> 34 us  [exchange(): lax.ppermute(value, 'dp', [(i, i ^ r << low) for i in range(dp_count)])]
    unnamed x137 -> x141, local copies, waits for them, and re-layouts: 20.9 us -> 20.7 us
  transfers between devices with their start and end apart: 66 -> 66, of which waited for: 24 -> 27; matrix products, arithmetic and copies ran while one was open for 4% -> 4% of each run, Pallas kernels for 42% -> 42%
where the time goes in v5:
time: 431 us; the launch traced here: 425 us
  Pallas kernels  252 us (58%)
  waiting for transfers between devices  77.4 us (18%)
  starting transfers between devices  60.4 us (14%)
  local copies, waits for them, and re-layouts  24.4 us (6%)
  other arithmetic  7.81 us (2%)
    pallas_call x2, Pallas kernels, rotate(): pl.pallas_call(functools.partial(k_rotate, plan, mp - 1, pairs, len(after...  39.2 us
    ppermute x24, starting transfers between devices, scatter_stage(): lax.ppermute(mine[r], 'dp', [(i, i ^ r << low) for i in range(dp_count)])  34 us
    ppermute x24, waiting for transfers between devices, exchange(): lax.ppermute(value, 'dp', [(i, i ^ r << low) for i in range(dp_count)])  34 us
    pallas_call x1, Pallas kernels, per_device(): pl.pallas_call(functools.partial(k_middle, mp), grid=(grid,), in_specs=[s...  33.3 us
    pallas_call x2, Pallas kernels, apply_moves(): pl.pallas_call(functools.partial(k_apply, plan, len(before)), grid=(plan....  31.9 us
    pallas_call x1, Pallas kernels, per_device(): pl.pallas_call(functools.partial(k_turn, mp), grid=(grid,), in_specs=[sme...  27.7 us
    pallas_call x4, Pallas kernels, weight_grads(): pl.pallas_call(functools.partial(k_grads, shifted, len(after)), grid=(per...  25.2 us
    pallas_call x1, Pallas kernels, per_device(): pl.pallas_call(functools.partial(k_return, mp), grid=(grid,), in_specs=[s...  23.6 us
  transfers between devices with their start and end apart: 66, of which 27 were waited for; matrix products, arithmetic and copies ran while one was open for 4% of the time, Pallas kernels for 42%

profile of v5, /device:TPU:0, one launch (start us, length us, event | category | flops | bytes accessed | tf_op | source)
XLA Modules:
  0.0 424.8 jit_solution(16612705551256368375)
XLA Ops:
  0.7 4.3 %cast.2.refs_0_.refs_19_.refs_16_ = bf16[4,512,512]{2,1,0:T(8,128)(2,1)} custom-call(f32[2,4,512,512]{3,2,1,0:T(8,128)} %refs_3_.3), custom_call_target="tpu_custom_call" | custom-call | bytes 6291456 | tf_op jit(solution)/shard_map/cast/pallas_call | solution.py:764
  5.4 7.4 %cast.3 = (bf16[2,512,1024]{2,1,0:T(8,128)(2,1)}, bf16[4,512,512]{2,1,0:T(8,128)(2,1)}, bf16[2,512,1024]{2,1,0:T(8,128)(2,1)}) custom-call(f32[2,2,512,1024]{3,2,1,0:T(8,128)} %refs_2_.7, f32[2,4,512,512]{3,2,1,0:T(8,128)} %refs_3_.3, f32[2,2,512,1024]{3,2,1,0:T(8,128)} %refs_2_.7), custom_call_target="tpu_custom_call" | custom-call | bytes 18874368 | tf_op jit(solution)/shard_map/cast/pallas_call | solution.py:764
  18.9 16.8 %gates_first.1 = (f32[1024,512]{1,0:T(8,128)}, bf16[1024,512]{1,0:T(8,128)(2,1)}, bf16[1024,1024]{1,0:T(8,128)(2,1)}, bf16[1024,1024]{1,0:T(8,128)(2,1)}, bf16[1...) custom-call(bf16[8,128,512]{2,1,0:T(8,128)(2,1)} %bitcast.19, ...), custom_call_target="tpu_custom_call" | custom-call | flops 3221225472 | bytes 25165824 | tf_op jit(solution)/shard_map/gates_first/pallas_call | solution.py:855
  37.7 33.3 %block_forward.1 = (bf16[1024,1024]{1,0:T(8,128)(2,1)}, f32[8,1024]{1,0:T(8,128)}, f32[1024,512]{1,0:T(8,128)}, bf16[1024,512]{1,0:T(8,128)(2,1)}, bf16[1024,204...) custom-call(s32[3]{0:T(128)} %pad_add_fusion.info.refs_1_, ...), custom_call_target="tpu_custom_call" | custom-call | flops 8589934592 | bytes 62914560 | tf_op jit(solution)/shard_map/block_forward/pallas_call | solution.py:871
  73.0 27.7 %block_turn.1 = (bf16[1024,1024]{1,0:T(8,128)(2,1)}, f32[8,1024]{1,0:T(8,128)}, bf16[1024,512]{1,0:T(8,128)(2,1)}, bf16[1024,2048]{1,0:T(8,128)(2,1)}, f32[8,128...) custom-call(s32[3]{0:T(128)} %pad_add_fusion.info.refs_1_, ...), custom_call_target="tpu_custom_call" | custom-call | flops 10737418240 | bytes 62914560 | tf_op jit(solution)/shard_map/block_turn/pallas_call | solution.py:897
  101.0 6.5 %weight_grads.4 = bf16[2,512,1024]{2,1,0:T(8,128)(2,1)} custom-call(bf16[1024,512]{1,0:T(8,128)(2,1)} %get-tuple-element.182.refs_0_.refs_4_, bf16[1024,512]{1,0:T(8,128)(2,1)} %get-tuple-element.183.refs_1_.refs_5_, bf16[1024,2048]{1,0:T(8,128)(2,1)} %get-tuple-element.184.refs_2_.refs_8_, bf16[1024,2048]{1,0:T(8,128)(2,1)} %get-tuple-element.185.refs_3_.refs_9_), custom_call_target="tpu_custom_call" | custom-call | flops 2147483648 | bytes 4194304 | tf_op jit(solution)/shard_map/weight_grads/pallas_call | solution.py:927
  108.4 23.6 %block_return.1 = (bf16[1024,1024]{1,0:T(8,128)(2,1)}, bf16[1024,1024]{1,0:T(8,128)(2,1)}, bf16[1024,1024]{1,0:T(8,128)(2,1)}, bf16[1024,512]{1,0:T(8,128)(2,1)}...) custom-call(s32[3]{0:T(128)} %pad_add_fusion.info.refs_1_, ...), custom_call_target="tpu_custom_call" | custom-call | flops 8589934592 | bytes 62914560 | tf_op jit(solution)/shard_map/block_return/pallas_call | solution.py:1155
  132.1 6.0 %weight_grads.5 = bf16[4,512,512]{2,1,0:T(8,128)(2,1)} custom-call(bf16[1024,512]{1,0:T(8,128)(2,1)} %get-tuple-element.186.refs_0_.refs_6_, bf16[1024,512]{1,0:T(8,128)(2,1)} %get-tuple-element.187.refs_1_.refs_7_, bf16[1024,1024]{1,0:T(8,128)(2,1)} %get-tuple-element.202.refs_2_.refs_10_, bf16[1024,1024]{1,0:T(8,128)(2,1)} %get-tuple-element.203.refs_3_.refs_11_, ...), custom_call_target="tpu_custom_call" | custom-call | flops 2147483648 | bytes 4194304 | tf_op jit(solution)/shard_map/weight_grads/pallas_call | solution.py:927
  138.9 3.7 collective-permute-done.9.refs_3_
  142.6 19.5 %rotate.2 = (bf16[256,1536]{1,0:T(8,128)(2,1)}, bf16[256,1536]{1,0:T(8,128)(2,1)}, bf16[256,1536]{1,0:T(8,128)(2,1)}, bf16[256,1536]{1,0:T(8,128)(2,1)}, bf16[25...) custom-call(s32[17]{0:T(128)} %pad_add_fusion.1.who, f32[2,6,512,512]{3,2,1,0:T(8,128)} %basis.7, ...), custom_call_target="tpu_custom_call" | custom-call | flops 25769803776 | bytes 25165824 | tf_op jit(solution)/shard_map/rotate/pallas_call | solution.py:986
  168.0 6.5 %weight_grads.6 = bf16[2,512,1024]{2,1,0:T(8,128)(2,1)} custom-call(bf16[256,1536]{1,0:T(8,128)(2,1)} %get-tuple-element.205.refs_0_, bf16[1024,512]{1,0:T(8,128)(2,1)} %get-tuple-element.224.refs_1_.refs_5_, bf16[1024,512]{1,0:T(8,128)(2,1)} %get-tuple-element.225.refs_2_.refs_6_, bf16[1024,2048]{1,0:T(8,128)(2,1)} %get-tuple-element.226.refs_3_.refs_9_, ...), custom_call_target="tpu_custom_call" | custom-call | flops 2147483648 | bytes 4194304 | tf_op jit(solution)/shard_map/weight_grads/pallas_call | solution.py:927
  175.6 12.8 %block_last.1 = (bf16[1024,1024]{1,0:T(8,128)(2,1)}, bf16[1024,1024]{1,0:T(8,128)(2,1)}, bf16[1024,1024]{1,0:T(8,128)(2,1)}, f32[8,128,512]{2,1,0:T(8,128)}, f32[8,512]{1,0:T(8,128)}, /*index=5*/f32[2,8,1024]{2,1,0:T(8,128)}) custom-call(bf16[256,1536]{1,0:T(8,128)(2,1)} %get-tuple-element.205.refs_0_, s32[3]{0:T(128)} %pad_add_fusion.info.refs_1_, ...), custom_call_target="tpu_custom_call" | custom-call | flops 3221225472 | bytes 31457280 | tf_op jit(solution)/shard_map/block_last/pallas_call | solution.py:1181
  189.7 3.3 combine.6
  193.0 6.1 %weight_grads.7 = bf16[4,512,512]{2,1,0:T(8,128)(2,1)} custom-call(bf16[128,1536]{1,0:T(8,128)(2,1)} %get-tuple-element.223.refs_0_.refs_1_, bf16[1024,512]{1,0:T(8,128)(2,1)} %get-tuple-element.228.refs_1_.refs_7_, bf16[1024,512]{1,0:T(8,128)(2,1)} %get-tuple-element.229.refs_2_.refs_8_, bf16[1024,1024]{1,0:T(8,128)(2,1)} %get-tuple-element.230.refs_3_.refs_11_, ...), custom_call_target="tpu_custom_call" | custom-call | flops 2147483648 | bytes 4194304 | tf_op jit(solution)/shard_map/weight_grads/pallas_call | solution.py:927
  208.1 19.7 %rotate.3 = (bf16[256,1536]{1,0:T(8,128)(2,1)}, bf16[256,1536]{1,0:T(8,128)(2,1)}, bf16[256,1536]{1,0:T(8,128)(2,1)}, bf16[256,1536]{1,0:T(8,128)(2,1)}, bf16[25...) custom-call(s32[17]{0:T(128)} %pad_add_fusion.1.who, f32[2,6,512,512]{3,2,1,0:T(8,128)} %basis.7, ...), custom_call_target="tpu_custom_call" | custom-call | flops 25769803776 | bytes 25165824 | tf_op jit(solution)/shard_map/rotate/pallas_call | solution.py:986
  235.4 3.1 collective-permute-done.37.refs_5_
  239.3 2.8 collective-permute-done.36.refs_3_
  256.3 3.4 adam.2
  262.9 7.6 %collective-permute-done.47 = bf16[32,1024]{1,0:T(8,128)(2,1)S(1)} collective-permute-done((bf16[32,1024]{1,0:T(8,128)(2,1)}, bf16[32,1024]{1,0:T(8,128)(2,1)S(1)}, u32[]{:S(2)}, u32[]{:S(2)}) %collective-permute-start.47) | collective-permute-done | bytes 65568 | tf_op jit(solution)/shard_map/ppermute | solution.py:955
  271.7 7.3 %collective-permute-done.44 = bf16[32,1536]{1,0:T(8,128)(2,1)S(1)} collective-permute-done((bf16[32,1536]{1,0:T(8,128)(2,1)}, bf16[32,1536]{1,0:T(8,128)(2,1)S(1)}, u32[]{:S(2)}, u32[]{:S(2)}) %collective-permute-start.44) | collective-permute-done | bytes 98336 | tf_op jit(solution)/shard_map/ppermute | solution.py:955
  279.9 5.0 %collective-permute-done.41 = bf16[32,1536]{1,0:T(8,128)(2,1)S(1)} collective-permute-done((bf16[32,1536]{1,0:T(8,128)(2,1)}, bf16[32,1536]{1,0:T(8,128)(2,1)S(1)}, u32[]{:S(2)}, u32[]{:S(2)}) %collective-permute-start.41) | collective-permute-done | bytes 98336 | tf_op jit(solution)/shard_map/ppermute | solution.py:955
  290.5 3.5 combine.7
  297.7 6.1 %collective-permute-done.24.refs_7_ = f32[32,128]{1,0:T(8,128)S(1)} collective-permute-done((f32[32,128]{1,0:T(8,128)}, f32[32,128]{1,0:T(8,128)S(1)}, u32[]{:S(2)}, u32[]{:S(2)}) %collective-permute-start.24) | collective-permute-done | bytes 16416 | tf_op jit(solution)/shard_map/ppermute | solution.py:1237
  310.0 3.9 collective-permute-start.27
  315.0 4.0 collective-permute-done.28.refs_7_
  321.6 5.8 %collective-permute-done.25.refs_1_ = bf16[64,1536]{1,0:T(8,128)(2,1)S(1)} collective-permute-done((bf16[64,1536]{1,0:T(8,128)(2,1)}, bf16[64,1536]{1,0:T(8,128)(2,1)S(1)}, u32[]{:S(2)}, u32[]{:S(2)}) %collective-permute-start.25) | collective-permute-done | bytes 196640 | tf_op jit(solution)/shard_map/ppermute | solution.py:1008
  344.1 3.4 adam.3
  358.5 5.1 %collective-permute-done.53 = bf16[32,1536]{1,0:T(8,128)(2,1)S(1)} collective-permute-done((bf16[32,1536]{1,0:T(8,128)(2,1)}, bf16[32,1536]{1,0:T(8,128)(2,1)S(1)}, u32[]{:S(2)}, u32[]{:S(2)}) %collective-permute-start.53) | collective-permute-done | bytes 98336 | tf_op jit(solution)/shard_map/ppermute | solution.py:955
  375.6 16.0 %apply_moves.2 = (f32[2,2,512,1024]{3,2,1,0:T(8,128)}, f32[2,4,512,512]{3,2,1,0:T(8,128)}) custom-call(s32[17]{0:T(128)} %pad_add_fusion.1.who, f32[2,6,512,512]{3,2,1,0:T(8,128)} %basis.7, f32[2,2,8,128,128]{4,3,2,1,0:T(8,128)} %refs_0_.9, f32[2,4,4,128,128]{4,3,2,1,0:T(8,128)} %refs_1_.9, f32[2,2,512,1024]{3,2,1,0:T(8,128)} %refs_2_.7, ...), custom_call_target="tpu_custom_call" | custom-call | flops 8589934592 | bytes 25165824 | tf_op jit(solution)/shard_map/apply_moves/pallas_call | solution.py:1106
  392.5 2.8 join.3
  399.1 5.9 %collective-permute-done.65 = f32[32,128]{1,0:T(8,128)S(1)} collective-permute-done((f32[32,128]{1,0:T(8,128)S(1)}, f32[32,128]{1,0:T(8,128)S(1)}, u32[]{:S(2)}, u32[]{:S(2)}) %collective-permute-start.65) | collective-permute-done | bytes 16416 | tf_op jit(solution)/shard_map/ppermute | solution.py:1237
  408.7 15.9 %apply_moves.3 = (f32[2,2,512,1024]{3,2,1,0:T(8,128)}, f32[2,4,512,512]{3,2,1,0:T(8,128)}) custom-call(s32[17]{0:T(128)} %pad_add_fusion.1.who, f32[2,6,512,512]{3,2,1,0:T(8,128)} %basis.7, f32[2,2,8,128,128]{4,3,2,1,0:T(8,128)} %refs_0_.9, f32[2,4,4,128,128]{4,3,2,1,0:T(8,128)} %refs_1_.9, ...), custom_call_target="tpu_custom_call", output_to_operand_aliasing={{0}: (12, {}), {1}: (13, {})} | custom-call | flops 8589934592 | bytes 25165824 | tf_op jit(solution)/shard_map/apply_moves/pallas_call | solution.py:1106
  (296 shorter events, 123.0 us)
Async XLA Ops:
  4.9 12.7 %collective-permute-start.1 = (bf16[4,512,512]{2,1,0:T(8,128)(2,1)}, bf16[4,512,512]{2,1,0:T(8,128)(2,1)S(1)}, u32[]{:S(2)}, u32[]{:S(2)}) collective-permute-start(bf16[4,512,512]{2,1,0:T(8,128)(2,1)} %cast.2.refs_0_.refs_19_.refs_16_), channel_id=1, source_target_pairs={{1,0},{0,1},{3,2},{2,3},{5,4},{4,5},{7,6},{6,7},{9,8},{8,9},{11,10... | collective-permute-start | bytes 6291464 | tf_op jit(solution)/shard_map/ppermute | solution.py:746
  12.8 23.7 %collective-permute-start.4 = (bf16[4,512,512]{2,1,0:T(8,128)(2,1)}, bf16[4,512,512]{2,1,0:T(8,128)(2,1)}, u32[]{:S(2)}, u32[]{:S(2)}) collective-permute-start(bf16[4,512,512]{2,1,0:T(8,128)(2,1)} %get-tuple-element.173.refs_4_.refs_0_.refs_15_), channel_id=1, source_target_pairs={{1,0},{0,1},{3,2},{2,3},{5,4},{4,5},{7,6},{6,7},{9,8},{8,9},{11,10... | collective-permute-start | bytes 6291464 | tf_op jit(solution)/shard_map/ppermute | solution.py:746
  12.8 23.6 %collective-permute-start.3 = (bf16[2,512,1024]{2,1,0:T(8,128)(2,1)}, bf16[2,512,1024]{2,1,0:T(8,128)(2,1)}, u32[]{:S(2)}, u32[]{:S(2)}) collective-permute-start(bf16[2,512,1024]{2,1,0:T(8,128)(2,1)} %get-tuple-element.172.refs_2_.refs_17_), channel_id=1, source_target_pairs={{1,0},{0,1},{3,2},{2,3},{5,4},{4,5},{7,6},{6,7},{9,8},{8,9},{11,10... | collective-permute-start | bytes 6291464 | tf_op jit(solution)/shard_map/ppermute | solution.py:746
  13.3 57.9 %collective-permute-start.6 = (bf16[2,512,1024]{2,1,0:T(8,128)(2,1)}, bf16[2,512,1024]{2,1,0:T(8,128)(2,1)}, u32[]{:S(2)}, u32[]{:S(2)}) collective-permute-start(bf16[2,512,1024]{2,1,0:T(8,128)(2,1)} %get-tuple-element.180.refs_2_), channel_id=1, source_target_pairs={{1,0},{0,1},{3,2},{2,3},{5,4},{4,5},{7,6},{6,7},{9,8},{8,9},{11,10... | collective-permute-start | bytes 6291464 | tf_op jit(solution)/shard_map/ppermute | solution.py:746
  107.5 31.5 %collective-permute-start.7 = (bf16[2,512,1024]{2,1,0:T(8,128)(2,1)}, bf16[2,512,1024]{2,1,0:T(8,128)(2,1)S(1)}, u32[]{:S(2)}, u32[]{:S(2)}) collective-permute-start(bf16[2,512,1024]{2,1,0:T(8,128)(2,1)} %weight_grads.4), channel_id=1, source_target_pairs={{0,1},{1,0},{2,3},{3,2},{4,5},{5,4},{6,7},{7,6},{8,9},{9,8},{10,11... | collective-permute-start | bytes 6291464 | tf_op jit(solution)/shard_map/ppermute | solution.py:942
  162.1 26.3 %collective-permute-start.11 = (bf16[256,1536]{1,0:T(8,128)(2,1)}, bf16[256,1536]{1,0:T(8,128)(2,1)S(1)}, u32[]{:S(2)}, u32[]{:S(2)}) collective-permute-start(bf16[256,1536]{1,0:T(8,128)(2,1)} %get-tuple-element.218), channel_id=1, source_target_pairs={{0,2},{2,0},{4,6},{6,4},{8,10},{10,8},{12,14},{14,12},{16,18},{18,... | collective-permute-start | bytes 2359304 | tf_op jit(solution)/shard_map/ppermute | solution.py:1008
  164.9 23.6 %collective-permute-start.12 = (bf16[256,1536]{1,0:T(8,128)(2,1)}, bf16[256,1536]{1,0:T(8,128)(2,1)S(1)}, u32[]{:S(2)}, u32[]{:S(2)}) collective-permute-start(bf16[256,1536]{1,0:T(8,128)(2,1)} %get-tuple-element.220), channel_id=1, source_target_pairs={{0,4},{2,6},{4,0},{6,2},{8,12},{10,14},{12,8},{14,10},{16,20},{18,... | collective-permute-start | bytes 2359304 | tf_op jit(solution)/shard_map/ppermute | solution.py:1008
  166.4 22.0 %collective-permute-start.13 = (bf16[256,1024]{1,0:T(8,128)(2,1)}, bf16[256,1024]{1,0:T(8,128)(2,1)S(1)}, u32[]{:S(2)}, u32[]{:S(2)}) collective-permute-start(bf16[256,1024]{1,0:T(8,128)(2,1)} %get-tuple-element.222), channel_id=1, source_target_pairs={{0,8},{2,10},{4,12},{6,14},{8,0},{10,2},{12,4},{14,6},{16,24},{18,... | collective-permute-start | bytes 1572872 | tf_op jit(solution)/shard_map/ppermute | solution.py:1008
  174.5 32.3 %collective-permute-start.14 = (bf16[2,512,1024]{2,1,0:T(8,128)(2,1)}, bf16[2,512,1024]{2,1,0:T(8,128)(2,1)}, u32[]{:S(2)}, u32[]{:S(2)}) collective-permute-start(bf16[2,512,1024]{2,1,0:T(8,128)(2,1)} %weight_grads.6), channel_id=1, source_target_pairs={{0,1},{1,0},{2,3},{3,2},{4,5},{5,4},{6,7},{7,6},{8,9},{9,8},{10,11... | collective-permute-start | bytes 6291464 | tf_op jit(solution)/shard_map/ppermute | solution.py:942
  203.0 24.7 %collective-permute-start.32 = (bf16[128,1536]{1,0:T(8,128)(2,1)S(1)}, bf16[128,1536]{1,0:T(8,128)(2,1)S(1)}, u32[]{:S(2)}, u32[]{:S(2)}) collective-permute-start(bf16[128,1536]{1,0:T(8,128)(2,1)S(1)} %copy-done.60), channel_id=1, source_target_pairs={{0,4},{2,6},{4,0},{6,2},{8,12},{10,14},{12,8},{14,10},{16,20},{18,... | collective-permute-start | bytes 1179656 | tf_op jit(solution)/shard_map/ppermute | solution.py:1008
  203.6 24.2 %collective-permute-start.33 = (bf16[128,1536]{1,0:T(8,128)(2,1)S(1)}, bf16[128,1536]{1,0:T(8,128)(2,1)S(1)}, u32[]{:S(2)}, u32[]{:S(2)}) collective-permute-start(bf16[128,1536]{1,0:T(8,128)(2,1)S(1)} %copy-done.59), channel_id=1, source_target_pairs={{0,2},{2,0},{4,6},{6,4},{8,10},{10,8},{12,14},{14,12},{16,18},{18,... | collective-permute-start | bytes 1179656 | tf_op jit(solution)/shard_map/ppermute | solution.py:1008
  204.1 23.6 %collective-permute-start.34 = (bf16[128,1024]{1,0:T(8,128)(2,1)}, bf16[128,1024]{1,0:T(8,128)(2,1)S(1)}, u32[]{:S(2)}, u32[]{:S(2)}) collective-permute-start(bf16[128,1024]{1,0:T(8,128)(2,1)} %get-tuple-element.271), channel_id=1, source_target_pairs={{0,16},{2,18},{4,20},{6,22},{8,24},{10,26},{12,28},{14,30},{16,0},... | collective-permute-start | bytes 786440 | tf_op jit(solution)/shard_map/ppermute | solution.py:1008
  234.8 14.5 %collective-permute-start.19 = (f32[32,128]{1,0:T(8,128)S(1)}, f32[32,128]{1,0:T(8,128)S(1)}, u32[]{:S(2)}, u32[]{:S(2)}) collective-permute-start(f32[32,128]{1,0:T(8,128)S(1)} %pad_maximum_fusion.6), channel_id=1, source_target_pairs={{0,1},{1,0},{2,3},{3,2},{4,5},{5,4},{6,7},{7,6},{8,9},{9,8},{10,11... | collective-permute-start | bytes 49160 | tf_op jit(solution)/shard_map/ppermute | solution.py:1234
  249.3 36.5 %collective-permute-start.20 = (f32[32,128]{1,0:T(8,128)S(1)}, f32[32,128]{1,0:T(8,128)S(1)}, u32[]{:S(2)}, u32[]{:S(2)}) collective-permute-start(f32[32,128]{1,0:T(8,128)S(1)} %fusion.refs_6_), channel_id=1, source_target_pairs={{0,2},{2,0},{4,6},{6,4},{8,10},{10,8},{12,14},{14,12},{16,18},{18,... | collective-permute-start | bytes 49160 | tf_op jit(solution)/shard_map/ppermute | solution.py:1237
  250.9 38.5 %collective-permute-start.16 = (bf16[256,1536]{1,0:T(8,128)(2,1)}, bf16[256,1536]{1,0:T(8,128)(2,1)S(1)}, u32[]{:S(2)}, u32[]{:S(2)}) collective-permute-start(bf16[256,1536]{1,0:T(8,128)(2,1)} %get-tuple-element.234), channel_id=1, source_target_pairs={{0,2},{2,0},{4,6},{6,4},{8,10},{10,8},{12,14},{14,12},{16,18},{18,... | collective-permute-start | bytes 2359304 | tf_op jit(solution)/shard_map/ppermute | solution.py:1008
  252.5 36.8 %collective-permute-start.17 = (bf16[256,1536]{1,0:T(8,128)(2,1)}, bf16[256,1536]{1,0:T(8,128)(2,1)S(1)}, u32[]{:S(2)}, u32[]{:S(2)}) collective-permute-start(bf16[256,1536]{1,0:T(8,128)(2,1)} %get-tuple-element.236), channel_id=1, source_target_pairs={{0,4},{2,6},{4,0},{6,2},{8,12},{10,14},{12,8},{14,10},{16,20},{18,... | collective-permute-start | bytes 2359304 | tf_op jit(solution)/shard_map/ppermute | solution.py:1008
  254.1 33.2 %collective-permute-start.18 = (bf16[256,1024]{1,0:T(8,128)(2,1)}, bf16[256,1024]{1,0:T(8,128)(2,1)S(1)}, u32[]{:S(2)}, u32[]{:S(2)}) collective-permute-start(bf16[256,1024]{1,0:T(8,128)(2,1)} %get-tuple-element.238), channel_id=1, source_target_pairs={{0,8},{2,10},{4,12},{6,14},{8,0},{10,2},{12,4},{14,6},{16,24},{18,... | collective-permute-start | bytes 1572872 | tf_op jit(solution)/shard_map/ppermute | solution.py:1008
  284.9 11.2 %collective-permute-start.45 = (bf16[64,1536]{1,0:T(8,128)(2,1)S(1)}, bf16[64,1536]{1,0:T(8,128)(2,1)S(1)}, u32[]{:S(2)}, u32[]{:S(2)}) collective-permute-start(bf16[64,1536]{1,0:T(8,128)(2,1)S(1)} %pad_maximum_fusion.1), channel_id=1, source_target_pairs={{0,8},{2,10},{4,12},{6,14},{8,0},{10,2},{12,4},{14,6},{16,24},{18,... | collective-permute-start | bytes 589832 | tf_op jit(solution)/shard_map/ppermute | solution.py:955
  285.8 28.1 %collective-permute-start.48 = (bf16[64,1024]{1,0:T(8,128)(2,1)S(1)}, bf16[64,1024]{1,0:T(8,128)(2,1)}, u32[]{:S(2)}, u32[]{:S(2)}) collective-permute-start(bf16[64,1024]{1,0:T(8,128)(2,1)S(1)} %pad_maximum_fusion.4), channel_id=1, source_target_pairs={{0,2},{2,0},{4,6},{6,4},{8,10},{10,8},{12,14},{14,12},{16,18},{18,... | collective-permute-start | bytes 393224 | tf_op jit(solution)/shard_map/ppermute | solution.py:955
  294.0 12.7 %collective-permute-start.21 = (bf16[128,1536]{1,0:T(8,128)(2,1)}, bf16[128,1536]{1,0:T(8,128)(2,1)S(1)}, u32[]{:S(2)}, u32[]{:S(2)}) collective-permute-start(bf16[128,1536]{1,0:T(8,128)(2,1)} %get-tuple-element.248), channel_id=1, source_target_pairs={{0,4},{2,6},{4,0},{6,2},{8,12},{10,14},{12,8},{14,10},{16,20},{18,... | collective-permute-start | bytes 1179656 | tf_op jit(solution)/shard_map/ppermute | solution.py:1008
  303.8 32.9 %collective-permute-start.46 = (bf16[128,1536]{1,0:T(8,128)(2,1)S(1)}, bf16[128,1536]{1,0:T(8,128)(2,1)S(1)}, u32[]{:S(2)}, u32[]{:S(2)}) collective-permute-start(bf16[128,1536]{1,0:T(8,128)(2,1)S(1)} %constant_dynamic-update-slice_fusion.5.refs_2_), channel_id=1, source_target_pairs={{0,2},{2,0},{4,6},{6,4},{8,10},{10,8},{12,14},{14,12},{16,18},{18,... | collective-permute-start | bytes 1179656 | tf_op jit(solution)/shard_map/ppermute | solution.py:955
  306.0 30.7 %collective-permute-start.43 = (bf16[128,1536]{1,0:T(8,128)(2,1)S(1)}, bf16[128,1536]{1,0:T(8,128)(2,1)S(1)}, u32[]{:S(2)}, u32[]{:S(2)}) collective-permute-start(bf16[128,1536]{1,0:T(8,128)(2,1)S(1)} %constant_dynamic-update-slice_fusion.2.refs_0_), channel_id=1, source_target_pairs={{0,4},{2,6},{4,0},{6,2},{8,12},{10,14},{12,8},{14,10},{16,20},{18,... | collective-permute-start | bytes 1179656 | tf_op jit(solution)/shard_map/ppermute | solution.py:955
  310.0 11.5 %collective-permute-start.27 = (bf16[64,1024]{1,0:T(8,128)(2,1)}, bf16[64,1024]{1,0:T(8,128)(2,1)S(1)}, u32[]{:S(2)}, u32[]{:S(2)}) collective-permute-start(bf16[64,1024]{1,0:T(8,128)(2,1)} %get-tuple-element.259), channel_id=1, source_target_pairs={{0,2},{2,0},{4,6},{6,4},{8,10},{10,8},{12,14},{14,12},{16,18},{18,... | collective-permute-start | bytes 393224 | tf_op jit(solution)/shard_map/ppermute | solution.py:1008
  314.9 20.3 %collective-permute-start.49 = (bf16[128,1024]{1,0:T(8,128)(2,1)S(1)}, bf16[128,1024]{1,0:T(8,128)(2,1)S(1)}, u32[]{:S(2)}, u32[]{:S(2)}) collective-permute-start(bf16[128,1024]{1,0:T(8,128)(2,1)S(1)} %constant_dynamic-update-slice_fusion.8.refs_4_), channel_id=1, source_target_pairs={{0,16},{2,18},{4,20},{6,22},{8,24},{10,26},{12,28},{14,30},{16,0},... | collective-permute-start | bytes 786440 | tf_op jit(solution)/shard_map/ppermute | solution.py:955
  340.9 32.9 %collective-permute-start.50 = (bf16[256,1536]{1,0:T(8,128)(2,1)}, bf16[256,1536]{1,0:T(8,128)(2,1)S(1)}, u32[]{:S(2)}, u32[]{:S(2)}) collective-permute-start(bf16[256,1536]{1,0:T(8,128)(2,1)} %get-tuple-element.298.refs_4_), channel_id=1, source_target_pairs={{0,2},{2,0},{4,6},{6,4},{8,10},{10,8},{12,14},{14,12},{16,18},{18,... | collective-permute-start | bytes 2359304 | tf_op jit(solution)/shard_map/ppermute | solution.py:955
  341.1 32.8 %collective-permute-start.51 = (bf16[256,1536]{1,0:T(8,128)(2,1)}, bf16[256,1536]{1,0:T(8,128)(2,1)S(1)}, u32[]{:S(2)}, u32[]{:S(2)}) collective-permute-start(bf16[256,1536]{1,0:T(8,128)(2,1)} %get-tuple-element.299.refs_6_), channel_id=1, source_target_pairs={{0,4},{2,6},{4,0},{6,2},{8,12},{10,14},{12,8},{14,10},{16,20},{18,... | collective-permute-start | bytes 2359304 | tf_op jit(solution)/shard_map/ppermute | solution.py:955
  341.8 30.0 %collective-permute-start.52 = (bf16[256,1024]{1,0:T(8,128)(2,1)}, bf16[256,1024]{1,0:T(8,128)(2,1)S(1)}, u32[]{:S(2)}, u32[]{:S(2)}) collective-permute-start(bf16[256,1024]{1,0:T(8,128)(2,1)} %get-tuple-element.300.refs_8_), channel_id=1, source_target_pairs={{0,8},{2,10},{4,12},{6,14},{8,0},{10,2},{12,4},{14,6},{16,24},{18,... | collective-permute-start | bytes 1572872 | tf_op jit(solution)/shard_map/ppermute | solution.py:955
  369.2 22.4 %collective-permute-start.61 = (bf16[128,1024]{1,0:T(8,128)(2,1)S(1)}, bf16[128,1024]{1,0:T(8,128)(2,1)}, u32[]{:S(2)}, u32[]{:S(2)}) collective-permute-start(bf16[128,1024]{1,0:T(8,128)(2,1)S(1)} %constant_dynamic-update-slice_fusion.17.refs_5_), channel_id=1, source_target_pairs={{0,16},{2,18},{4,20},{6,22},{8,24},{10,26},{12,28},{14,30},{16,0},... | collective-permute-start | bytes 786440 | tf_op jit(solution)/shard_map/ppermute | solution.py:955
  371.4 20.3 %collective-permute-start.58 = (bf16[128,1536]{1,0:T(8,128)(2,1)S(1)}, bf16[128,1536]{1,0:T(8,128)(2,1)S(1)}, u32[]{:S(2)}, u32[]{:S(2)}) collective-permute-start(bf16[128,1536]{1,0:T(8,128)(2,1)S(1)} %constant_dynamic-update-slice_fusion.14.refs_3_), channel_id=1, source_target_pairs={{0,2},{2,0},{4,6},{6,4},{8,10},{10,8},{12,14},{14,12},{16,18},{18,... | collective-permute-start | bytes 1179656 | tf_op jit(solution)/shard_map/ppermute | solution.py:955
  371.8 19.8 %collective-permute-start.55 = (bf16[128,1536]{1,0:T(8,128)(2,1)S(1)}, bf16[128,1536]{1,0:T(8,128)(2,1)S(1)}, u32[]{:S(2)}, u32[]{:S(2)}) collective-permute-start(bf16[128,1536]{1,0:T(8,128)(2,1)S(1)} %constant_dynamic-update-slice_fusion.11.refs_1_), channel_id=1, source_target_pairs={{0,4},{2,6},{4,0},{6,2},{8,12},{10,14},{12,8},{14,10},{16,20},{18,... | collective-permute-start | bytes 1179656 | tf_op jit(solution)/shard_map/ppermute | solution.py:955
  395.3 12.2 %collective-permute-start.62 = (bf16[256,1536]{1,0:T(8,128)(2,1)}, bf16[256,1536]{1,0:T(8,128)(2,1)S(1)}, u32[]{:S(2)}, u32[]{:S(2)}) collective-permute-start(bf16[256,1536]{1,0:T(8,128)(2,1)} %get-tuple-element.305.refs_4_), channel_id=1, source_target_pairs={{0,2},{2,0},{4,6},{6,4},{8,10},{10,8},{12,14},{14,12},{16,18},{18,... | collective-permute-start | bytes 2359304 | tf_op jit(solution)/shard_map/ppermute | solution.py:955
  395.4 12.2 %collective-permute-start.63 = (bf16[256,1536]{1,0:T(8,128)(2,1)}, bf16[256,1536]{1,0:T(8,128)(2,1)S(1)}, u32[]{:S(2)}, u32[]{:S(2)}) collective-permute-start(bf16[256,1536]{1,0:T(8,128)(2,1)} %get-tuple-element.306.refs_6_), channel_id=1, source_target_pairs={{0,4},{2,6},{4,0},{6,2},{8,12},{10,14},{12,8},{14,10},{16,20},{18,... | collective-permute-start | bytes 2359304 | tf_op jit(solution)/shard_map/ppermute | solution.py:955
  (99 other events, 703.2 us)
